TPU v7x, 256 devices: a whole 4x4x8 slice. The times are simulated.
256 devices in a mesh: pair: 64 (over z, y, core), rep: 4 (over x).
Axes of the slice: x: 4, y: 4, z: 8, core: 2. Of those that a mesh axis runs over, the one named last changes fastest.
Arguments:
- t_amp: bfloat16 [65536, 1536], P('pair', 'rep'), may hold values from -6 to 6
- t_mask: int32 [512, 12], P('pair', 'rep'), may hold values 0 or 1
- v_int: bfloat16 [1536, 8192], P('rep', 'pair'), may hold values from -0.15625 to 0.15625
- v_mask: int32 [12, 64], P('rep', 'pair'), may hold values 0 or 1
- ab_order: int32 [64], replicated, may hold values from 0 to 63, each once
- r_mask: int32 [512, 64], P('pair', 'rep'), may hold values 0 or 1
- r_old: bfloat16 [65536, 8192], P('pair', 'rep'), may hold values from -6 to 6
Outputs:
- r_new: bfloat16 [65536, 8192], P('pair', 'rep')
Inputs may be any that keep to these rules, and one draw needn't show every extreme that they name: `ab_order`: a permutation of the 64 tile indices.
All inputs are finite; a program needn't handle non-finite values. No bound on the sum of `t_mask` or of `v_mask` or of `r_mask` on one device may be relied on, other than what follows from the above.
Results may differ from a plain program's by a relative error of at most 0.001.
Values may be sent and summed in bfloat16 or wider, within the bound.
No kernel may reach another device: no remote copies, remote signals or barrier semaphores. Data moves between devices by JAX's collectives and lax.ppermute only.
A program may use at most 128 MiB of HBM per device.

v0:
```python
import jax
import jax.numpy as jnp
from jax import lax
from jax.sharding import PartitionSpec as P

TILE = 128


def inverse_order(ab_order):
    count = ab_order.shape[0]
    return jnp.zeros((count,), jnp.int32).at[ab_order].set(jnp.arange(count, dtype=jnp.int32))


def body(t_amp, t_mask, v_int, v_mask, ab_order, r_mask, r_old):
    tile = TILE
    i_loc, c_loc = t_mask.shape
    c_v, a_loc = v_mask.shape
    quarter_tiles = r_mask.shape[1]
    t_kept = (
        t_amp.reshape(i_loc, tile, c_loc, tile) * t_mask[:, None, :, None].astype(t_amp.dtype)
    ).reshape(i_loc * tile, c_loc * tile)
    v_kept = (
        v_int.reshape(c_v, tile, a_loc, tile) * v_mask[:, None, :, None].astype(v_int.dtype)
    ).reshape(c_v * tile, a_loc * tile)
    inverse = inverse_order(ab_order)
    wanted = lax.dynamic_slice_in_dim(
        inverse, lax.axis_index("rep") * quarter_tiles, quarter_tiles, 0
    )
    v_deep = lax.all_gather(v_kept, "rep", axis=0, tiled=True)
    v_full = lax.all_gather(v_deep, "pair", axis=1, tiled=True)
    blocks = v_full.reshape(v_full.shape[0], -1, tile)
    v_slab = jnp.take(blocks, wanted, axis=1).reshape(v_full.shape[0], quarter_tiles * tile)
    ladder = jnp.dot(
        lax.all_gather(t_kept, "rep", axis=1, tiled=True),
        v_slab,
        preferred_element_type=jnp.float32,
    )
    row_mask = jnp.repeat(r_mask, tile, axis=0)
    kept = ladder.reshape(i_loc * tile, quarter_tiles, tile) * row_mask[:, :, None].astype(
        jnp.float32
    )
    return (r_old.astype(jnp.float32) + kept.reshape(i_loc * tile, quarter_tiles * tile)).astype(
        jnp.bfloat16
    )


def solution(mesh):
    placed = (
        P("pair", "rep"),
        P("pair", "rep"),
        P("rep", "pair"),
        P("rep", "pair"),
        P(),
        P("pair", "rep"),
        P("pair", "rep"),
    )
    return jax.shard_map(
        body, mesh=mesh, in_specs=placed, out_specs=P("pair", "rep"), check_vma=False
    )
```

profile of v0, /device:TPU:1, one launch (start us, length us, event | category | flops | bytes accessed | tf_op | source)
XLA Modules:
  0.0 243.4 jit_solution(14492398847992674994)
XLA Ops:
  6.5 0.0 copy-start
  6.5 0.0 copy-start.1
  6.5 0.0 all-gather.5.cloned.1.call-start
  6.5 1.0 copy.16
  7.6 0.7 convert_bitcast_fusion
  8.2 0.1 broadcast_bitcast_fusion.1
  8.3 12.7 %all_gather.10 = bf16[1536,128]{0,1:T(8,128)(2,1)} all-gather(bf16[384,128]{0,1:T(8,128)(2,1)S(1)} %broadcast_multiply_fusion.1), channel_id=1, replica_groups=mesh['pair'=64,'rep'=4] {'rep'}, dimensions={0}, use_global_device_ids=true | all-gather | bytes 491520 | tf_op jit(solution)/shard_map/all_gather | solution.py:29
  21.0 0.0 all-gather.5.cloned.1.call-update
  21.1 0.0 all-gather.3.cloned.1.call-start
  21.1 0.7 convert_element_type.34
  21.8 0.2 mul.37
  22.0 0.2 copy.25
  22.2 0.4 copy.15
  22.5 2.2 mul.39
  24.7 0.0 all-gather.3.cloned.1.call-update
  24.8 0.0 copy-done
  24.8 0.1 copy.19
  24.9 0.1 broadcast_in_dim.30
  25.0 0.0 copy-done.1
  25.0 0.8 scatter_custom_fusion
  25.8 0.1 compare_and_fusion
  25.9 0.1 broadcast_bitcast_fusion
  25.9 121.9 %all-gather.5.cloned.1.call-done = bf16[1536,8192]{0,1:T(8,128)(2,1)} async-done(((bf16[1536,128]{0,1:T(8,128)(2,1)}), bf16[1536,8192]{0,1:T(8,128)(2,1)}) %all-gather.5.cloned.1.call-update) | async-done | bytes 25165840 | tf_op jit(solution)/shard_map/all_gather | solution.py:30
  147.9 32.6 %copy.17 = bf16[1536,64,128]{2,0,1:T(8,128)(2,1)} copy(bf16[1536,64,128]{0,2,1:T(8,128)(2,1)} %bitcast.31) | data formatting | bytes 50331648 | tf_op jit(solution)/shard_map/reshape | solution.py:31
  180.4 12.2 %gather_fusion = bf16[16,1536,128]{2,1,0:T(8,128)(2,1)} fusion(bf16[1536,64,128]{2,0,1:T(8,128)(2,1)} %copy.17, s32[1024]{0:T(1024)S(1)} %pad_clamp_fusion), kind=kCustom, calls=%fused_computation | custom fusion | bytes 12582976 | tf_op jit(solution)/shard_map/jit(_take)/gather | solution.py:32
  192.6 8.7 %copy.18 = bf16[1536,16,128]{0,2,1:T(8,128)(2,1)} copy(bf16[1536,16,128]{2,0,1:T(8,128)(2,1)} %bitcast.32) | data formatting | bytes 12582912 | tf_op jit(solution)/shard_map/jit(_take)/gather | solution.py:32
  201.3 6.1 %bitcast_select_fusion = bf16[1536,2048]{0,1:T(8,128)(2,1)} fusion(bf16[1536,16,128]{0,2,1:T(8,128)(2,1)} %copy.18, pred[2048]{0:T(1024)(128)(4,1)S(1)} %broadcast_bitcast_fusion), kind=kLoop, calls=%fused_computation.3 | loop fusion | flops 3145728 | bytes 12584960 | tf_op jit(solution)/shard_map/jit(_take)/select_n | solution.py:32
  207.4 0.0 all-gather.3.cloned.1.call-done
  207.4 11.7 %broadcast_multiply_fusion = f32[1024,16,128]{0,2,1:T(8,128)} fusion(f32[1024,16]{0,1:T(8,128)S(1)} %bitcast.38, bf16[16,128,1536]{2,1,0:T(8,128)(2,1)} %bitcast.34, bf16[1024,1536]{1,0:T(8,128)(2,1)} %all-gather.3.cloned.1.call-done), kind=kOutput, calls=%fused_computation.4 | convolution fusion | flops 6444548096 | bytes 17891328 | tf_op jit(solution)/shard_map/dot_general | solution.py:33
  219.2 9.1 %copy.20 = f32[1024,2048]{1,0:T(8,128)} copy(f32[1024,2048]{0,1:T(8,128)} %bitcast.33) | data formatting | bytes 16777216 | tf_op jit(solution)/shard_map/reshape | solution.py:42
  228.3 8.3 %add_convert_fusion = bf16[1024,2048]{1,0:T(8,128)(2,1)} fusion(f32[1024,2048]{1,0:T(8,128)} %copy.20, bf16[1024,2048]{1,0:T(8,128)(2,1)} %param.13), kind=kLoop, calls=%fused_computation.2 | loop fusion | flops 6291456 | bytes 16777216 | tf_op jit(solution)/shard_map/convert_element_type | solution.py:42
  (6 shorter events, 0.1 us)
Async XLA Ops:
  6.5 18.2 %copy-start = (s32[8,16]{1,0:T(8,128)S(1)}, s32[8,16]{1,0:T(8,128)}, u32[]{:S(2)}) copy-start(s32[8,16]{1,0:T(8,128)} %param.12) | copy-start | bytes 1540
  6.5 18.4 %copy-start.1 = (s32[64]{0:T(128)S(1)}, s32[64]{0:T(128)}, u32[]{:S(2)}) copy-start(s32[64]{0:T(128)} %param.11) | copy-start | bytes 772
  6.5 141.3 %all-gather.5.cloned.1.call-start = ((), (), s32[]{:S(2)}) async-start(), calls=%async_computation.1 | async-start | bytes 25559040 | tf_op jit(solution)/shard_map/all_gather | solution.py:30
  21.1 186.3 %all-gather.3.cloned.1.call-start = ((), (), s32[]{:S(2)}) async-start(), calls=%async_computation | async-start | bytes 3932160 | tf_op jit(solution)/shard_map/all_gather | solution.py:34
Sparse Core Ops, SparseCore 0:
  21.2 126.6 all-gather.4
  149.7 38.6 all-gather.2
where the time goes:
time: 245 us; the launch traced here: 243 us
  waiting for transfers between devices  122 us (50%)
  local copies, waits for them, and re-layouts  65.4 us (27%)
  other arithmetic  18.1 us (7%)
  between operations  13.5 us (6%)
  blocking collectives  12.7 us (5%)
  matrix products  11.7 us (5%)
    all_gather x1, waiting for transfers between devices, body(): v_full = lax.all_gather(v_deep, 'pair', axis=1, tiled=True)  122 us
    reshape x1, local copies, waits for them, and re-layouts, body(): blocks = v_full.reshape(v_full.shape[0], -1, tile)  32.6 us
    gather x2, local copies, waits for them, and re-layouts, body(): jnp.take(blocks, wanted, axis=1)  20.8 us
    all_gather x1, blocking collectives, body(): v_deep = lax.all_gather(v_kept, 'rep', axis=0, tiled=True)  12.7 us
    dot_general x1, matrix products, body(): jnp.dot(lax.all_gather(t_kept, 'rep', axis=1, tiled=True), v_slab, prefer...  11.7 us
    reshape x1, local copies, waits for them, and re-layouts, body(): kept.reshape(i_loc * tile, quarter_tiles * tile)  9.12 us
    convert_element_type x1, other arithmetic, body(): (r_old.astype(jnp.float32) + kept.reshape(i_loc * tile, quarter_tiles * t...  8.29 us
    select_n x1, other arithmetic, body(): jnp.take(blocks, wanted, axis=1)  6.13 us
  transfers between devices with their start and end apart: 2, of which 1 were waited for; matrix products, arithmetic and copies ran while one was open for 26% of the time, Pallas kernels for 0%

commit v1 on v0

v1 whole, which is shorter than its diff:
```python
import functools

import jax
import jax.numpy as jnp
from jax import lax
from jax.experimental import pallas as pl
from jax.experimental.pallas import tpu as pltpu
from jax.sharding import Mesh
from jax.sharding import PartitionSpec as P

TILE = 128
NZ, NY, NX = 8, 4, 4
CHUNK = 48
ROWS = 256
COLS = 16
SPAN = 8
BLOCKS = 16
HALF = 8
SMALL = 16 * 1024 * 1024
LARGE = 60 * 1024 * 1024


def pairs_zc(d):
    return [(z * 2 + c, ((z + (d if c == 0 else -d)) % NZ) * 2 + c) for z in range(NZ) for c in range(2)]


def pairs_yc(d):
    return [(y * 2 + c, ((y + (d if c == 0 else -d)) % NY) * 2 + c) for y in range(NY) for c in range(2)]


def pairs_cx(d):
    return [(c * NX + x, c * NX + (x + (d if c == 0 else -d)) % NX) for c in range(2) for x in range(NX)]


def move_z(v):
    return lax.ppermute(v, ("z", "c"), pairs_zc(1))


def move_y(v):
    return lax.ppermute(v, ("y", "c"), pairs_yc(1))


def move_x(v, d=1):
    return lax.ppermute(v, ("c", "x"), pairs_cx(d))


def swap(v):
    return lax.ppermute(v, "c", [(0, 1), (1, 0)])


def cost(flops, moved):
    return pl.CostEstimate(flops=flops, bytes_accessed=moved, transcendentals=0)


def in_smem():
    return pl.BlockSpec(memory_space=pltpu.SMEM)


def in_vmem():
    return pl.BlockSpec(memory_space=pltpu.VMEM)


def keep_t_kernel(mask_ref, t_ref, out_ref):
    i = pl.program_id(0)
    rows, cols = t_ref.shape
    for a in range(rows // TILE):
        for j in range(cols // TILE):
            at = (slice(a * TILE, (a + 1) * TILE), slice(j * TILE, (j + 1) * TILE))
            kept = mask_ref[i * (rows // TILE) + a, j] != 0
            out_ref[at] = jnp.where(kept, t_ref[at], jnp.zeros((TILE, TILE), t_ref.dtype))


def keep_t(mask, t):
    rows, cols = t.shape
    block = pl.BlockSpec((ROWS, cols), lambda i: (i, 0))
    return pl.pallas_call(
        keep_t_kernel,
        grid=(rows // ROWS,),
        out_shape=jax.ShapeDtypeStruct(t.shape, t.dtype),
        in_specs=[in_smem(), block],
        out_specs=block,
        compiler_params=pltpu.CompilerParams(vmem_limit_bytes=SMALL),
        cost_estimate=cost(rows * cols, 4 * rows * cols),
        name="keep_t",
    )(mask, t)


def spread_v_kernel(mask_ref, v_ref, out_ref):
    for g in range(8):
        for k in range(CHUNK // 16):
            row = g * CHUNK + k * 16
            kept = mask_ref[row // TILE, 0] != 0
            v = jnp.where(kept, v_ref[row : row + 16, :], jnp.zeros((16, TILE), v_ref.dtype))
            for zz in range(2):
                for yy in range(2):
                    chip = (zz * 4 + g // 2) * NY + yy * 2 + g % 2
                    out_ref[chip, k * 16 : k * 16 + 16, :] = v


def spread_v(mask, v):
    return pl.pallas_call(
        spread_v_kernel,
        out_shape=jax.ShapeDtypeStruct((NZ * NY, CHUNK, TILE), v.dtype),
        in_specs=[in_smem(), in_vmem()],
        out_specs=in_vmem(),
        compiler_params=pltpu.CompilerParams(vmem_limit_bytes=SMALL),
        cost_estimate=cost(v.size, 12 * v.size),
        name="spread_v",
    )(mask, v)


def select_kernel(place_ref, order_ref, a_ref, b_ref, own_ref, near_ref, far_ref, slot_ref):
    c, x = place_ref[2], place_ref[3]
    for k in range(order_ref.shape[0]):
        slot_ref[order_ref[k]] = k

    def put(out_ref, first, count):
        for j in range(count):
            k = slot_ref[first + j]
            chip = lax.div(k, 2)
            out_ref[j] = jnp.where(lax.rem(k, 2) == c, a_ref[chip], b_ref[chip])

    put(own_ref, x * COLS, COLS)
    put(near_ref, lax.rem(x + 1 - 2 * c + NX, NX) * COLS, COLS)
    put(far_ref, lax.rem(x + 2, NX) * COLS + c * HALF, HALF)


def select(place, order, a, b):
    shape = lambda n: jax.ShapeDtypeStruct((n, CHUNK, TILE), a.dtype)
    return pl.pallas_call(
        select_kernel,
        out_shape=(shape(COLS), shape(COLS), shape(HALF)),
        in_specs=[in_smem(), in_smem(), in_vmem(), in_vmem()],
        out_specs=(in_vmem(),) * 3,
        scratch_shapes=[pltpu.SMEM((order.shape[0],), jnp.int32)],
        compiler_params=pltpu.CompilerParams(vmem_limit_bytes=SMALL),
        cost_estimate=cost(0, 2 << 20),
        name="select_columns",
    )(place, order, a, b)


def pack_kernel(place_ref, own_ref, r1_ref, w1_ref, r2_ref, w2_ref, ahead_ref, rest_ref):
    c = place_ref[2]
    for j in range(COLS):
        opposite = jnp.where(c == j // HALF, r2_ref[j % HALF], w2_ref[j % HALF])
        left = jnp.where(c == 0, r1_ref[j], w1_ref[j])
        right = jnp.where(c == 0, w1_ref[j], r1_ref[j])
        ahead_ref[j, 0] = jnp.where(c == 0, own_ref[j], left)
        ahead_ref[j, 1] = jnp.where(c == 0, opposite, right)
        rest_ref[j, 0] = jnp.where(c == 0, left, own_ref[j])
        rest_ref[j, 1] = jnp.where(c == 0, right, opposite)


def pack(place, own, r1, w1, r2, w2):
    shape = jax.ShapeDtypeStruct((COLS, 2, CHUNK, TILE), own.dtype)
    return pl.pallas_call(
        pack_kernel,
        out_shape=(shape, shape),
        in_specs=[in_smem()] + [in_vmem()] * 5,
        out_specs=(in_vmem(),) * 2,
        compiler_params=pltpu.CompilerParams(vmem_limit_bytes=SMALL),
        cost_estimate=cost(0, 3 << 20),
        name="pack_shard",
    )(place, own, r1, w1, r2, w2)


def ladder_kernel(place_ref, mask_ref, t0, t1, t2, t3, r_ref, *rest):
    blocks, (out_ref, slab, sems) = rest[:BLOCKS], rest[BLOCKS:]
    i = pl.program_id(0)
    z, y, c = (place_ref[n] for n in range(3))
    s = 1 - 2 * c

    def copies(part):
        cols = pl.ds(part * SPAN, SPAN)
        zs = (z, z, z - s, z - s, z + s, z + s, z + 2, z + 2)
        halves = (c, 1 - c, c, 1 - c, 1 - c, c, c, 1 - c)
        for n, ref in enumerate(blocks):
            zz, half, yy = zs[n % 8], halves[n % 8], y + n // 8
            g = lax.rem(zz + NZ, 4) * 2 + lax.rem(yy, 2)
            yield pltpu.make_async_copy(ref.at[cols], slab.at[cols, pl.ds(2 * half, 2), g], sems.at[part, n])

    @pl.when(i == 0)
    def _():
        for part in range(COLS // SPAN):
            for copy in copies(part):
                copy.start()

    left = jnp.where(c == 0, t1[...], t2[...])
    right = jnp.where(c == 0, t2[...], t1[...])
    t = jnp.concatenate([t0[...], t3[...], left, right], axis=1)
    depth = t.shape[1]
    for n in range(COLS // 2):
        if 2 * n % SPAN == 0:

            @pl.when(i == 0)
            def _(part=2 * n // SPAN):
                for copy in copies(part):
                    copy.wait()

        pair = jnp.concatenate([slab[2 * n + k].reshape(depth, TILE) for k in range(2)], axis=1)
        acc = jnp.dot(t, pair, preferred_element_type=jnp.float32)
        for a in range(ROWS // TILE):
            rows = slice(a * TILE, (a + 1) * TILE)
            for j in range(2):
                cols = slice((2 * n + j) * TILE, (2 * n + j + 1) * TILE)
                m = mask_ref[i * (ROWS // TILE) + a, 2 * n + j].astype(jnp.float32)
                kept = acc[rows, j * TILE : (j + 1) * TILE] * m
                out_ref[rows, cols] = (r_ref[rows, cols].astype(jnp.float32) + kept).astype(out_ref.dtype)


def ladder(place, r_mask, ts, r_old, blocks):
    rows, width = r_old.shape
    part = ts[0].shape[1]
    depth = NX * part
    wide = pl.BlockSpec((ROWS, width), lambda i: (i, 0))
    return pl.pallas_call(
        ladder_kernel,
        grid=(rows // ROWS,),
        out_shape=jax.ShapeDtypeStruct(r_old.shape, r_old.dtype),
        in_specs=[in_smem(), in_smem()]
        + [pl.BlockSpec((ROWS, part), lambda i: (i, 0))] * NX
        + [wide]
        + [pl.BlockSpec(memory_space=pl.ANY)] * BLOCKS,
        out_specs=wide,
        scratch_shapes=[
            pltpu.VMEM((COLS, NX, 8, CHUNK, TILE), r_old.dtype),
            pltpu.SemaphoreType.DMA((COLS // SPAN, BLOCKS)),
        ],
        compiler_params=pltpu.CompilerParams(vmem_limit_bytes=LARGE, dimension_semantics=("arbitrary",)),
        cost_estimate=cost(2 * rows * depth * width, 4 * rows * width + 2 * rows * depth + 2 * depth * width),
        name="ladder",
    )(place, r_mask, *ts, r_old, *blocks)


def body(t_amp, t_mask, v_int, v_mask, ab_order, r_mask, r_old):
    z, y, c, x = (lax.axis_index(n) for n in ("z", "y", "c", "x"))
    place = jnp.stack([z, y, c, x]).astype(jnp.int32)

    t0 = keep_t(t_mask, t_amp)
    t1 = move_x(t0)
    t2 = move_x(t0, -1)
    t0, v_int = lax.optimization_barrier((t0, v_int))
    mine = lax.all_to_all(spread_v(v_mask, v_int), ("z", "y"), 0, 0)
    own, near, opposite = select(place, ab_order, mine, swap(mine))

    r1 = move_x(near)
    r2 = lax.ppermute(opposite, "x", [(i, (i + 2) % NX) for i in range(NX)])
    w1, w2 = swap(r1), swap(r2)
    ahead, rest = pack(place, own, r1, w1, r2, w2)
    t1, w2 = lax.optimization_barrier((t1, w2))
    t3 = move_x(t1)

    p1a, q0 = move_z(ahead), move_y(ahead)
    p1r = move_z(rest)
    p2, q1a = move_z(p1a), move_y(p1a)
    q1r, q2 = move_y(p1r), move_y(p2)
    blocks = [ahead, rest, p1a, p1r, swap(p1a), swap(p1r), p2, swap(p2)]
    blocks += [q0, swap(q0), q1a, q1r, swap(q1a), swap(q1r), q2, swap(q2)]
    return ladder(place, r_mask, (t0, t1, t2, t3), r_old, blocks)


def solution(mesh):
    torus = Mesh(mesh.devices.reshape(NZ, NY, 2, NX), ("z", "y", "c", "x"))
    pair = ("z", "y", "c")
    placed = (P(pair, "x"), P(pair, "x"), P("x", pair), P("x", pair), P(), P(pair, "x"), P(pair, "x"))
    return jax.shard_map(body, mesh=torus, in_specs=placed, out_specs=P(pair, "x"), check_vma=False)
```

time: 245 us -> 98.3 us (0.40)
  waiting for transfers between devices: 122 us -> 32.4 us
  local copies, waits for them, and re-layouts: 65.4 us -> 6.9 us
  starting transfers between devices: 0.04 us -> 41.2 us
  other arithmetic: 18.1 us -> 0.08 us
  Pallas kernels: 0 us -> 17 us
  between operations: 13.5 us -> 0.39 us
  blocking collectives: 12.7 us -> 0 us
  matrix products: 11.7 us -> 0 us
    all_gather x2 -> x0, waiting for transfers between devices: 122 us -> none  [the longest x1 122 us: body(): v_full = lax.all_gather(v_deep, 'pair', axis=1, tiled=True)]
    reshape x2 -> x0, local copies, waits for them, and re-layouts: 41.7 us -> none  [the longest x1 32.6 us: body(): blocks = v_full.reshape(v_full.shape[0], -1, tile)]
    ppermute x0 -> x22, starting transfers between devices: none -> 29.1 us  [the longest x10 14.5 us: swap(): return lax.ppermute(v, 'c', [(0, 1), (1, 0)])]
    ppermute x0 -> x22, waiting for transfers between devices: none -> 21.2 us  [the longest x3 7.43 us: move_z(): return lax.ppermute(v, ('z', 'c'), pairs_zc(1))]
    gather x2 -> x0, local copies, waits for them, and re-layouts: 20.8 us -> none  [body(): jnp.take(blocks, wanted, axis=1)]
    pallas_call x0 -> x5, Pallas kernels: none -> 17 us  [the longest x1 13.2 us: ladder(): pl.pallas_call(ladder_kernel, grid=(rows // ROWS,), out_shape=jax.ShapeDt...]
    all_gather x1 -> x0, blocking collectives: 12.7 us -> none  [body(): v_deep = lax.all_gather(v_kept, 'rep', axis=0, tiled=True)]
    all_to_all x0 -> x1, starting transfers between devices: none -> 12 us  [body(): mine = lax.all_to_all(spread_v(v_mask, v_int), ('z', 'y'), 0, 0)]
  transfers between devices with their start and end apart: 2 -> 23, of which waited for: 1 -> 10; matrix products, arithmetic and copies ran while one was open for 26% -> 0% of each run, Pallas kernels for 0% -> 2%
where the time goes in v1:
time: 98.3 us; the launch traced here: 98 us
  starting transfers between devices  41.2 us (42%)
  waiting for transfers between devices  32.4 us (33%)
  Pallas kernels  17 us (17%)
  local copies, waits for them, and re-layouts  6.9 us (7%)
    ppermute x10, starting transfers between devices, swap(): return lax.ppermute(v, 'c', [(0, 1), (1, 0)])  14.5 us
    pallas_call x1, Pallas kernels, ladder(): pl.pallas_call(ladder_kernel, grid=(rows // ROWS,), out_shape=jax.ShapeDt...  13.2 us
    all_to_all x1, starting transfers between devices, body(): mine = lax.all_to_all(spread_v(v_mask, v_int), ('z', 'y'), 0, 0)  12 us
    all_to_all x1, waiting for transfers between devices, body(): mine = lax.all_to_all(spread_v(v_mask, v_int), ('z', 'y'), 0, 0)  11.2 us
    ppermute x3, waiting for transfers between devices, move_z(): return lax.ppermute(v, ('z', 'c'), pairs_zc(1))  7.43 us
    ppermute x4, waiting for transfers between devices, move_x(): return lax.ppermute(v, ('c', 'x'), pairs_cx(d))  7.04 us
    ppermute x4, starting transfers between devices, move_x(): return lax.ppermute(v, ('c', 'x'), pairs_cx(d))  6.93 us
    unnamed x48, local copies, waits for them, and re-layouts  6.9 us
  transfers between devices with their start and end apart: 23, of which 10 were waited for; matrix products, arithmetic and copies ran while one was open for 0% of the time, Pallas kernels for 2%

profile of v1, /device:TPU:1, one launch (start us, length us, event | category | flops | bytes accessed | tf_op | source)
XLA Modules:
  0.0 98.0 jit_solution(10488908321996079367)
XLA Ops:
  0.0 0.7 copy.9.mask_ref
  0.7 0.8 copy.8.mask_ref
  1.5 1.1 %copy-done = bf16[1024,384]{1,0:T(8,128)(2,1)S(1)} copy-done((bf16[1024,384]{1,0:T(8,128)(2,1)S(1)}, bf16[1024,384]{1,0:T(8,128)(2,1)}, u32[]{:S(2)}) %copy-start) | copy-done | bytes 786456
  2.6 0.9 keep_t.1.t0
  3.5 0.9 copy-done.2
  4.4 1.4 %spread_v.1 = bf16[32,48,128]{2,1,0:T(8,128)(2,1)} custom-call(s32[3,1]{1,0:T(4,128)S(1)} %copy.9.mask_ref, bf16[384,128]{1,0:T(8,128)(2,1)S(1)} %copy-done.2), custom_call_target="tpu_custom_call" | custom-call | flops 49152 | bytes 589824 | tf_op jit(solution)/shard_map/spread_v/pallas_call | solution.py:101
  5.8 12.0 %all-to-all-start = ((bf16[32,48,128]{2,1,0:T(8,128)(2,1)}), bf16[32,48,128]{2,1,0:T(8,128)(2,1)S(1)}, u32[]{:S(2)}, u32[]{:S(2)}) async-start(bf16[32,48,128]{2,1,0:T(8,128)(2,1)} %spread_v.1), calls=%async_computation | async-start | bytes 786432 | tf_op jit(solution)/shard_map/all_to_all | solution.py:243
  17.8 2.6 %collective-permute-start = (bf16[1024,384]{1,0:T(8,128)(2,1)S(1)}, bf16[1024,384]{1,0:T(8,128)(2,1)S(1)}, u32[]{:S(2)}, u32[]{:S(2)}) collective-permute-start(bf16[1024,384]{1,0:T(8,128)(2,1)S(1)} %keep_t.1.t0), channel_id=1, source_target_pairs={{0,1},{1,2},{2,3},{3,0},{4,7},{5,4},{6,5},{7,6},{8,9},{9,10},{10,1... | collective-permute-start | bytes 2359304 | tf_op jit(solution)/shard_map/ppermute | solution.py:44
  20.4 11.2 %all-to-all-done.a_ref = bf16[32,48,128]{2,1,0:T(8,128)(2,1)S(1)} async-done(((bf16[32,48,128]{2,1,0:T(8,128)(2,1)}), bf16[32,48,128]{2,1,0:T(8,128)(2,1)S(1)}, u32[]{:S(2)}, u32[]{:S(2)}) %all-to-all-start) | async-done | bytes 393248 | tf_op jit(solution)/shard_map/all_to_all | solution.py:243
  31.6 2.5 %collective-permute-start.1 = (bf16[32,48,128]{2,1,0:T(8,128)(2,1)S(1)}, bf16[32,48,128]{2,1,0:T(8,128)(2,1)S(1)}, u32[]{:S(2)}, u32[]{:S(2)}) collective-permute-start(bf16[32,48,128]{2,1,0:T(8,128)(2,1)S(1)} %all-to-all-done.a_ref), channel_id=1, source_target_pairs={{0,4},{4,0},{1,5},{5,1},{2,6},{6,2},{3,7},{7,3},{8,12},{12,8},{9,1... | collective-permute-start | bytes 1179656 | tf_op jit(solution)/shard_map/ppermute | solution.py:48
  34.1 0.1 pad_add_fusion.place_ref
  34.2 1.3 %collective-permute-done.1.b_ref = bf16[32,48,128]{2,1,0:T(8,128)(2,1)S(1)} collective-permute-done((bf16[32,48,128]{2,1,0:T(8,128)(2,1)S(1)}, bf16[32,48,128]{2,1,0:T(8,128)(2,1)S(1)}, u32[]{:S(2)}, u32[]{:S(2)}) %collective-permute-start.1) | collective-permute-done | bytes 393248 | tf_op jit(solution)/shard_map/ppermute | solution.py:48
  35.5 0.7 copy-done.4
  36.1 0.8 select_columns.1
  37.0 2.6 %collective-permute-start.6 = (bf16[16,48,128]{2,1,0:T(8,128)(2,1)S(1)}, bf16[16,48,128]{2,1,0:T(8,128)(2,1)S(1)}, u32[]{:S(2)}, u32[]{:S(2)}) collective-permute-start(bf16[16,48,128]{2,1,0:T(8,128)(2,1)S(1)} %get-tuple-element.18), channel_id=1, source_target_pairs={{0,1},{1,2},{2,3},{3,0},{4,7},{5,4},{6,5},{7,6},{8,9},{9,10},{10,1... | collective-permute-start | bytes 589832 | tf_op jit(solution)/shard_map/ppermute | solution.py:44
  39.5 0.5 collective-permute-start.2
  40.1 4.2 %collective-permute-done.6.r1_ref = bf16[16,48,128]{2,1,0:T(8,128)(2,1)S(1)} collective-permute-done((bf16[16,48,128]{2,1,0:T(8,128)(2,1)S(1)}, bf16[16,48,128]{2,1,0:T(8,128)(2,1)S(1)}, u32[]{:S(2)}, u32[]{:S(2)}) %collective-permute-start.6) | collective-permute-done | bytes 196640 | tf_op jit(solution)/shard_map/ppermute | solution.py:44
  44.3 0.2 collective-permute-start.7
  44.5 1.1 %collective-permute-done.2.r2_ref = bf16[8,48,128]{2,1,0:T(8,128)(2,1)S(1)} collective-permute-done((bf16[8,48,128]{2,1,0:T(8,128)(2,1)S(1)}, bf16[8,48,128]{2,1,0:T(8,128)(2,1)S(1)}, u32[]{:S(2)}, u32[]{:S(2)}) %collective-permute-start.2) | collective-permute-done | bytes 98336 | tf_op jit(solution)/shard_map/ppermute | solution.py:247
  45.5 1.9 %collective-permute-start.3 = (bf16[8,48,128]{2,1,0:T(8,128)(2,1)S(1)}, bf16[8,48,128]{2,1,0:T(8,128)(2,1)S(1)}, u32[]{:S(2)}, u32[]{:S(2)}) collective-permute-start(bf16[8,48,128]{2,1,0:T(8,128)(2,1)S(1)} %collective-permute-done.2.r2_ref), channel_id=1, source_target_pairs={{0,4},{4,0},{1,5},{5,1},{2,6},{6,2},{3,7},{7,3},{8,12},{12,8},{9,1... | collective-permute-start | bytes 294920 | tf_op jit(solution)/shard_map/ppermute | solution.py:48
  47.4 0.9 collective-permute-done.3.w2_ref
  48.3 1.8 %collective-permute-start.5 = (bf16[1024,384]{1,0:T(8,128)(2,1)S(1)}, bf16[1024,384]{1,0:T(8,128)(2,1)S(1)}, u32[]{:S(2)}, u32[]{:S(2)}) collective-permute-start(bf16[1024,384]{1,0:T(8,128)(2,1)S(1)} %collective-permute-done.t1), channel_id=1, source_target_pairs={{0,1},{1,2},{2,3},{3,0},{4,7},{5,4},{6,5},{7,6},{8,9},{9,10},{10,1... | collective-permute-start | bytes 2359304 | tf_op jit(solution)/shard_map/ppermute | solution.py:44
  50.2 0.7 pack_shard.1
  50.9 0.2 collective-permute-start.8
  51.1 1.1 %collective-permute-start.9 = (bf16[16,2,48,128]{3,2,1,0:T(8,128)(2,1)S(1)}, bf16[16,2,48,128]{3,2,1,0:T(8,128)(2,1)S(1)}, u32[]{:S(2)}, u32[]{:S(2)}) collective-permute-start(bf16[16,2,48,128]{3,2,1,0:T(8,128)(2,1)S(1)} %get-tuple-element.20.rest_1_), channel_id=1, source_target_pairs={{0,32},{4,228},{32,64},{36,4},{64,96},{68,36},{96,128},{100,68},{1... | collective-permute-start | bytes 1179656 | tf_op jit(solution)/shard_map/ppermute | solution.py:36
  52.2 1.0 %collective-permute-start.14 = (bf16[16,2,48,128]{3,2,1,0:T(8,128)(2,1)S(1)}, bf16[16,2,48,128]{3,2,1,0:T(8,128)(2,1)S(1)}, u32[]{:S(2)}, u32[]{:S(2)}) collective-permute-start(bf16[16,2,48,128]{3,2,1,0:T(8,128)(2,1)S(1)} %get-tuple-element.19.rest_0_), channel_id=1, source_target_pairs={{0,8},{4,28},{8,16},{12,4},{16,24},{20,12},{24,0},{28,20},{1,9},{5... | collective-permute-start | bytes 1179656 | tf_op jit(solution)/shard_map/ppermute | solution.py:40
  53.3 4.6 %collective-permute-done.8.rest_2_ = bf16[16,2,48,128]{3,2,1,0:T(8,128)(2,1)S(1)} collective-permute-done((bf16[16,2,48,128]{3,2,1,0:T(8,128)(2,1)S(1)}, bf16[16,2,48,128]{3,2,1,0:T(8,128)(2,1)S(1)}, u32[]{:S(2)}, u32[]{:S(2)}) %collective-permute-start.8) | collective-permute-done | bytes 393248 | tf_op jit(solution)/shard_map/ppermute | solution.py:36
  57.9 1.4 %collective-permute-start.12 = (bf16[16,2,48,128]{3,2,1,0:T(8,128)(2,1)S(1)}, bf16[16,2,48,128]{3,2,1,0:T(8,128)(2,1)S(1)}, u32[]{:S(2)}, u32[]{:S(2)}) collective-permute-start(bf16[16,2,48,128]{3,2,1,0:T(8,128)(2,1)S(1)} %collective-permute-done.8.rest_2_), channel_id=1, source_target_pairs={{0,32},{4,228},{32,64},{36,4},{64,96},{68,36},{96,128},{100,68},{1... | collective-permute-start | bytes 1179656 | tf_op jit(solution)/shard_map/ppermute | solution.py:36
  59.3 2.8 %collective-permute-done.9.rest_3_ = bf16[16,2,48,128]{3,2,1,0:T(8,128)(2,1)S(1)} collective-permute-done((bf16[16,2,48,128]{3,2,1,0:T(8,128)(2,1)S(1)}, bf16[16,2,48,128]{3,2,1,0:T(8,128)(2,1)S(1)}, u32[]{:S(2)}, u32[]{:S(2)}) %collective-permute-start.9) | collective-permute-done | bytes 393248 | tf_op jit(solution)/shard_map/ppermute | solution.py:36
  62.1 1.4 %collective-permute-start.17 = (bf16[16,2,48,128]{3,2,1,0:T(8,128)(2,1)S(1)}, bf16[16,2,48,128]{3,2,1,0:T(8,128)(2,1)S(1)}, u32[]{:S(2)}, u32[]{:S(2)}) collective-permute-start(bf16[16,2,48,128]{3,2,1,0:T(8,128)(2,1)S(1)} %collective-permute-done.9.rest_3_), channel_id=1, source_target_pairs={{0,8},{4,28},{8,16},{12,4},{16,24},{20,12},{24,0},{28,20},{1,9},{5... | collective-permute-start | bytes 1179656 | tf_op jit(solution)/shard_map/ppermute | solution.py:40
  63.5 2.8 %collective-permute-done.4.t2 = bf16[1024,384]{1,0:T(8,128)(2,1)S(1)} collective-permute-done((bf16[1024,384]{1,0:T(8,128)(2,1)S(1)}, bf16[1024,384]{1,0:T(8,128)(2,1)S(1)}, u32[]{:S(2)}, u32[]{:S(2)}) %collective-permute-start.4) | collective-permute-done | bytes 786464 | tf_op jit(solution)/shard_map/ppermute | solution.py:44
  66.3 1.1 %collective-permute-start.11 = (bf16[16,2,48,128]{3,2,1,0:T(8,128)(2,1)S(1)}, bf16[16,2,48,128]{3,2,1,0:T(8,128)(2,1)S(1)}, u32[]{:S(2)}, u32[]{:S(2)}) collective-permute-start(bf16[16,2,48,128]{3,2,1,0:T(8,128)(2,1)S(1)} %collective-permute-done.9.rest_3_), channel_id=1, source_target_pairs={{0,4},{4,0},{1,5},{5,1},{2,6},{6,2},{3,7},{7,3},{8,12},{12,8},{9,1... | collective-permute-start | bytes 1179656 | tf_op jit(solution)/shard_map/ppermute | solution.py:48
  67.4 0.1 collective-permute-start.15
  67.5 0.9 copy-done.9
  68.4 1.4 %collective-permute-start.16 = (bf16[16,2,48,128]{3,2,1,0:T(8,128)(2,1)S(1)}, bf16[16,2,48,128]{3,2,1,0:T(8,128)(2,1)S(1)}, u32[]{:S(2)}, u32[]{:S(2)}) collective-permute-start(bf16[16,2,48,128]{3,2,1,0:T(8,128)(2,1)S(1)} %collective-permute-done.8.rest_2_), channel_id=1, source_target_pairs={{0,8},{4,28},{8,16},{12,4},{16,24},{20,12},{24,0},{28,20},{1,9},{5... | collective-permute-start | bytes 1179656 | tf_op jit(solution)/shard_map/ppermute | solution.py:40
  69.8 0.6 collective-permute-start.20
  70.4 2.1 %collective-permute-start.10 = (bf16[16,2,48,128]{3,2,1,0:T(8,128)(2,1)S(1)}, bf16[16,2,48,128]{3,2,1,0:T(8,128)(2,1)S(1)}, u32[]{:S(2)}, u32[]{:S(2)}) collective-permute-start(bf16[16,2,48,128]{3,2,1,0:T(8,128)(2,1)S(1)} %collective-permute-done.8.rest_2_), channel_id=1, source_target_pairs={{0,4},{4,0},{1,5},{5,1},{2,6},{6,2},{3,7},{7,3},{8,12},{12,8},{9,1... | collective-permute-start | bytes 1179656 | tf_op jit(solution)/shard_map/ppermute | solution.py:48
  72.5 0.1 collective-permute-start.13
  72.6 0.4 collective-permute-start.19
  73.0 2.3 %collective-permute-done.16.rest_10_ = bf16[16,2,48,128]{3,2,1,0:T(8,128)(2,1)S(1)} collective-permute-done((bf16[16,2,48,128]{3,2,1,0:T(8,128)(2,1)S(1)}, bf16[16,2,48,128]{3,2,1,0:T(8,128)(2,1)S(1)}, u32[]{:S(2)}, u32[]{:S(2)}) %collective-permute-start.16) | collective-permute-done | bytes 393248 | tf_op jit(solution)/shard_map/ppermute | solution.py:40
  75.4 3.1 %collective-permute-start.18 = (bf16[16,2,48,128]{3,2,1,0:T(8,128)(2,1)S(1)}, bf16[16,2,48,128]{3,2,1,0:T(8,128)(2,1)S(1)}, u32[]{:S(2)}, u32[]{:S(2)}) collective-permute-start(bf16[16,2,48,128]{3,2,1,0:T(8,128)(2,1)S(1)} %collective-permute-done.16.rest_10_), channel_id=1, source_target_pairs={{0,4},{4,0},{1,5},{5,1},{2,6},{6,2},{3,7},{7,3},{8,12},{12,8},{9,1... | collective-permute-start | bytes 1179656 | tf_op jit(solution)/shard_map/ppermute | solution.py:48
  78.4 1.1 %collective-permute-done.20.rest_14_ = bf16[16,2,48,128]{3,2,1,0:T(8,128)(2,1)S(1)} collective-permute-done((bf16[16,2,48,128]{3,2,1,0:T(8,128)(2,1)S(1)}, bf16[16,2,48,128]{3,2,1,0:T(8,128)(2,1)S(1)}, u32[]{:S(2)}, u32[]{:S(2)}) %collective-permute-start.20) | collective-permute-done | bytes 393248 | tf_op jit(solution)/shard_map/ppermute | solution.py:40
  79.6 3.1 %collective-permute-start.21 = (bf16[16,2,48,128]{3,2,1,0:T(8,128)(2,1)S(1)}, bf16[16,2,48,128]{3,2,1,0:T(8,128)(2,1)}, u32[]{:S(2)}, u32[]{:S(2)}) collective-permute-start(bf16[16,2,48,128]{3,2,1,0:T(8,128)(2,1)S(1)} %collective-permute-done.20.rest_14_), channel_id=1, source_target_pairs={{0,4},{4,0},{1,5},{5,1},{2,6},{6,2},{3,7},{7,3},{8,12},{12,8},{9,1... | collective-permute-start | bytes 1179656 | tf_op jit(solution)/shard_map/ppermute | solution.py:48
  82.8 0.7 copy-done.19
  83.5 0.1 copy-done.21
  83.6 0.2 copy-done.22
  83.8 0.8 copy-done.20
  84.6 13.2 %ladder.1 = bf16[1024,2048]{1,0:T(8,128)(2,1)} custom-call(s32[4]{0:T(128)} %copy-done.3, s32[8,16]{1,0:T(8,128)} %mask_ref.3, bf16[1024,384]{1,0:T(8,128)(2,1)} %copy-done.1, bf16[1024,384]{1,0:T(8,128)(2,1)} %copy-done.7, bf16[1024,384]{1,0:T(8,128)(2,1)} %copy-done.8, bf16[1024,384]{1,0:T(8,128)(2,1)} %copy-done.9, bf16[1024,2048]{1,0:T(8,128)(2,1)} %r_ref.1, ...), custom_call_target="tpu_custom_call" | custom-call | flops 6442450944 | bytes 17825792 | tf_op jit(solution)/shard_map/ladder/pallas_call | solution.py:216
  (52 shorter events, 0.1 us)
Async XLA Ops:
  1.5 1.1 %copy-start = (bf16[1024,384]{1,0:T(8,128)(2,1)S(1)}, bf16[1024,384]{1,0:T(8,128)(2,1)}, u32[]{:S(2)}) copy-start(bf16[1024,384]{1,0:T(8,128)(2,1)} %t_ref.1) | copy-start | bytes 2359300
  3.5 0.9 copy-start.2
  4.4 80.1 %copy-start.1 = (bf16[1024,384]{1,0:T(8,128)(2,1)}, bf16[1024,384]{1,0:T(8,128)(2,1)S(1)}, u32[]{:S(2)}) copy-start(bf16[1024,384]{1,0:T(8,128)(2,1)S(1)} %keep_t.1.t0) | copy-start | bytes 2359300
  5.8 25.8 %all-to-all-start = ((bf16[32,48,128]{2,1,0:T(8,128)(2,1)}), bf16[32,48,128]{2,1,0:T(8,128)(2,1)S(1)}, u32[]{:S(2)}, u32[]{:S(2)}) async-start(bf16[32,48,128]{2,1,0:T(8,128)(2,1)} %spread_v.1), calls=%async_computation | async-start | bytes 786432 | tf_op jit(solution)/shard_map/all_to_all | solution.py:243
  17.8 29.6 %collective-permute-start = (bf16[1024,384]{1,0:T(8,128)(2,1)S(1)}, bf16[1024,384]{1,0:T(8,128)(2,1)S(1)}, u32[]{:S(2)}, u32[]{:S(2)}) collective-permute-start(bf16[1024,384]{1,0:T(8,128)(2,1)S(1)} %keep_t.1.t0), channel_id=1, source_target_pairs={{0,1},{1,2},{2,3},{3,0},{4,7},{5,4},{6,5},{7,6},{8,9},{9,10},{10,1... | collective-permute-start | bytes 2359304 | tf_op jit(solution)/shard_map/ppermute | solution.py:44
  31.6 3.8 %collective-permute-start.1 = (bf16[32,48,128]{2,1,0:T(8,128)(2,1)S(1)}, bf16[32,48,128]{2,1,0:T(8,128)(2,1)S(1)}, u32[]{:S(2)}, u32[]{:S(2)}) collective-permute-start(bf16[32,48,128]{2,1,0:T(8,128)(2,1)S(1)} %all-to-all-done.a_ref), channel_id=1, source_target_pairs={{0,4},{4,0},{1,5},{5,1},{2,6},{6,2},{3,7},{7,3},{8,12},{12,8},{9,1... | collective-permute-start | bytes 1179656 | tf_op jit(solution)/shard_map/ppermute | solution.py:48
  34.2 50.3 %copy-start.3 = (s32[4]{0:T(128)}, s32[4]{0:T(128)S(1)}, u32[]{:S(2)}) copy-start(s32[4]{0:T(128)S(1)} %pad_add_fusion.place_ref) | copy-start | bytes 52
  35.5 0.7 copy-start.4
  37.0 7.3 %collective-permute-start.6 = (bf16[16,48,128]{2,1,0:T(8,128)(2,1)S(1)}, bf16[16,48,128]{2,1,0:T(8,128)(2,1)S(1)}, u32[]{:S(2)}, u32[]{:S(2)}) collective-permute-start(bf16[16,48,128]{2,1,0:T(8,128)(2,1)S(1)} %get-tuple-element.18), channel_id=1, source_target_pairs={{0,1},{1,2},{2,3},{3,0},{4,7},{5,4},{6,5},{7,6},{8,9},{9,10},{10,1... | collective-permute-start | bytes 589832 | tf_op jit(solution)/shard_map/ppermute | solution.py:44
  39.5 6.0 %collective-permute-start.2 = (bf16[8,48,128]{2,1,0:T(8,128)(2,1)S(1)}, bf16[8,48,128]{2,1,0:T(8,128)(2,1)S(1)}, u32[]{:S(2)}, u32[]{:S(2)}) collective-permute-start(bf16[8,48,128]{2,1,0:T(8,128)(2,1)S(1)} %get-tuple-element.15), channel_id=1, source_target_pairs={{0,2},{1,3},{2,0},{3,1},{4,6},{5,7},{6,4},{7,5},{8,10},{9,11},{10,... | collective-permute-start | bytes 294920 | tf_op jit(solution)/shard_map/ppermute | solution.py:247
  44.3 5.9 %collective-permute-start.7 = (bf16[16,48,128]{2,1,0:T(8,128)(2,1)S(1)}, bf16[16,48,128]{2,1,0:T(8,128)(2,1)S(1)}, u32[]{:S(2)}, u32[]{:S(2)}) collective-permute-start(bf16[16,48,128]{2,1,0:T(8,128)(2,1)S(1)} %collective-permute-done.6.r1_ref), channel_id=1, source_target_pairs={{0,4},{4,0},{1,5},{5,1},{2,6},{6,2},{3,7},{7,3},{8,12},{12,8},{9,1... | collective-permute-start | bytes 589832 | tf_op jit(solution)/shard_map/ppermute | solution.py:48
  45.5 2.8 %collective-permute-start.3 = (bf16[8,48,128]{2,1,0:T(8,128)(2,1)S(1)}, bf16[8,48,128]{2,1,0:T(8,128)(2,1)S(1)}, u32[]{:S(2)}, u32[]{:S(2)}) collective-permute-start(bf16[8,48,128]{2,1,0:T(8,128)(2,1)S(1)} %collective-permute-done.2.r2_ref), channel_id=1, source_target_pairs={{0,4},{4,0},{1,5},{5,1},{2,6},{6,2},{3,7},{7,3},{8,12},{12,8},{9,1... | collective-permute-start | bytes 294920 | tf_op jit(solution)/shard_map/ppermute | solution.py:48
  47.4 18.9 %collective-permute-start.4 = (bf16[1024,384]{1,0:T(8,128)(2,1)S(1)}, bf16[1024,384]{1,0:T(8,128)(2,1)S(1)}, u32[]{:S(2)}, u32[]{:S(2)}) collective-permute-start(bf16[1024,384]{1,0:T(8,128)(2,1)S(1)} %keep_t.1.t0), channel_id=1, source_target_pairs={{0,3},{1,0},{2,1},{3,2},{4,5},{5,6},{6,7},{7,4},{8,11},{9,8},{10,9... | collective-permute-start | bytes 2359304 | tf_op jit(solution)/shard_map/ppermute | solution.py:44
  47.4 37.1 %copy-start.7 = (bf16[1024,384]{1,0:T(8,128)(2,1)}, bf16[1024,384]{1,0:T(8,128)(2,1)S(1)}, u32[]{:S(2)}) copy-start(bf16[1024,384]{1,0:T(8,128)(2,1)S(1)} %collective-permute-done.t1) | copy-start | bytes 2359300
  48.3 19.2 %collective-permute-start.5 = (bf16[1024,384]{1,0:T(8,128)(2,1)S(1)}, bf16[1024,384]{1,0:T(8,128)(2,1)S(1)}, u32[]{:S(2)}, u32[]{:S(2)}) collective-permute-start(bf16[1024,384]{1,0:T(8,128)(2,1)S(1)} %collective-permute-done.t1), channel_id=1, source_target_pairs={{0,1},{1,2},{2,3},{3,0},{4,7},{5,4},{6,5},{7,6},{8,9},{9,10},{10,1... | collective-permute-start | bytes 2359304 | tf_op jit(solution)/shard_map/ppermute | solution.py:44
  50.9 33.7 %copy-start.5 = (bf16[16,2,48,128]{3,2,1,0:T(8,128)(2,1)}, bf16[16,2,48,128]{3,2,1,0:T(8,128)(2,1)S(1)}, u32[]{:S(2)}) copy-start(bf16[16,2,48,128]{3,2,1,0:T(8,128)(2,1)S(1)} %get-tuple-element.19.rest_0_) | copy-start | bytes 1179652
  50.9 33.7 %copy-start.6 = (bf16[16,2,48,128]{3,2,1,0:T(8,128)(2,1)}, bf16[16,2,48,128]{3,2,1,0:T(8,128)(2,1)S(1)}, u32[]{:S(2)}) copy-start(bf16[16,2,48,128]{3,2,1,0:T(8,128)(2,1)S(1)} %get-tuple-element.20.rest_1_) | copy-start | bytes 1179652
  50.9 7.0 %collective-permute-start.8 = (bf16[16,2,48,128]{3,2,1,0:T(8,128)(2,1)S(1)}, bf16[16,2,48,128]{3,2,1,0:T(8,128)(2,1)S(1)}, u32[]{:S(2)}, u32[]{:S(2)}) collective-permute-start(bf16[16,2,48,128]{3,2,1,0:T(8,128)(2,1)S(1)} %get-tuple-element.19.rest_0_), channel_id=1, source_target_pairs={{0,32},{4,228},{32,64},{36,4},{64,96},{68,36},{96,128},{100,68},{1... | collective-permute-start | bytes 1179656 | tf_op jit(solution)/shard_map/ppermute | solution.py:36
  51.1 11.0 %collective-permute-start.9 = (bf16[16,2,48,128]{3,2,1,0:T(8,128)(2,1)S(1)}, bf16[16,2,48,128]{3,2,1,0:T(8,128)(2,1)S(1)}, u32[]{:S(2)}, u32[]{:S(2)}) collective-permute-start(bf16[16,2,48,128]{3,2,1,0:T(8,128)(2,1)S(1)} %get-tuple-element.20.rest_1_), channel_id=1, source_target_pairs={{0,32},{4,228},{32,64},{36,4},{64,96},{68,36},{96,128},{100,68},{1... | collective-permute-start | bytes 1179656 | tf_op jit(solution)/shard_map/ppermute | solution.py:36
  52.2 15.2 %collective-permute-start.14 = (bf16[16,2,48,128]{3,2,1,0:T(8,128)(2,1)S(1)}, bf16[16,2,48,128]{3,2,1,0:T(8,128)(2,1)S(1)}, u32[]{:S(2)}, u32[]{:S(2)}) collective-permute-start(bf16[16,2,48,128]{3,2,1,0:T(8,128)(2,1)S(1)} %get-tuple-element.19.rest_0_), channel_id=1, source_target_pairs={{0,8},{4,28},{8,16},{12,4},{16,24},{20,12},{24,0},{28,20},{1,9},{5... | collective-permute-start | bytes 1179656 | tf_op jit(solution)/shard_map/ppermute | solution.py:40
  57.9 26.7 %copy-start.10 = (bf16[16,2,48,128]{3,2,1,0:T(8,128)(2,1)}, bf16[16,2,48,128]{3,2,1,0:T(8,128)(2,1)S(1)}, u32[]{:S(2)}) copy-start(bf16[16,2,48,128]{3,2,1,0:T(8,128)(2,1)S(1)} %collective-permute-done.8.rest_2_) | copy-start | bytes 1179652
  57.9 11.9 %collective-permute-start.12 = (bf16[16,2,48,128]{3,2,1,0:T(8,128)(2,1)S(1)}, bf16[16,2,48,128]{3,2,1,0:T(8,128)(2,1)S(1)}, u32[]{:S(2)}, u32[]{:S(2)}) collective-permute-start(bf16[16,2,48,128]{3,2,1,0:T(8,128)(2,1)S(1)} %collective-permute-done.8.rest_2_), channel_id=1, source_target_pairs={{0,32},{4,228},{32,64},{36,4},{64,96},{68,36},{96,128},{100,68},{1... | collective-permute-start | bytes 1179656 | tf_op jit(solution)/shard_map/ppermute | solution.py:36
  62.1 22.5 %copy-start.11 = (bf16[16,2,48,128]{3,2,1,0:T(8,128)(2,1)}, bf16[16,2,48,128]{3,2,1,0:T(8,128)(2,1)S(1)}, u32[]{:S(2)}) copy-start(bf16[16,2,48,128]{3,2,1,0:T(8,128)(2,1)S(1)} %collective-permute-done.9.rest_3_) | copy-start | bytes 1179652
  62.1 8.3 %collective-permute-start.17 = (bf16[16,2,48,128]{3,2,1,0:T(8,128)(2,1)S(1)}, bf16[16,2,48,128]{3,2,1,0:T(8,128)(2,1)S(1)}, u32[]{:S(2)}, u32[]{:S(2)}) collective-permute-start(bf16[16,2,48,128]{3,2,1,0:T(8,128)(2,1)S(1)} %collective-permute-done.9.rest_3_), channel_id=1, source_target_pairs={{0,8},{4,28},{8,16},{12,4},{16,24},{20,12},{24,0},{28,20},{1,9},{5... | collective-permute-start | bytes 1179656 | tf_op jit(solution)/shard_map/ppermute | solution.py:40
  66.3 18.3 %copy-start.8 = (bf16[1024,384]{1,0:T(8,128)(2,1)}, bf16[1024,384]{1,0:T(8,128)(2,1)S(1)}, u32[]{:S(2)}) copy-start(bf16[1024,384]{1,0:T(8,128)(2,1)S(1)} %collective-permute-done.4.t2) | copy-start | bytes 2359300
  66.3 6.2 %collective-permute-start.11 = (bf16[16,2,48,128]{3,2,1,0:T(8,128)(2,1)S(1)}, bf16[16,2,48,128]{3,2,1,0:T(8,128)(2,1)S(1)}, u32[]{:S(2)}, u32[]{:S(2)}) collective-permute-start(bf16[16,2,48,128]{3,2,1,0:T(8,128)(2,1)S(1)} %collective-permute-done.9.rest_3_), channel_id=1, source_target_pairs={{0,4},{4,0},{1,5},{5,1},{2,6},{6,2},{3,7},{7,3},{8,12},{12,8},{9,1... | collective-permute-start | bytes 1179656 | tf_op jit(solution)/shard_map/ppermute | solution.py:48
  67.4 15.2 %copy-start.12 = (bf16[16,2,48,128]{3,2,1,0:T(8,128)(2,1)}, bf16[16,2,48,128]{3,2,1,0:T(8,128)(2,1)S(1)}, u32[]{:S(2)}) copy-start(bf16[16,2,48,128]{3,2,1,0:T(8,128)(2,1)S(1)} %collective-permute-done.14.rest_8_) | copy-start | bytes 1179652
  67.4 5.2 %collective-permute-start.15 = (bf16[16,2,48,128]{3,2,1,0:T(8,128)(2,1)S(1)}, bf16[16,2,48,128]{3,2,1,0:T(8,128)(2,1)S(1)}, u32[]{:S(2)}, u32[]{:S(2)}) collective-permute-start(bf16[16,2,48,128]{3,2,1,0:T(8,128)(2,1)S(1)} %collective-permute-done.14.rest_8_), channel_id=1, source_target_pairs={{0,4},{4,0},{1,5},{5,1},{2,6},{6,2},{3,7},{7,3},{8,12},{12,8},{9,1... | collective-permute-start | bytes 1179656 | tf_op jit(solution)/shard_map/ppermute | solution.py:48
  67.5 0.9 copy-start.9
  68.4 6.9 %collective-permute-start.16 = (bf16[16,2,48,128]{3,2,1,0:T(8,128)(2,1)S(1)}, bf16[16,2,48,128]{3,2,1,0:T(8,128)(2,1)S(1)}, u32[]{:S(2)}, u32[]{:S(2)}) collective-permute-start(bf16[16,2,48,128]{3,2,1,0:T(8,128)(2,1)S(1)} %collective-permute-done.8.rest_2_), channel_id=1, source_target_pairs={{0,8},{4,28},{8,16},{12,4},{16,24},{20,12},{24,0},{28,20},{1,9},{5... | collective-permute-start | bytes 1179656 | tf_op jit(solution)/shard_map/ppermute | solution.py:40
  69.8 12.8 %copy-start.13 = (bf16[16,2,48,128]{3,2,1,0:T(8,128)(2,1)}, bf16[16,2,48,128]{3,2,1,0:T(8,128)(2,1)S(1)}, u32[]{:S(2)}) copy-start(bf16[16,2,48,128]{3,2,1,0:T(8,128)(2,1)S(1)} %collective-permute-done.12.rest_6_) | copy-start | bytes 1179652
  69.8 9.7 %collective-permute-start.20 = (bf16[16,2,48,128]{3,2,1,0:T(8,128)(2,1)S(1)}, bf16[16,2,48,128]{3,2,1,0:T(8,128)(2,1)S(1)}, u32[]{:S(2)}, u32[]{:S(2)}) collective-permute-start(bf16[16,2,48,128]{3,2,1,0:T(8,128)(2,1)S(1)} %collective-permute-done.12.rest_6_), channel_id=1, source_target_pairs={{0,8},{4,28},{8,16},{12,4},{16,24},{20,12},{24,0},{28,20},{1,9},{5... | collective-permute-start | bytes 1179656 | tf_op jit(solution)/shard_map/ppermute | solution.py:40
  70.4 12.3 %copy-start.14 = (bf16[16,2,48,128]{3,2,1,0:T(8,128)(2,1)}, bf16[16,2,48,128]{3,2,1,0:T(8,128)(2,1)S(1)}, u32[]{:S(2)}) copy-start(bf16[16,2,48,128]{3,2,1,0:T(8,128)(2,1)S(1)} %collective-permute-done.17.rest_11_) | copy-start | bytes 1179652
  70.4 12.2 %collective-permute-start.10 = (bf16[16,2,48,128]{3,2,1,0:T(8,128)(2,1)S(1)}, bf16[16,2,48,128]{3,2,1,0:T(8,128)(2,1)S(1)}, u32[]{:S(2)}, u32[]{:S(2)}) collective-permute-start(bf16[16,2,48,128]{3,2,1,0:T(8,128)(2,1)S(1)} %collective-permute-done.8.rest_2_), channel_id=1, source_target_pairs={{0,4},{4,0},{1,5},{5,1},{2,6},{6,2},{3,7},{7,3},{8,12},{12,8},{9,1... | collective-permute-start | bytes 1179656 | tf_op jit(solution)/shard_map/ppermute | solution.py:48
  72.5 10.2 %copy-start.15 = (bf16[16,2,48,128]{3,2,1,0:T(8,128)(2,1)}, bf16[16,2,48,128]{3,2,1,0:T(8,128)(2,1)S(1)}, u32[]{:S(2)}) copy-start(bf16[16,2,48,128]{3,2,1,0:T(8,128)(2,1)S(1)} %collective-permute-done.11.rest_5_) | copy-start | bytes 1179652
  72.5 10.2 %collective-permute-start.13 = (bf16[16,2,48,128]{3,2,1,0:T(8,128)(2,1)S(1)}, bf16[16,2,48,128]{3,2,1,0:T(8,128)(2,1)S(1)}, u32[]{:S(2)}, u32[]{:S(2)}) collective-permute-start(bf16[16,2,48,128]{3,2,1,0:T(8,128)(2,1)S(1)} %collective-permute-done.12.rest_6_), channel_id=1, source_target_pairs={{0,4},{4,0},{1,5},{5,1},{2,6},{6,2},{3,7},{7,3},{8,12},{12,8},{9,1... | collective-permute-start | bytes 1179656 | tf_op jit(solution)/shard_map/ppermute | solution.py:48
  72.6 10.1 %copy-start.16 = (bf16[16,2,48,128]{3,2,1,0:T(8,128)(2,1)}, bf16[16,2,48,128]{3,2,1,0:T(8,128)(2,1)S(1)}, u32[]{:S(2)}) copy-start(bf16[16,2,48,128]{3,2,1,0:T(8,128)(2,1)S(1)} %collective-permute-done.15.rest_9_) | copy-start | bytes 1179652
  72.6 10.0 %collective-permute-start.19 = (bf16[16,2,48,128]{3,2,1,0:T(8,128)(2,1)S(1)}, bf16[16,2,48,128]{3,2,1,0:T(8,128)(2,1)S(1)}, u32[]{:S(2)}, u32[]{:S(2)}) collective-permute-start(bf16[16,2,48,128]{3,2,1,0:T(8,128)(2,1)S(1)} %collective-permute-done.17.rest_11_), channel_id=1, source_target_pairs={{0,4},{4,0},{1,5},{5,1},{2,6},{6,2},{3,7},{7,3},{8,12},{12,8},{9,1... | collective-permute-start | bytes 1179656 | tf_op jit(solution)/shard_map/ppermute | solution.py:48
  75.4 7.4 %copy-start.17 = (bf16[16,2,48,128]{3,2,1,0:T(8,128)(2,1)}, bf16[16,2,48,128]{3,2,1,0:T(8,128)(2,1)S(1)}, u32[]{:S(2)}) copy-start(bf16[16,2,48,128]{3,2,1,0:T(8,128)(2,1)S(1)} %collective-permute-done.16.rest_10_) | copy-start | bytes 1179652
  75.4 7.3 %collective-permute-start.18 = (bf16[16,2,48,128]{3,2,1,0:T(8,128)(2,1)S(1)}, bf16[16,2,48,128]{3,2,1,0:T(8,128)(2,1)S(1)}, u32[]{:S(2)}, u32[]{:S(2)}) collective-permute-start(bf16[16,2,48,128]{3,2,1,0:T(8,128)(2,1)S(1)} %collective-permute-done.16.rest_10_), channel_id=1, source_target_pairs={{0,4},{4,0},{1,5},{5,1},{2,6},{6,2},{3,7},{7,3},{8,12},{12,8},{9,1... | collective-permute-start | bytes 1179656 | tf_op jit(solution)/shard_map/ppermute | solution.py:48
  79.6 3.2 %copy-start.18 = (bf16[16,2,48,128]{3,2,1,0:T(8,128)(2,1)}, bf16[16,2,48,128]{3,2,1,0:T(8,128)(2,1)S(1)}, u32[]{:S(2)}) copy-start(bf16[16,2,48,128]{3,2,1,0:T(8,128)(2,1)S(1)} %collective-permute-done.20.rest_14_) | copy-start | bytes 1179652
  79.6 5.0 %collective-permute-start.21 = (bf16[16,2,48,128]{3,2,1,0:T(8,128)(2,1)S(1)}, bf16[16,2,48,128]{3,2,1,0:T(8,128)(2,1)}, u32[]{:S(2)}, u32[]{:S(2)}) collective-permute-start(bf16[16,2,48,128]{3,2,1,0:T(8,128)(2,1)S(1)} %collective-permute-done.20.rest_14_), channel_id=1, source_target_pairs={{0,4},{4,0},{1,5},{5,1},{2,6},{6,2},{3,7},{7,3},{8,12},{12,8},{9,1... | collective-permute-start | bytes 1179656 | tf_op jit(solution)/shard_map/ppermute | solution.py:48
  82.7 0.8 copy-start.19
  82.7 0.9 copy-start.21
  82.7 1.1 %copy-start.22 = (bf16[16,2,48,128]{3,2,1,0:T(8,128)(2,1)}, bf16[16,2,48,128]{3,2,1,0:T(8,128)(2,1)S(1)}, u32[]{:S(2)}) copy-start(bf16[16,2,48,128]{3,2,1,0:T(8,128)(2,1)S(1)} %collective-permute-done.18.rest_12_) | copy-start | bytes 1179652
  83.8 0.8 copy-start.20

commit v2 on v0

v2 whole, which is shorter than its diff:
```python
import functools

import jax
import jax.numpy as jnp
from jax import lax
from jax.experimental import pallas as pl
from jax.experimental.pallas import tpu as pltpu
from jax.sharding import Mesh
from jax.sharding import PartitionSpec as P

TILE = 128
NZ, NY, NX = 8, 4, 4
CHUNK = 48
ROWS = 256
COLS = 16
HALF = 8
SMALL = 16 * 1024 * 1024
LARGE = 28 * 1024 * 1024
WHOLE = 60 * 1024 * 1024


def pairs_zc(d):
    return [(z * 2 + c, ((z + (d if c == 0 else -d)) % NZ) * 2 + c) for z in range(NZ) for c in range(2)]


def pairs_yc(d):
    return [(y * 2 + c, ((y + (d if c == 0 else -d)) % NY) * 2 + c) for y in range(NY) for c in range(2)]


def pairs_cx(d):
    return [(c * NX + x, c * NX + (x + (d if c == 0 else -d)) % NX) for c in range(2) for x in range(NX)]


def move_z(name, v):
    with jax.named_scope(name):
        return lax.ppermute(v, ("z", "c"), pairs_zc(1))


def move_y(name, v):
    with jax.named_scope(name):
        return lax.ppermute(v, ("y", "c"), pairs_yc(1))


def move_x(name, v, d=1):
    with jax.named_scope(name):
        return lax.ppermute(v, ("c", "x"), pairs_cx(d))


def swap(name, v):
    with jax.named_scope(name):
        return lax.ppermute(v, "c", [(0, 1), (1, 0)])


def cost(flops, moved):
    return pl.CostEstimate(flops=flops, bytes_accessed=moved, transcendentals=0)


def in_smem():
    return pl.BlockSpec(memory_space=pltpu.SMEM)


def in_vmem():
    return pl.BlockSpec(memory_space=pltpu.VMEM)


def prepare_kernel(t_mask_ref, v_mask_ref, t_ref, v_ref, t_out, v_out, perm):
    rows, cols = t_ref.shape
    z, y, c = (lax.axis_index(n) for n in ("z", "y", "c"))
    s = 1 - 2 * c
    for g in range(8):
        for k in range(CHUNK // 16):
            row = g * CHUNK + k * 16
            v = v_ref[row : row + 16, :]
            v = jnp.where(v_mask_ref[0, row // TILE] != 0, v, jnp.zeros_like(v))
            for zz in range(2):
                for yy in range(2):
                    v_out[(zz * 4 + g // 2) * NY + yy * 2 + g % 2, k * 16 : k * 16 + 16, :] = v

    source = lax.broadcasted_iota(jnp.int32, (cols, cols), 0)
    target = lax.broadcasted_iota(jnp.int32, (cols, cols), 1)
    shift = jnp.zeros((1, cols), jnp.int32)
    lane = lax.broadcasted_iota(jnp.int32, (1, cols), 1)
    steps = ((0, 0), (-s, 0), (s, 0), (0, 1), (2, 0), (-s, 1), (s, 1), (2, 1))
    for q, (dz, dy) in enumerate(steps):
        g = lax.rem(z + dz + NZ, 4) * 2 + lax.rem(y + dy, 2)
        shift = jnp.where(lane >= q * CHUNK, (g - q) * CHUNK, shift)
    perm[...] = jnp.where(source == target + shift, 1.0, 0.0).astype(perm.dtype)

    @pl.loop(0, rows // TILE)
    def _(a):
        at = pl.ds(pl.multiple_of(a * TILE, TILE), TILE)
        tiles = []
        for j in range(cols // TILE):
            t = t_ref[at, j * TILE : (j + 1) * TILE]
            tiles.append(jnp.where(t_mask_ref[j, a] != 0, t, jnp.zeros_like(t)))
        kept = jnp.concatenate(tiles, axis=1)
        t_out[at, :] = jnp.dot(kept, perm[...], preferred_element_type=jnp.float32).astype(t_out.dtype)


def prepare(t_mask, v_mask, t, v):
    return pl.pallas_call(
        prepare_kernel,
        out_shape=(
            jax.ShapeDtypeStruct(t.shape, t.dtype),
            jax.ShapeDtypeStruct((NZ * NY, CHUNK, TILE), v.dtype),
        ),
        in_specs=[in_smem()] * 2 + [in_vmem()] * 2,
        out_specs=(in_vmem(), in_vmem()),
        scratch_shapes=[pltpu.VMEM((t.shape[1], t.shape[1]), t.dtype)],
        compiler_params=pltpu.CompilerParams(vmem_limit_bytes=WHOLE),
        cost_estimate=cost(2 * t.size * t.shape[1], 4 * t.size + 12 * v.size),
        name="prepare",
    )(t_mask.T, v_mask.T, t, v)


def select_kernel(pick_ref, a_ref, b_ref, own_ref, near_ref, far_ref):
    start = 0
    for out_ref in (own_ref, near_ref, far_ref):
        for j in range(out_ref.shape[0]):
            k = pick_ref[start + j]
            chip = lax.rem(k, NZ * NY)
            out_ref[j] = jnp.where(k < NZ * NY, a_ref[chip], b_ref[chip])
        start += out_ref.shape[0]


def select(picks, a, b):
    shape = lambda n: jax.ShapeDtypeStruct((n, CHUNK, TILE), a.dtype)
    return pl.pallas_call(
        select_kernel,
        out_shape=(shape(COLS), shape(COLS), shape(HALF)),
        in_specs=[in_smem(), in_vmem(), in_vmem()],
        out_specs=(in_vmem(),) * 3,
        compiler_params=pltpu.CompilerParams(vmem_limit_bytes=SMALL),
        cost_estimate=cost(0, 2 << 20),
        name="select_columns",
    )(picks, a, b)


def column_picks(order):
    c, x = lax.axis_index("c"), lax.axis_index("x")
    lane = jnp.arange(2 * COLS + HALF, dtype=jnp.int32)
    near = lax.rem(x + 1 - 2 * c + NX, NX) * COLS + lane - COLS
    far = lax.rem(x + 2, NX) * COLS + c * HALF + lane - 2 * COLS
    wanted = jnp.where(lane < COLS, x * COLS + lane, jnp.where(lane < 2 * COLS, near, far))
    stored = jnp.arange(order.shape[0], dtype=jnp.int32)
    held = stored // 2 + jnp.where(stored % 2 == c, 0, NZ * NY)
    return jnp.sum(jnp.where(order[None, :] == wanted[:, None], held[None, :], 0), axis=1).astype(jnp.int32)


def pack_kernel(own_ref, r1_ref, w1_ref, r2_ref, w2_ref, ahead_ref, rest_ref):
    c = lax.axis_index("c")
    for j in range(COLS):
        opposite = jnp.where(c == j // HALF, r2_ref[j % HALF], w2_ref[j % HALF])
        left = jnp.where(c == 0, r1_ref[j], w1_ref[j])
        right = jnp.where(c == 0, w1_ref[j], r1_ref[j])
        ahead_ref[j, 0] = jnp.where(c == 0, own_ref[j], left)
        ahead_ref[j, 1] = jnp.where(c == 0, opposite, right)
        rest_ref[j, 0] = jnp.where(c == 0, left, own_ref[j])
        rest_ref[j, 1] = jnp.where(c == 0, right, opposite)


def pack(own, r1, w1, r2, w2):
    shape = jax.ShapeDtypeStruct((COLS, 2, CHUNK, TILE), own.dtype)
    return pl.pallas_call(
        pack_kernel,
        out_shape=(shape, shape),
        in_specs=[in_vmem()] * 5,
        out_specs=(in_vmem(),) * 2,
        compiler_params=pltpu.CompilerParams(vmem_limit_bytes=SMALL),
        cost_estimate=cost(0, 3 << 20),
        name="pack_shard",
    )(own, r1, w1, r2, w2)


def arrange_kernel(t0, t1, t2, t3, early_ref, late_ref):
    c = lax.axis_index("c")
    rows, cols = t0.shape
    half = cols // 2

    def run(parts):
        @pl.loop(0, rows // TILE)
        def _(a):
            at = pl.ds(pl.multiple_of(a * TILE, TILE), TILE)
            whole = [p[at, :] for p in parts]
            early_ref[at, :] = jnp.concatenate([w[:, :half] for w in whole], axis=1)
            late_ref[at, :] = jnp.concatenate([w[:, half:] for w in whole], axis=1)

    @pl.when(c == 0)
    def _():
        run((t0, t3, t1, t2))

    @pl.when(c != 0)
    def _():
        run((t2, t1, t0, t3))


def arrange(ts):
    rows, cols = ts[0].shape
    shape = jax.ShapeDtypeStruct((rows, NX * cols // 2), ts[0].dtype)
    return pl.pallas_call(
        arrange_kernel,
        out_shape=(shape, shape),
        in_specs=[in_vmem()] * NX,
        out_specs=(in_vmem(), in_vmem()),
        compiler_params=pltpu.CompilerParams(vmem_limit_bytes=SMALL),
        cost_estimate=cost(0, 16 * rows * cols),
        name="arrange_t",
    )(*ts)


def product(t, blocks, n):
    columns = []
    for j in (n, n + 1):
        pieces = [blocks[q + r // 2 * 4][j, r % 2] for r in range(NX) for q in range(4)]
        columns.append(jnp.concatenate(pieces, axis=0))
    return jnp.dot(t, jnp.concatenate(columns, axis=1), preferred_element_type=jnp.float32)


def early_kernel(first, mask_ref, t_ref, r_ref, *rest):
    blocks, acc_ref = rest[:8], rest[8]

    @pl.loop(0, t_ref.shape[0] // ROWS)
    def _(i):
        at = pl.multiple_of(i * ROWS, ROWS)
        t = t_ref[pl.ds(at, ROWS), :]
        for n in range(0, HALF, 2):
            part = product(t, blocks, first + n)
            for a in range(ROWS // TILE):
                rows = pl.ds(pl.multiple_of(at + a * TILE, TILE), TILE)
                for j in range(2):
                    m = mask_ref[i * (ROWS // TILE) + a, first + n + j].astype(jnp.float32)
                    kept = part[a * TILE : (a + 1) * TILE, j * TILE : (j + 1) * TILE] * m
                    old = r_ref[rows, (first + n + j) * TILE : (first + n + j + 1) * TILE].astype(jnp.float32)
                    acc_ref[rows, (n + j) * TILE : (n + j + 1) * TILE] = old + kept


def early(first, r_mask, t, r_old, blocks):
    rows, depth = t.shape
    width = HALF * TILE
    return pl.pallas_call(
        functools.partial(early_kernel, first),
        out_shape=jax.ShapeDtypeStruct((rows, width), jnp.float32),
        in_specs=[in_smem()] + [in_vmem()] * 10,
        out_specs=in_vmem(),
        compiler_params=pltpu.CompilerParams(vmem_limit_bytes=LARGE),
        cost_estimate=cost(2 * rows * depth * width, 6 * rows * width + 2 * rows * depth + 2 * depth * width),
        name="ladder_early",
    )(r_mask, t, r_old, *blocks)


def late_kernel(mask_ref, t_ref, acc0, acc1, *rest):
    blocks, (out_ref, buffer, sems) = rest[:8], rest[8:]
    steps = t_ref.shape[0] // ROWS

    def send(i):
        rows = pl.ds(pl.multiple_of(i * ROWS, ROWS), ROWS)
        return pltpu.make_async_copy(buffer.at[i], out_ref.at[rows, :], sems.at[i])

    @pl.loop(0, steps)
    def _(i):
        at = pl.multiple_of(i * ROWS, ROWS)
        t = t_ref[pl.ds(at, ROWS), :]
        for n in range(0, COLS, 2):
            part = product(t, blocks, n)
            for a in range(ROWS // TILE):
                rows = pl.ds(pl.multiple_of(at + a * TILE, TILE), TILE)
                for j in range(2):
                    k = n + j
                    m = mask_ref[i * (ROWS // TILE) + a, k].astype(jnp.float32)
                    kept = part[a * TILE : (a + 1) * TILE, j * TILE : (j + 1) * TILE] * m
                    acc = (acc0, acc1)[k // HALF]
                    total = acc[rows, k % HALF * TILE : (k % HALF + 1) * TILE] + kept
                    buffer[i, a * TILE : (a + 1) * TILE, k * TILE : (k + 1) * TILE] = total.astype(buffer.dtype)
        send(i).start()

    @pl.loop(0, steps)
    def _(i):
        send(i).wait()


def late(r_mask, t, accs, blocks):
    rows, depth = t.shape
    width = COLS * TILE
    return pl.pallas_call(
        late_kernel,
        out_shape=jax.ShapeDtypeStruct((rows, width), t.dtype),
        in_specs=[in_smem()] + [in_vmem()] * 11,
        out_specs=pl.BlockSpec(memory_space=pl.ANY),
        scratch_shapes=[pltpu.VMEM((rows // ROWS, ROWS, width), t.dtype), pltpu.SemaphoreType.DMA((rows // ROWS,))],
        compiler_params=pltpu.CompilerParams(vmem_limit_bytes=LARGE),
        cost_estimate=cost(2 * rows * depth * width, 6 * rows * width + 2 * rows * depth + 2 * depth * width),
        name="ladder_late",
    )(r_mask, t, *accs, *blocks)


def body(t_amp, t_mask, v_int, v_mask, ab_order, r_mask, r_old):
    hold = lax.optimization_barrier
    picks = column_picks(ab_order)
    t0, spread = prepare(t_mask, v_mask, t_amp, v_int)
    t1 = move_x("t_near", t0)
    t2 = move_x("t_back", t0, -1)
    mine = lax.all_to_all(spread, ("z", "y"), 0, 0)
    partner = swap("v_swap", mine)
    own, near, opposite = select(picks, mine, partner)

    r1 = move_x("r_near", near)
    with jax.named_scope("r_far"):
        r2 = lax.ppermute(opposite, "x", [(i, (i + 2) % NX) for i in range(NX)])
    w1, w2 = swap("r_near_swap", r1), swap("r_far_swap", r2)
    t1, t2, w2 = hold((t1, t2, w2))
    ahead, rest = pack(own, r1, w1, r2, w2)
    t3 = move_x("t_far", t1)

    p1a = move_z("p1a", ahead)
    p1r = move_z("p1r", rest)
    q0 = move_y("q0", ahead)
    p2, q1a, q1r = move_z("p2", p1a), move_y("q1a", p1a), move_y("q1r", p1r)
    q2 = move_y("q2", p2)
    t_early, t_late = arrange((t0, t1, t2, t3))
    blocks = (ahead, p1a, swap("p1r_swap", p1r), q0, rest, p1r, swap("p1a_swap", p1a), swap("q0_swap", q0))
    acc0 = early(0, r_mask, t_early, r_old, blocks)
    p2, q1a, q1r, acc0 = hold((p2, q1a, q1r, acc0))
    acc1 = early(HALF, r_mask, t_early, r_old, blocks)
    q2, acc1 = hold((q2, acc1))
    swapped = [swap(n + "_swap", v) for n, v in (("q1r", q1r), ("p2", p2), ("q1a", q1a), ("q2", q2))]
    blocks = (p2, q1a, swapped[0], q2, swapped[1], q1r, swapped[2], swapped[3])
    return late(r_mask, t_late, (acc0, acc1), blocks)


def solution(mesh):
    torus = Mesh(mesh.devices.reshape(NZ, NY, 2, NX), ("z", "y", "c", "x"))
    pair = ("z", "y", "c")
    placed = (P(pair, "x"), P(pair, "x"), P("x", pair), P("x", pair), P(), P(pair, "x"), P(pair, "x"))
    return jax.shard_map(body, mesh=torus, in_specs=placed, out_specs=P(pair, "x"), check_vma=False)
```

time: 245 us -> 86 us (0.35)
  waiting for transfers between devices: 122 us -> 24.9 us
  local copies, waits for them, and re-layouts: 65.4 us -> 1.14 us
  starting transfers between devices: 0.04 us -> 40.7 us
  Pallas kernels: 0 us -> 17.8 us
  other arithmetic: 18.1 us -> 1 us
  between operations: 13.5 us -> 0.29 us
  blocking collectives: 12.7 us -> 0 us
  matrix products: 11.7 us -> 0 us
    all_gather x2 -> x0, waiting for transfers between devices: 122 us -> none  [the longest x1 122 us: body(): v_full = lax.all_gather(v_deep, 'pair', axis=1, tiled=True)]
    reshape x2 -> x0, local copies, waits for them, and re-layouts: 41.7 us -> none  [the longest x1 32.6 us: body(): blocks = v_full.reshape(v_full.shape[0], -1, tile)]
    ppermute x0 -> x22, starting transfers between devices: none -> 28.6 us  [the longest x10 9.57 us: swap(): return lax.ppermute(v, 'c', [(0, 1), (1, 0)])]
    gather x2 -> x0, local copies, waits for them, and re-layouts: 20.8 us -> none  [body(): jnp.take(blocks, wanted, axis=1)]
    pallas_call x0 -> x7, Pallas kernels: none -> 17.8 us  [the longest x2 6.39 us: early(): pl.pallas_call(functools.partial(early_kernel, first), out_shape=jax.Shap...]
    ppermute x0 -> x22, waiting for transfers between devices: none -> 13.8 us  [the longest x3 5.63 us: move_z(): return lax.ppermute(v, ('z', 'c'), pairs_zc(1))]
    all_gather x1 -> x0, blocking collectives: 12.7 us -> none  [body(): v_deep = lax.all_gather(v_kept, 'rep', axis=0, tiled=True)]
    all_to_all x0 -> x1, starting transfers between devices: none -> 12 us  [body(): mine = lax.all_to_all(spread, ('z', 'y'), 0, 0)]
  transfers between devices with their start and end apart: 2 -> 23, of which waited for: 1 -> 9; matrix products, arithmetic and copies ran while one was open for 26% -> 1% of each run, Pallas kernels for 0% -> 10%
where the time goes in v2:
time: 86 us; the launch traced here: 85.8 us
  starting transfers between devices  40.7 us (47%)
  waiting for transfers between devices  24.9 us (29%)
  Pallas kernels  17.8 us (21%)
  local copies, waits for them, and re-layouts  1.14 us (1%)
  other arithmetic  1 us (1%)
    all_to_all x1, starting transfers between devices, body(): mine = lax.all_to_all(spread, ('z', 'y'), 0, 0)  12 us
    all_to_all x1, waiting for transfers between devices, body(): mine = lax.all_to_all(spread, ('z', 'y'), 0, 0)  11.1 us
    ppermute x10, starting transfers between devices, swap(): return lax.ppermute(v, 'c', [(0, 1), (1, 0)])  9.57 us
    ppermute x4, starting transfers between devices, move_y(): return lax.ppermute(v, ('y', 'c'), pairs_yc(1))  7.81 us
    pallas_call x2, Pallas kernels, early(): pl.pallas_call(functools.partial(early_kernel, first), out_shape=jax.Shap...  6.39 us
    ppermute x4, starting transfers between devices, move_x(): return lax.ppermute(v, ('c', 'x'), pairs_cx(d))  5.92 us
    ppermute x3, waiting for transfers between devices, move_z(): return lax.ppermute(v, ('z', 'c'), pairs_zc(1))  5.63 us
    pallas_call x1, Pallas kernels, late(): pl.pallas_call(late_kernel, out_shape=jax.ShapeDtypeStruct((rows, width),...  5.56 us
  transfers between devices with their start and end apart: 23, of which 9 were waited for; matrix products, arithmetic and copies ran while one was open for 1% of the time, Pallas kernels for 10%

profile of v2, /device:TPU:1, one launch (start us, length us, event | category | flops | bytes accessed | tf_op | source)
XLA Modules:
  0.0 85.8 jit_solution(10100107898702822631)
XLA Ops:
  0.0 3.9 %prepare.1 = (bf16[1024,384]{1,0:T(8,128)(2,1)}, bf16[32,48,128]{2,1,0:T(8,128)(2,1)}) custom-call(s32[3,8]{1,0:T(4,128)} %bitcast.2, s32[1,3]{1,0:T(1,128)} %bitcast.3, bf16[1024,384]{1,0:T(8,128)(2,1)} %t_ref.1, bf16[384,128]{1,0:T(8,128)(2,1)} %v_ref.1), custom_call_target="tpu_custom_call" | custom-call | flops 301989888 | bytes 2162688 | tf_op jit(solution)/shard_map/prepare/pallas_call | solution.py:101
  3.9 12.0 %all-to-all-start = ((bf16[32,48,128]{2,1,0:T(8,128)(2,1)}), bf16[32,48,128]{2,1,0:T(8,128)(2,1)S(1)}, u32[]{:S(2)}, u32[]{:S(2)}) async-start(bf16[32,48,128]{2,1,0:T(8,128)(2,1)} %get-tuple-element.24), calls=%async_computation | async-start | bytes 786432 | tf_op jit(solution)/shard_map/all_to_all | solution.py:302
  15.9 1.3 %collective-permute-start.1 = (bf16[1024,384]{1,0:T(8,128)(2,1)}, bf16[1024,384]{1,0:T(8,128)(2,1)S(1)}, u32[]{:S(2)}, u32[]{:S(2)}) collective-permute-start(bf16[1024,384]{1,0:T(8,128)(2,1)} %get-tuple-element.23.t0), channel_id=1, source_target_pairs={{0,3},{1,0},{2,1},{3,2},{4,5},{5,6},{6,7},{7,4},{8,11},{9,8},{10,9... | collective-permute-start | bytes 2359304 | tf_op jit(solution)/shard_map/t_back/ppermute | solution.py:46
  17.2 1.5 %collective-permute-start = (bf16[1024,384]{1,0:T(8,128)(2,1)}, bf16[1024,384]{1,0:T(8,128)(2,1)S(1)}, u32[]{:S(2)}, u32[]{:S(2)}) collective-permute-start(bf16[1024,384]{1,0:T(8,128)(2,1)} %get-tuple-element.23.t0), channel_id=1, source_target_pairs={{0,1},{1,2},{2,3},{3,0},{4,7},{5,4},{6,5},{7,6},{8,9},{9,10},{10,1... | collective-permute-start | bytes 2359304 | tf_op jit(solution)/shard_map/t_near/ppermute | solution.py:46
  18.7 11.1 %all-to-all-done.a_ref = bf16[32,48,128]{2,1,0:T(8,128)(2,1)S(1)} async-done(((bf16[32,48,128]{2,1,0:T(8,128)(2,1)}), bf16[32,48,128]{2,1,0:T(8,128)(2,1)S(1)}, u32[]{:S(2)}, u32[]{:S(2)}) %all-to-all-start) | async-done | bytes 393248 | tf_op jit(solution)/shard_map/all_to_all | solution.py:302
  29.7 2.5 %collective-permute-start.2 = (bf16[32,48,128]{2,1,0:T(8,128)(2,1)S(1)}, bf16[32,48,128]{2,1,0:T(8,128)(2,1)S(1)}, u32[]{:S(2)}, u32[]{:S(2)}) collective-permute-start(bf16[32,48,128]{2,1,0:T(8,128)(2,1)S(1)} %all-to-all-done.a_ref), channel_id=1, source_target_pairs={{0,4},{4,0},{1,5},{5,1},{2,6},{6,2},{3,7},{7,3},{8,12},{12,8},{9,1... | collective-permute-start | bytes 1179656 | tf_op jit(solution)/shard_map/v_swap/ppermute | solution.py:51
  32.2 1.0 %select_reduce_fusion.pick_ref = s32[40]{0:T(128)S(1)} fusion(s32[64]{0:T(128)S(1)} %fusion, s32[64]{0:T(128)} %param.11, s32[40]{0:T(128)S(1)} %compare_select_fusion.2), kind=kLoop, calls=%fused_computation | loop fusion | flops 7640 | bytes 832 | tf_op jit(solution)/shard_map/reduce_sum | solution.py:147
  33.2 0.3 collective-permute-done.2.b_ref
  33.6 0.8 select_columns.1
  34.3 2.6 %collective-permute-start.6 = (bf16[16,48,128]{2,1,0:T(8,128)(2,1)S(1)}, bf16[16,48,128]{2,1,0:T(8,128)(2,1)S(1)}, u32[]{:S(2)}, u32[]{:S(2)}) collective-permute-start(bf16[16,48,128]{2,1,0:T(8,128)(2,1)S(1)} %get-tuple-element.30), channel_id=1, source_target_pairs={{0,1},{1,2},{2,3},{3,0},{4,7},{5,4},{6,5},{7,6},{8,9},{9,10},{10,1... | collective-permute-start | bytes 589832 | tf_op jit(solution)/shard_map/r_near/ppermute | solution.py:46
  36.9 0.5 collective-permute-start.3
  37.4 4.2 %collective-permute-done.6.r1_ref = bf16[16,48,128]{2,1,0:T(8,128)(2,1)S(1)} collective-permute-done((bf16[16,48,128]{2,1,0:T(8,128)(2,1)S(1)}, bf16[16,48,128]{2,1,0:T(8,128)(2,1)S(1)}, u32[]{:S(2)}, u32[]{:S(2)}) %collective-permute-start.6) | collective-permute-done | bytes 196640 | tf_op jit(solution)/shard_map/r_near/ppermute | solution.py:46
  41.6 0.2 collective-permute-start.7
  41.8 1.1 %collective-permute-done.3.r2_ref = bf16[8,48,128]{2,1,0:T(8,128)(2,1)S(1)} collective-permute-done((bf16[8,48,128]{2,1,0:T(8,128)(2,1)S(1)}, bf16[8,48,128]{2,1,0:T(8,128)(2,1)S(1)}, u32[]{:S(2)}, u32[]{:S(2)}) %collective-permute-start.3) | collective-permute-done | bytes 98336 | tf_op jit(solution)/shard_map/r_far/ppermute | solution.py:308
  42.9 1.9 %collective-permute-start.4 = (bf16[8,48,128]{2,1,0:T(8,128)(2,1)S(1)}, bf16[8,48,128]{2,1,0:T(8,128)(2,1)S(1)}, u32[]{:S(2)}, u32[]{:S(2)}) collective-permute-start(bf16[8,48,128]{2,1,0:T(8,128)(2,1)S(1)} %collective-permute-done.3.r2_ref), channel_id=1, source_target_pairs={{0,4},{4,0},{1,5},{5,1},{2,6},{6,2},{3,7},{7,3},{8,12},{12,8},{9,1... | collective-permute-start | bytes 294920 | tf_op jit(solution)/shard_map/r_far_swap/ppermute | solution.py:51
  44.8 0.9 %collective-permute-done.4.w2_ref = bf16[8,48,128]{2,1,0:T(8,128)(2,1)S(1)} collective-permute-done((bf16[8,48,128]{2,1,0:T(8,128)(2,1)S(1)}, bf16[8,48,128]{2,1,0:T(8,128)(2,1)S(1)}, u32[]{:S(2)}, u32[]{:S(2)}) %collective-permute-start.4) | collective-permute-done | bytes 98336 | tf_op jit(solution)/shard_map/r_far_swap/ppermute | solution.py:51
  45.7 0.6 collective-permute-start.5
  46.3 0.0 collective-permute-done.7.w1_ref
  46.3 0.2 pack_shard.1
  46.5 1.4 %collective-permute-start.11 = (bf16[16,2,48,128]{3,2,1,0:T(8,128)(2,1)S(1)}, bf16[16,2,48,128]{3,2,1,0:T(8,128)(2,1)S(1)}, u32[]{:S(2)}, u32[]{:S(2)}) collective-permute-start(bf16[16,2,48,128]{3,2,1,0:T(8,128)(2,1)S(1)} %get-tuple-element.33.rest_4_), channel_id=1, source_target_pairs={{0,32},{4,228},{32,64},{36,4},{64,96},{68,36},{96,128},{100,68},{1... | collective-permute-start | bytes 1179656 | tf_op jit(solution)/shard_map/p1r/ppermute | solution.py:36
  47.9 1.2 %collective-permute-start.8 = (bf16[16,2,48,128]{3,2,1,0:T(8,128)(2,1)S(1)}, bf16[16,2,48,128]{3,2,1,0:T(8,128)(2,1)S(1)}, u32[]{:S(2)}, u32[]{:S(2)}) collective-permute-start(bf16[16,2,48,128]{3,2,1,0:T(8,128)(2,1)S(1)} %get-tuple-element.32.rest_0_), channel_id=1, source_target_pairs={{0,32},{4,228},{32,64},{36,4},{64,96},{68,36},{96,128},{100,68},{1... | collective-permute-start | bytes 1179656 | tf_op jit(solution)/shard_map/p1a/ppermute | solution.py:36
  49.1 2.4 %collective-permute-start.14 = (bf16[16,2,48,128]{3,2,1,0:T(8,128)(2,1)S(1)}, bf16[16,2,48,128]{3,2,1,0:T(8,128)(2,1)S(1)}, u32[]{:S(2)}, u32[]{:S(2)}) collective-permute-start(bf16[16,2,48,128]{3,2,1,0:T(8,128)(2,1)S(1)} %get-tuple-element.32.rest_0_), channel_id=1, source_target_pairs={{0,8},{4,28},{8,16},{12,4},{16,24},{20,12},{24,0},{28,20},{1,9},{5... | collective-permute-start | bytes 1179656 | tf_op jit(solution)/shard_map/q0/ppermute | solution.py:41
  51.5 2.0 %collective-permute-done.11.rest_5_ = bf16[16,2,48,128]{3,2,1,0:T(8,128)(2,1)S(1)} collective-permute-done((bf16[16,2,48,128]{3,2,1,0:T(8,128)(2,1)S(1)}, bf16[16,2,48,128]{3,2,1,0:T(8,128)(2,1)S(1)}, u32[]{:S(2)}, u32[]{:S(2)}) %collective-permute-start.11) | collective-permute-done | bytes 393248 | tf_op jit(solution)/shard_map/p1r/ppermute | solution.py:36
  53.5 1.8 %collective-permute-start.13 = (bf16[16,2,48,128]{3,2,1,0:T(8,128)(2,1)S(1)}, bf16[16,2,48,128]{3,2,1,0:T(8,128)(2,1)S(1)}, u32[]{:S(2)}, u32[]{:S(2)}) collective-permute-start(bf16[16,2,48,128]{3,2,1,0:T(8,128)(2,1)S(1)} %collective-permute-done.11.rest_5_), channel_id=1, source_target_pairs={{0,4},{4,0},{1,5},{5,1},{2,6},{6,2},{3,7},{7,3},{8,12},{12,8},{9,1... | collective-permute-start | bytes 1179656 | tf_op jit(solution)/shard_map/p1r_swap/ppermute | solution.py:51
  55.3 2.4 %collective-permute-done.8.rest_1_ = bf16[16,2,48,128]{3,2,1,0:T(8,128)(2,1)S(1)} collective-permute-done((bf16[16,2,48,128]{3,2,1,0:T(8,128)(2,1)S(1)}, bf16[16,2,48,128]{3,2,1,0:T(8,128)(2,1)S(1)}, u32[]{:S(2)}, u32[]{:S(2)}) %collective-permute-start.8) | collective-permute-done | bytes 393248 | tf_op jit(solution)/shard_map/p1a/ppermute | solution.py:36
  57.7 2.3 %collective-permute-start.9 = (bf16[16,2,48,128]{3,2,1,0:T(8,128)(2,1)S(1)}, bf16[16,2,48,128]{3,2,1,0:T(8,128)(2,1)S(1)}, u32[]{:S(2)}, u32[]{:S(2)}) collective-permute-start(bf16[16,2,48,128]{3,2,1,0:T(8,128)(2,1)S(1)} %collective-permute-done.8.rest_1_), channel_id=1, source_target_pairs={{0,32},{4,228},{32,64},{36,4},{64,96},{68,36},{96,128},{100,68},{1... | collective-permute-start | bytes 1179656 | tf_op jit(solution)/shard_map/p2/ppermute | solution.py:36
  60.0 0.0 collective-permute-done.14.rest_3_
  60.0 0.5 collective-permute-start.15
  60.5 2.4 %collective-permute-start.12 = (bf16[16,2,48,128]{3,2,1,0:T(8,128)(2,1)S(1)}, bf16[16,2,48,128]{3,2,1,0:T(8,128)(2,1)S(1)}, u32[]{:S(2)}, u32[]{:S(2)}) collective-permute-start(bf16[16,2,48,128]{3,2,1,0:T(8,128)(2,1)S(1)} %collective-permute-done.11.rest_5_), channel_id=1, source_target_pairs={{0,8},{4,28},{8,16},{12,4},{16,24},{20,12},{24,0},{28,20},{1,9},{5... | collective-permute-start | bytes 1179656 | tf_op jit(solution)/shard_map/q1r/ppermute | solution.py:41
  62.9 0.0 collective-permute-done.13.rest_2_
  62.9 0.6 collective-permute-start.10
  63.5 1.2 %collective-permute-done.9.rest_0_ = bf16[16,2,48,128]{3,2,1,0:T(8,128)(2,1)S(1)} collective-permute-done((bf16[16,2,48,128]{3,2,1,0:T(8,128)(2,1)S(1)}, bf16[16,2,48,128]{3,2,1,0:T(8,128)(2,1)S(1)}, u32[]{:S(2)}, u32[]{:S(2)}) %collective-permute-start.9) | collective-permute-done | bytes 393248 | tf_op jit(solution)/shard_map/p2/ppermute | solution.py:36
  64.7 2.4 %collective-permute-start.17 = (bf16[16,2,48,128]{3,2,1,0:T(8,128)(2,1)S(1)}, bf16[16,2,48,128]{3,2,1,0:T(8,128)(2,1)S(1)}, u32[]{:S(2)}, u32[]{:S(2)}) collective-permute-start(bf16[16,2,48,128]{3,2,1,0:T(8,128)(2,1)S(1)} %collective-permute-done.9.rest_0_), channel_id=1, source_target_pairs={{0,8},{4,28},{8,16},{12,4},{16,24},{20,12},{24,0},{28,20},{1,9},{5... | collective-permute-start | bytes 1179656 | tf_op jit(solution)/shard_map/q2/ppermute | solution.py:41
  67.1 1.1 %copy-done.1 = bf16[1024,384]{1,0:T(8,128)(2,1)S(1)} copy-done((bf16[1024,384]{1,0:T(8,128)(2,1)S(1)}, bf16[1024,384]{1,0:T(8,128)(2,1)}, u32[]{:S(2)}) %copy-start.1) | copy-done | bytes 786456
  68.2 1.1 %arrange_t.1 = (bf16[1024,768]{1,0:T(8,128)(2,1)S(1)}, bf16[1024,768]{1,0:T(8,128)(2,1)S(1)}) custom-call(bf16[1024,384]{1,0:T(8,128)(2,1)S(1)} %copy-done.1, bf16[1024,384]{1,0:T(8,128)(2,1)S(1)} %collective-permute-done.t1, bf16[1024,384]{1,0:T(8,128)(2,1)S(1)} %collective-permute-done.1.t2, bf16[1024,384]{1,0:T(8,128)(2,1)S(1)} %collective-permute-done.5.t3), custom_call_target="tpu_custom_call" | custom-call | bytes 6291456 | tf_op jit(solution)/shard_map/arrange_t/pallas_call | solution.py:200
  69.3 0.0 collective-permute-done.15.rest_6_
  69.4 3.2 %ladder_early.2.acc0 = f32[1024,1024]{1,0:T(8,128)S(1)} custom-call(s32[8,16]{1,0:T(8,128)S(1)} %copy-done.2, bf16[1024,768]{1,0:T(8,128)(2,1)S(1)} %get-tuple-element.34.t_ref, bf16[1024,2048]{1,0:T(8,128)(2,1)S(1)} %copy-done, bf16[16,2,48,128]{3,2,1,0:T(8,128)(2,1)S(1)} %get-tuple-element.32.rest_0_, ...), custom_call_target="tpu_custom_call" | custom-call | flops 1610612736 | bytes 9437184 | tf_op jit(solution)/shard_map/ladder_early/pallas_call | solution.py:240
  72.6 0.0 collective-permute-done.12.rest_5_
  72.6 2.0 %collective-permute-start.19 = (bf16[16,2,48,128]{3,2,1,0:T(8,128)(2,1)S(1)}, bf16[16,2,48,128]{3,2,1,0:T(8,128)(2,1)S(1)}, u32[]{:S(2)}, u32[]{:S(2)}) collective-permute-start(bf16[16,2,48,128]{3,2,1,0:T(8,128)(2,1)S(1)} %collective-permute-done.9.rest_0_), channel_id=1, source_target_pairs={{0,4},{4,0},{1,5},{5,1},{2,6},{6,2},{3,7},{7,3},{8,12},{12,8},{9,1... | collective-permute-start | bytes 1179656 | tf_op jit(solution)/shard_map/p2_swap/ppermute | solution.py:51
  74.6 0.1 collective-permute-start.20
  74.7 0.4 collective-permute-start.18
  75.1 3.2 %ladder_early.3.acc1 = f32[1024,1024]{1,0:T(8,128)S(1)} custom-call(s32[8,16]{1,0:T(8,128)S(1)} %copy-done.2, bf16[1024,768]{1,0:T(8,128)(2,1)S(1)} %get-tuple-element.34.t_ref, bf16[1024,2048]{1,0:T(8,128)(2,1)S(1)} %copy-done, bf16[16,2,48,128]{3,2,1,0:T(8,128)(2,1)S(1)} %get-tuple-element.32.rest_0_, ...), custom_call_target="tpu_custom_call" | custom-call | flops 1610612736 | bytes 9437184 | tf_op jit(solution)/shard_map/ladder_early/pallas_call | solution.py:240
  78.3 0.0 collective-permute-done.17.rest_3_
  78.3 0.2 collective-permute-start.21
  78.5 0.0 collective-permute-done.19.rest_4_
  78.5 0.0 collective-permute-done.20.rest_6_
  78.5 1.6 %collective-permute-done.21.rest_7_ = bf16[16,2,48,128]{3,2,1,0:T(8,128)(2,1)S(1)} collective-permute-done((bf16[16,2,48,128]{3,2,1,0:T(8,128)(2,1)S(1)}, bf16[16,2,48,128]{3,2,1,0:T(8,128)(2,1)S(1)}, u32[]{:S(2)}, u32[]{:S(2)}) %collective-permute-start.21) | collective-permute-done | bytes 393248 | tf_op jit(solution)/shard_map/q2_swap/ppermute | solution.py:51
  80.1 5.6 %ladder_late.1 = bf16[1024,2048]{1,0:T(8,128)(2,1)} custom-call(s32[8,16]{1,0:T(8,128)S(1)} %copy-done.2, bf16[1024,768]{1,0:T(8,128)(2,1)S(1)} %get-tuple-element.28.t_ref, f32[1024,1024]{1,0:T(8,128)S(1)} %ladder_early.2.acc0, f32[1024,1024]{1,0:T(8,128)S(1)} %ladder_early.3.acc1, bf16[16,2,48,128]{3,2,1,0:T(8,128)(2,1)S(1)} %collective-permute-done.9.rest_0_, ...), custom_call_target="tpu_custom_call" | custom-call | flops 3221225472 | bytes 17301504 | tf_op jit(solution)/shard_map/ladder_late/pallas_call | solution.py:284
  (14 shorter events, 0.0 us)
Async XLA Ops:
  0.0 69.3 %copy-start.2 = (s32[8,16]{1,0:T(8,128)S(1)}, s32[8,16]{1,0:T(8,128)}, u32[]{:S(2)}) copy-start(s32[8,16]{1,0:T(8,128)} %mask_ref.5) | copy-start | bytes 1540
  3.9 25.8 %all-to-all-start = ((bf16[32,48,128]{2,1,0:T(8,128)(2,1)}), bf16[32,48,128]{2,1,0:T(8,128)(2,1)S(1)}, u32[]{:S(2)}, u32[]{:S(2)}) async-start(bf16[32,48,128]{2,1,0:T(8,128)(2,1)} %get-tuple-element.24), calls=%async_computation | async-start | bytes 786432 | tf_op jit(solution)/shard_map/all_to_all | solution.py:302
  15.9 28.9 %collective-permute-start.1 = (bf16[1024,384]{1,0:T(8,128)(2,1)}, bf16[1024,384]{1,0:T(8,128)(2,1)S(1)}, u32[]{:S(2)}, u32[]{:S(2)}) collective-permute-start(bf16[1024,384]{1,0:T(8,128)(2,1)} %get-tuple-element.23.t0), channel_id=1, source_target_pairs={{0,3},{1,0},{2,1},{3,2},{4,5},{5,6},{6,7},{7,4},{8,11},{9,8},{10,9... | collective-permute-start | bytes 2359304 | tf_op jit(solution)/shard_map/t_back/ppermute | solution.py:46
  17.2 27.6 %collective-permute-start = (bf16[1024,384]{1,0:T(8,128)(2,1)}, bf16[1024,384]{1,0:T(8,128)(2,1)S(1)}, u32[]{:S(2)}, u32[]{:S(2)}) collective-permute-start(bf16[1024,384]{1,0:T(8,128)(2,1)} %get-tuple-element.23.t0), channel_id=1, source_target_pairs={{0,1},{1,2},{2,3},{3,0},{4,7},{5,4},{6,5},{7,6},{8,9},{9,10},{10,1... | collective-permute-start | bytes 2359304 | tf_op jit(solution)/shard_map/t_near/ppermute | solution.py:46
  29.7 3.8 %collective-permute-start.2 = (bf16[32,48,128]{2,1,0:T(8,128)(2,1)S(1)}, bf16[32,48,128]{2,1,0:T(8,128)(2,1)S(1)}, u32[]{:S(2)}, u32[]{:S(2)}) collective-permute-start(bf16[32,48,128]{2,1,0:T(8,128)(2,1)S(1)} %all-to-all-done.a_ref), channel_id=1, source_target_pairs={{0,4},{4,0},{1,5},{5,1},{2,6},{6,2},{3,7},{7,3},{8,12},{12,8},{9,1... | collective-permute-start | bytes 1179656 | tf_op jit(solution)/shard_map/v_swap/ppermute | solution.py:51
  32.2 37.1 %copy-start = (bf16[1024,2048]{1,0:T(8,128)(2,1)S(1)}, bf16[1024,2048]{1,0:T(8,128)(2,1)}, u32[]{:S(2)}) copy-start(bf16[1024,2048]{1,0:T(8,128)(2,1)} %r_ref.3) | copy-start | bytes 12582916
  34.3 7.3 %collective-permute-start.6 = (bf16[16,48,128]{2,1,0:T(8,128)(2,1)S(1)}, bf16[16,48,128]{2,1,0:T(8,128)(2,1)S(1)}, u32[]{:S(2)}, u32[]{:S(2)}) collective-permute-start(bf16[16,48,128]{2,1,0:T(8,128)(2,1)S(1)} %get-tuple-element.30), channel_id=1, source_target_pairs={{0,1},{1,2},{2,3},{3,0},{4,7},{5,4},{6,5},{7,6},{8,9},{9,10},{10,1... | collective-permute-start | bytes 589832 | tf_op jit(solution)/shard_map/r_near/ppermute | solution.py:46
  36.9 6.0 %collective-permute-start.3 = (bf16[8,48,128]{2,1,0:T(8,128)(2,1)S(1)}, bf16[8,48,128]{2,1,0:T(8,128)(2,1)S(1)}, u32[]{:S(2)}, u32[]{:S(2)}) collective-permute-start(bf16[8,48,128]{2,1,0:T(8,128)(2,1)S(1)} %get-tuple-element.25), channel_id=1, source_target_pairs={{0,2},{1,3},{2,0},{3,1},{4,6},{5,7},{6,4},{7,5},{8,10},{9,11},{10,... | collective-permute-start | bytes 294920 | tf_op jit(solution)/shard_map/r_far/ppermute | solution.py:308
  41.6 4.7 %collective-permute-start.7 = (bf16[16,48,128]{2,1,0:T(8,128)(2,1)S(1)}, bf16[16,48,128]{2,1,0:T(8,128)(2,1)S(1)}, u32[]{:S(2)}, u32[]{:S(2)}) collective-permute-start(bf16[16,48,128]{2,1,0:T(8,128)(2,1)S(1)} %collective-permute-done.6.r1_ref), channel_id=1, source_target_pairs={{0,4},{4,0},{1,5},{5,1},{2,6},{6,2},{3,7},{7,3},{8,12},{12,8},{9,1... | collective-permute-start | bytes 589832 | tf_op jit(solution)/shard_map/r_near_swap/ppermute | solution.py:51
  42.9 2.8 %collective-permute-start.4 = (bf16[8,48,128]{2,1,0:T(8,128)(2,1)S(1)}, bf16[8,48,128]{2,1,0:T(8,128)(2,1)S(1)}, u32[]{:S(2)}, u32[]{:S(2)}) collective-permute-start(bf16[8,48,128]{2,1,0:T(8,128)(2,1)S(1)} %collective-permute-done.3.r2_ref), channel_id=1, source_target_pairs={{0,4},{4,0},{1,5},{5,1},{2,6},{6,2},{3,7},{7,3},{8,12},{12,8},{9,1... | collective-permute-start | bytes 294920 | tf_op jit(solution)/shard_map/r_far_swap/ppermute | solution.py:51
  45.7 14.8 %collective-permute-start.5 = (bf16[1024,384]{1,0:T(8,128)(2,1)S(1)}, bf16[1024,384]{1,0:T(8,128)(2,1)S(1)}, u32[]{:S(2)}, u32[]{:S(2)}) collective-permute-start(bf16[1024,384]{1,0:T(8,128)(2,1)S(1)} %collective-permute-done.t1), channel_id=1, source_target_pairs={{0,1},{1,2},{2,3},{3,0},{4,7},{5,4},{6,5},{7,6},{8,9},{9,10},{10,1... | collective-permute-start | bytes 2359304 | tf_op jit(solution)/shard_map/t_far/ppermute | solution.py:46
  46.5 7.0 %collective-permute-start.11 = (bf16[16,2,48,128]{3,2,1,0:T(8,128)(2,1)S(1)}, bf16[16,2,48,128]{3,2,1,0:T(8,128)(2,1)S(1)}, u32[]{:S(2)}, u32[]{:S(2)}) collective-permute-start(bf16[16,2,48,128]{3,2,1,0:T(8,128)(2,1)S(1)} %get-tuple-element.33.rest_4_), channel_id=1, source_target_pairs={{0,32},{4,228},{32,64},{36,4},{64,96},{68,36},{96,128},{100,68},{1... | collective-permute-start | bytes 1179656 | tf_op jit(solution)/shard_map/p1r/ppermute | solution.py:36
  47.9 9.8 %collective-permute-start.8 = (bf16[16,2,48,128]{3,2,1,0:T(8,128)(2,1)S(1)}, bf16[16,2,48,128]{3,2,1,0:T(8,128)(2,1)S(1)}, u32[]{:S(2)}, u32[]{:S(2)}) collective-permute-start(bf16[16,2,48,128]{3,2,1,0:T(8,128)(2,1)S(1)} %get-tuple-element.32.rest_0_), channel_id=1, source_target_pairs={{0,32},{4,228},{32,64},{36,4},{64,96},{68,36},{96,128},{100,68},{1... | collective-permute-start | bytes 1179656 | tf_op jit(solution)/shard_map/p1a/ppermute | solution.py:36
  49.1 10.9 %collective-permute-start.14 = (bf16[16,2,48,128]{3,2,1,0:T(8,128)(2,1)S(1)}, bf16[16,2,48,128]{3,2,1,0:T(8,128)(2,1)S(1)}, u32[]{:S(2)}, u32[]{:S(2)}) collective-permute-start(bf16[16,2,48,128]{3,2,1,0:T(8,128)(2,1)S(1)} %get-tuple-element.32.rest_0_), channel_id=1, source_target_pairs={{0,8},{4,28},{8,16},{12,4},{16,24},{20,12},{24,0},{28,20},{1,9},{5... | collective-permute-start | bytes 1179656 | tf_op jit(solution)/shard_map/q0/ppermute | solution.py:41
  53.5 9.4 %collective-permute-start.13 = (bf16[16,2,48,128]{3,2,1,0:T(8,128)(2,1)S(1)}, bf16[16,2,48,128]{3,2,1,0:T(8,128)(2,1)S(1)}, u32[]{:S(2)}, u32[]{:S(2)}) collective-permute-start(bf16[16,2,48,128]{3,2,1,0:T(8,128)(2,1)S(1)} %collective-permute-done.11.rest_5_), channel_id=1, source_target_pairs={{0,4},{4,0},{1,5},{5,1},{2,6},{6,2},{3,7},{7,3},{8,12},{12,8},{9,1... | collective-permute-start | bytes 1179656 | tf_op jit(solution)/shard_map/p1r_swap/ppermute | solution.py:51
  57.7 7.0 %collective-permute-start.9 = (bf16[16,2,48,128]{3,2,1,0:T(8,128)(2,1)S(1)}, bf16[16,2,48,128]{3,2,1,0:T(8,128)(2,1)S(1)}, u32[]{:S(2)}, u32[]{:S(2)}) collective-permute-start(bf16[16,2,48,128]{3,2,1,0:T(8,128)(2,1)S(1)} %collective-permute-done.8.rest_1_), channel_id=1, source_target_pairs={{0,32},{4,228},{32,64},{36,4},{64,96},{68,36},{96,128},{100,68},{1... | collective-permute-start | bytes 1179656 | tf_op jit(solution)/shard_map/p2/ppermute | solution.py:36
  60.0 9.4 %collective-permute-start.16 = (bf16[16,2,48,128]{3,2,1,0:T(8,128)(2,1)S(1)}, bf16[16,2,48,128]{3,2,1,0:T(8,128)(2,1)S(1)}, u32[]{:S(2)}, u32[]{:S(2)}) collective-permute-start(bf16[16,2,48,128]{3,2,1,0:T(8,128)(2,1)S(1)} %collective-permute-done.14.rest_3_), channel_id=1, source_target_pairs={{0,4},{4,0},{1,5},{5,1},{2,6},{6,2},{3,7},{7,3},{8,12},{12,8},{9,1... | collective-permute-start | bytes 1179656 | tf_op jit(solution)/shard_map/q0_swap/ppermute | solution.py:51
  60.0 9.4 %collective-permute-start.15 = (bf16[16,2,48,128]{3,2,1,0:T(8,128)(2,1)S(1)}, bf16[16,2,48,128]{3,2,1,0:T(8,128)(2,1)S(1)}, u32[]{:S(2)}, u32[]{:S(2)}) collective-permute-start(bf16[16,2,48,128]{3,2,1,0:T(8,128)(2,1)S(1)} %collective-permute-done.8.rest_1_), channel_id=1, source_target_pairs={{0,4},{4,0},{1,5},{5,1},{2,6},{6,2},{3,7},{7,3},{8,12},{12,8},{9,1... | collective-permute-start | bytes 1179656 | tf_op jit(solution)/shard_map/p1a_swap/ppermute | solution.py:51
  60.5 12.1 %collective-permute-start.12 = (bf16[16,2,48,128]{3,2,1,0:T(8,128)(2,1)S(1)}, bf16[16,2,48,128]{3,2,1,0:T(8,128)(2,1)S(1)}, u32[]{:S(2)}, u32[]{:S(2)}) collective-permute-start(bf16[16,2,48,128]{3,2,1,0:T(8,128)(2,1)S(1)} %collective-permute-done.11.rest_5_), channel_id=1, source_target_pairs={{0,8},{4,28},{8,16},{12,4},{16,24},{20,12},{24,0},{28,20},{1,9},{5... | collective-permute-start | bytes 1179656 | tf_op jit(solution)/shard_map/q1r/ppermute | solution.py:41
  62.9 9.7 %collective-permute-start.10 = (bf16[16,2,48,128]{3,2,1,0:T(8,128)(2,1)S(1)}, bf16[16,2,48,128]{3,2,1,0:T(8,128)(2,1)S(1)}, u32[]{:S(2)}, u32[]{:S(2)}) collective-permute-start(bf16[16,2,48,128]{3,2,1,0:T(8,128)(2,1)S(1)} %collective-permute-done.8.rest_1_), channel_id=1, source_target_pairs={{0,8},{4,28},{8,16},{12,4},{16,24},{20,12},{24,0},{28,20},{1,9},{5... | collective-permute-start | bytes 1179656 | tf_op jit(solution)/shard_map/q1a/ppermute | solution.py:41
  64.7 13.6 %collective-permute-start.17 = (bf16[16,2,48,128]{3,2,1,0:T(8,128)(2,1)S(1)}, bf16[16,2,48,128]{3,2,1,0:T(8,128)(2,1)S(1)}, u32[]{:S(2)}, u32[]{:S(2)}) collective-permute-start(bf16[16,2,48,128]{3,2,1,0:T(8,128)(2,1)S(1)} %collective-permute-done.9.rest_0_), channel_id=1, source_target_pairs={{0,8},{4,28},{8,16},{12,4},{16,24},{20,12},{24,0},{28,20},{1,9},{5... | collective-permute-start | bytes 1179656 | tf_op jit(solution)/shard_map/q2/ppermute | solution.py:41
  67.1 1.1 %copy-start.1 = (bf16[1024,384]{1,0:T(8,128)(2,1)S(1)}, bf16[1024,384]{1,0:T(8,128)(2,1)}, u32[]{:S(2)}) copy-start(bf16[1024,384]{1,0:T(8,128)(2,1)} %get-tuple-element.23.t0) | copy-start | bytes 2359300
  72.6 5.9 %collective-permute-start.19 = (bf16[16,2,48,128]{3,2,1,0:T(8,128)(2,1)S(1)}, bf16[16,2,48,128]{3,2,1,0:T(8,128)(2,1)S(1)}, u32[]{:S(2)}, u32[]{:S(2)}) collective-permute-start(bf16[16,2,48,128]{3,2,1,0:T(8,128)(2,1)S(1)} %collective-permute-done.9.rest_0_), channel_id=1, source_target_pairs={{0,4},{4,0},{1,5},{5,1},{2,6},{6,2},{3,7},{7,3},{8,12},{12,8},{9,1... | collective-permute-start | bytes 1179656 | tf_op jit(solution)/shard_map/p2_swap/ppermute | solution.py:51
  74.6 3.9 %collective-permute-start.20 = (bf16[16,2,48,128]{3,2,1,0:T(8,128)(2,1)S(1)}, bf16[16,2,48,128]{3,2,1,0:T(8,128)(2,1)S(1)}, u32[]{:S(2)}, u32[]{:S(2)}) collective-permute-start(bf16[16,2,48,128]{3,2,1,0:T(8,128)(2,1)S(1)} %collective-permute-done.10.rest_1_), channel_id=1, source_target_pairs={{0,4},{4,0},{1,5},{5,1},{2,6},{6,2},{3,7},{7,3},{8,12},{12,8},{9,1... | collective-permute-start | bytes 1179656 | tf_op jit(solution)/shard_map/q1a_swap/ppermute | solution.py:51
  74.7 3.8 %collective-permute-start.18 = (bf16[16,2,48,128]{3,2,1,0:T(8,128)(2,1)S(1)}, bf16[16,2,48,128]{3,2,1,0:T(8,128)(2,1)S(1)}, u32[]{:S(2)}, u32[]{:S(2)}) collective-permute-start(bf16[16,2,48,128]{3,2,1,0:T(8,128)(2,1)S(1)} %collective-permute-done.12.rest_5_), channel_id=1, source_target_pairs={{0,4},{4,0},{1,5},{5,1},{2,6},{6,2},{3,7},{7,3},{8,12},{12,8},{9,1... | collective-permute-start | bytes 1179656 | tf_op jit(solution)/shard_map/q1r_swap/ppermute | solution.py:51
  78.3 1.8 %collective-permute-start.21 = (bf16[16,2,48,128]{3,2,1,0:T(8,128)(2,1)S(1)}, bf16[16,2,48,128]{3,2,1,0:T(8,128)(2,1)S(1)}, u32[]{:S(2)}, u32[]{:S(2)}) collective-permute-start(bf16[16,2,48,128]{3,2,1,0:T(8,128)(2,1)S(1)} %collective-permute-done.17.rest_3_), channel_id=1, source_target_pairs={{0,4},{4,0},{1,5},{5,1},{2,6},{6,2},{3,7},{7,3},{8,12},{12,8},{9,1... | collective-permute-start | bytes 1179656 | tf_op jit(solution)/shard_map/q2_swap/ppermute | solution.py:51

commit v3 on v2

--- a/solution.py
+++ b/solution.py
@@ -306,18 +306,20 @@
     r1 = move_x("r_near", near)
     with jax.named_scope("r_far"):
         r2 = lax.ppermute(opposite, "x", [(i, (i + 2) % NX) for i in range(NX)])
+    t1, t2, r1 = hold((t1, t2, r1))
+    t3 = move_x("t_far", t1)
     w1, w2 = swap("r_near_swap", r1), swap("r_far_swap", r2)
-    t1, t2, w2 = hold((t1, t2, w2))
     ahead, rest = pack(own, r1, w1, r2, w2)
-    t3 = move_x("t_far", t1)
 
     p1a = move_z("p1a", ahead)
     p1r = move_z("p1r", rest)
     q0 = move_y("q0", ahead)
-    p2, q1a, q1r = move_z("p2", p1a), move_y("q1a", p1a), move_y("q1r", p1r)
+    p2, q1a, q1r = move_z("p2", p1a), move_z("q1a", q0), move_y("q1r", p1r)
     q2 = move_y("q2", p2)
     t_early, t_late = arrange((t0, t1, t2, t3))
-    blocks = (ahead, p1a, swap("p1r_swap", p1r), q0, rest, p1r, swap("p1a_swap", p1a), swap("q0_swap", q0))
+    p1a_swap, near_r, t_early = hold((swap("p1a_swap", p1a), p1r, t_early))
+    p1r_swap = swap("p1r_swap", near_r)
+    blocks = (ahead, p1a, p1r_swap, q0, rest, p1r, p1a_swap, swap("q0_swap", q0))
     acc0 = early(0, r_mask, t_early, r_old, blocks)
     p2, q1a, q1r, acc0 = hold((p2, q1a, q1r, acc0))
     acc1 = early(HALF, r_mask, t_early, r_old, blocks)

time: 86 us -> 82.8 us (0.963)
  starting transfers between devices: 40.7 us -> 38.4 us
  waiting for transfers between devices: 24.9 us -> 23.9 us
    ppermute x4 -> x3, starting transfers between devices: 7.81 us -> 4.4 us  [move_y(): return lax.ppermute(v, ('y', 'c'), pairs_yc(1))]
    ppermute x10, starting transfers between devices: 9.57 us -> 12.2 us  [swap(): return lax.ppermute(v, 'c', [(0, 1), (1, 0)])]
    ppermute x3 -> x4, waiting for transfers between devices: 5.63 us -> 3.87 us  [move_z(): return lax.ppermute(v, ('z', 'c'), pairs_zc(1))]
    ppermute x3 -> x4, starting transfers between devices: 4.82 us -> 3.44 us  [move_z(): return lax.ppermute(v, ('z', 'c'), pairs_zc(1))]
  transfers between devices with their start and end apart: 23 -> 23, of which waited for: 9 -> 12; matrix products, arithmetic and copies ran while one was open for 1% -> 1% of each run, Pallas kernels for 10% -> 10%
where the time goes in v3:
time: 82.8 us; the launch traced here: 82.6 us
  starting transfers between devices  38.4 us (46%)
  waiting for transfers between devices  23.9 us (29%)
  Pallas kernels  17.8 us (21%)
  local copies, waits for them, and re-layouts  1.14 us (1%)
  other arithmetic  1 us (1%)
    ppermute x10, starting transfers between devices, swap(): return lax.ppermute(v, 'c', [(0, 1), (1, 0)])  12.2 us
    all_to_all x1, starting transfers between devices, body(): mine = lax.all_to_all(spread, ('z', 'y'), 0, 0)  12 us
    all_to_all x1, waiting for transfers between devices, body(): mine = lax.all_to_all(spread, ('z', 'y'), 0, 0)  11.1 us
    pallas_call x2, Pallas kernels, early(): pl.pallas_call(functools.partial(early_kernel, first), out_shape=jax.Shap...  6.39 us
    ppermute x4, starting transfers between devices, move_x(): return lax.ppermute(v, ('c', 'x'), pairs_cx(d))  5.8 us
    pallas_call x1, Pallas kernels, late(): pl.pallas_call(late_kernel, out_shape=jax.ShapeDtypeStruct((rows, width),...  5.56 us
    ppermute x3, starting transfers between devices, move_y(): return lax.ppermute(v, ('y', 'c'), pairs_yc(1))  4.4 us
    ppermute x4, waiting for transfers between devices, move_x(): return lax.ppermute(v, ('c', 'x'), pairs_cx(d))  4.21 us
  transfers between devices with their start and end apart: 23, of which 12 were waited for; matrix products, arithmetic and copies ran while one was open for 1% of the time, Pallas kernels for 10%

profile of v3, /device:TPU:1, one launch (start us, length us, event | category | flops | bytes accessed | tf_op | source)
XLA Modules:
  0.0 82.6 jit_solution(622248678751563522)
XLA Ops:
  0.0 3.9 %prepare.1 = (bf16[1024,384]{1,0:T(8,128)(2,1)}, bf16[32,48,128]{2,1,0:T(8,128)(2,1)}) custom-call(s32[3,8]{1,0:T(4,128)} %bitcast.2, s32[1,3]{1,0:T(1,128)} %bitcast.3, bf16[1024,384]{1,0:T(8,128)(2,1)} %t_ref.1, bf16[384,128]{1,0:T(8,128)(2,1)} %v_ref.1), custom_call_target="tpu_custom_call" | custom-call | flops 301989888 | bytes 2162688 | tf_op jit(solution)/shard_map/prepare/pallas_call | solution.py:101
  3.9 12.0 %all-to-all-start = ((bf16[32,48,128]{2,1,0:T(8,128)(2,1)}), bf16[32,48,128]{2,1,0:T(8,128)(2,1)S(1)}, u32[]{:S(2)}, u32[]{:S(2)}) async-start(bf16[32,48,128]{2,1,0:T(8,128)(2,1)} %get-tuple-element.27), calls=%async_computation | async-start | bytes 786432 | tf_op jit(solution)/shard_map/all_to_all | solution.py:302
  15.9 1.3 %collective-permute-start.1 = (bf16[1024,384]{1,0:T(8,128)(2,1)}, bf16[1024,384]{1,0:T(8,128)(2,1)S(1)}, u32[]{:S(2)}, u32[]{:S(2)}) collective-permute-start(bf16[1024,384]{1,0:T(8,128)(2,1)} %get-tuple-element.26.t0), channel_id=1, source_target_pairs={{0,3},{1,0},{2,1},{3,2},{4,5},{5,6},{6,7},{7,4},{8,11},{9,8},{10,9... | collective-permute-start | bytes 2359304 | tf_op jit(solution)/shard_map/t_back/ppermute | solution.py:46
  17.2 1.5 %collective-permute-start = (bf16[1024,384]{1,0:T(8,128)(2,1)}, bf16[1024,384]{1,0:T(8,128)(2,1)S(1)}, u32[]{:S(2)}, u32[]{:S(2)}) collective-permute-start(bf16[1024,384]{1,0:T(8,128)(2,1)} %get-tuple-element.26.t0), channel_id=1, source_target_pairs={{0,1},{1,2},{2,3},{3,0},{4,7},{5,4},{6,5},{7,6},{8,9},{9,10},{10,1... | collective-permute-start | bytes 2359304 | tf_op jit(solution)/shard_map/t_near/ppermute | solution.py:46
  18.7 11.1 %all-to-all-done.a_ref = bf16[32,48,128]{2,1,0:T(8,128)(2,1)S(1)} async-done(((bf16[32,48,128]{2,1,0:T(8,128)(2,1)}), bf16[32,48,128]{2,1,0:T(8,128)(2,1)S(1)}, u32[]{:S(2)}, u32[]{:S(2)}) %all-to-all-start) | async-done | bytes 393248 | tf_op jit(solution)/shard_map/all_to_all | solution.py:302
  29.7 2.5 %collective-permute-start.2 = (bf16[32,48,128]{2,1,0:T(8,128)(2,1)S(1)}, bf16[32,48,128]{2,1,0:T(8,128)(2,1)S(1)}, u32[]{:S(2)}, u32[]{:S(2)}) collective-permute-start(bf16[32,48,128]{2,1,0:T(8,128)(2,1)S(1)} %all-to-all-done.a_ref), channel_id=1, source_target_pairs={{0,4},{4,0},{1,5},{5,1},{2,6},{6,2},{3,7},{7,3},{8,12},{12,8},{9,1... | collective-permute-start | bytes 1179656 | tf_op jit(solution)/shard_map/v_swap/ppermute | solution.py:51
  32.2 1.0 %select_reduce_fusion.pick_ref = s32[40]{0:T(128)S(1)} fusion(s32[64]{0:T(128)S(1)} %fusion, s32[64]{0:T(128)} %param.11, s32[40]{0:T(128)S(1)} %compare_select_fusion.2), kind=kLoop, calls=%fused_computation | loop fusion | flops 7640 | bytes 832 | tf_op jit(solution)/shard_map/reduce_sum | solution.py:147
  33.2 0.3 collective-permute-done.2.b_ref
  33.6 0.8 select_columns.1
  34.3 2.6 %collective-permute-start.3 = (bf16[16,48,128]{2,1,0:T(8,128)(2,1)S(1)}, bf16[16,48,128]{2,1,0:T(8,128)(2,1)S(1)}, u32[]{:S(2)}, u32[]{:S(2)}) collective-permute-start(bf16[16,48,128]{2,1,0:T(8,128)(2,1)S(1)} %get-tuple-element.28), channel_id=1, source_target_pairs={{0,1},{1,2},{2,3},{3,0},{4,7},{5,4},{6,5},{7,6},{8,9},{9,10},{10,1... | collective-permute-start | bytes 589832 | tf_op jit(solution)/shard_map/r_near/ppermute | solution.py:46
  36.9 0.5 collective-permute-start.6
  37.4 0.0 collective-permute-done.1.t2
  37.4 0.0 collective-permute-done.t1
  37.4 4.2 %collective-permute-done.3.r1_ref = bf16[16,48,128]{2,1,0:T(8,128)(2,1)S(1)} collective-permute-done((bf16[16,48,128]{2,1,0:T(8,128)(2,1)S(1)}, bf16[16,48,128]{2,1,0:T(8,128)(2,1)S(1)}, u32[]{:S(2)}, u32[]{:S(2)}) %collective-permute-start.3) | collective-permute-done | bytes 196640 | tf_op jit(solution)/shard_map/r_near/ppermute | solution.py:46
  41.6 0.2 collective-permute-start.5
  41.8 1.1 %collective-permute-done.6.r2_ref = bf16[8,48,128]{2,1,0:T(8,128)(2,1)S(1)} collective-permute-done((bf16[8,48,128]{2,1,0:T(8,128)(2,1)S(1)}, bf16[8,48,128]{2,1,0:T(8,128)(2,1)S(1)}, u32[]{:S(2)}, u32[]{:S(2)}) %collective-permute-start.6) | collective-permute-done | bytes 98336 | tf_op jit(solution)/shard_map/r_far/ppermute | solution.py:308
  42.9 1.9 %collective-permute-start.7 = (bf16[8,48,128]{2,1,0:T(8,128)(2,1)S(1)}, bf16[8,48,128]{2,1,0:T(8,128)(2,1)S(1)}, u32[]{:S(2)}, u32[]{:S(2)}) collective-permute-start(bf16[8,48,128]{2,1,0:T(8,128)(2,1)S(1)} %collective-permute-done.6.r2_ref), channel_id=1, source_target_pairs={{0,4},{4,0},{1,5},{5,1},{2,6},{6,2},{3,7},{7,3},{8,12},{12,8},{9,1... | collective-permute-start | bytes 294920 | tf_op jit(solution)/shard_map/r_far_swap/ppermute | solution.py:51
  44.8 0.5 collective-permute-start.4
  45.3 0.5 collective-permute-done.7.w2_ref
  45.7 0.2 pack_shard.1
  45.9 1.0 %collective-permute-start.8 = (bf16[16,2,48,128]{3,2,1,0:T(8,128)(2,1)S(1)}, bf16[16,2,48,128]{3,2,1,0:T(8,128)(2,1)S(1)}, u32[]{:S(2)}, u32[]{:S(2)}) collective-permute-start(bf16[16,2,48,128]{3,2,1,0:T(8,128)(2,1)S(1)} %get-tuple-element.35.rest_0_), channel_id=1, source_target_pairs={{0,32},{4,228},{32,64},{36,4},{64,96},{68,36},{96,128},{100,68},{1... | collective-permute-start | bytes 1179656 | tf_op jit(solution)/shard_map/p1a/ppermute | solution.py:36
  46.8 2.4 %collective-permute-start.10 = (bf16[16,2,48,128]{3,2,1,0:T(8,128)(2,1)S(1)}, bf16[16,2,48,128]{3,2,1,0:T(8,128)(2,1)S(1)}, u32[]{:S(2)}, u32[]{:S(2)}) collective-permute-start(bf16[16,2,48,128]{3,2,1,0:T(8,128)(2,1)S(1)} %get-tuple-element.35.rest_0_), channel_id=1, source_target_pairs={{0,8},{4,28},{8,16},{12,4},{16,24},{20,12},{24,0},{28,20},{1,9},{5... | collective-permute-start | bytes 1179656 | tf_op jit(solution)/shard_map/q0/ppermute | solution.py:41
  49.3 1.2 %collective-permute-start.12 = (bf16[16,2,48,128]{3,2,1,0:T(8,128)(2,1)S(1)}, bf16[16,2,48,128]{3,2,1,0:T(8,128)(2,1)S(1)}, u32[]{:S(2)}, u32[]{:S(2)}) collective-permute-start(bf16[16,2,48,128]{3,2,1,0:T(8,128)(2,1)S(1)} %get-tuple-element.36.rest_4_), channel_id=1, source_target_pairs={{0,32},{4,228},{32,64},{36,4},{64,96},{68,36},{96,128},{100,68},{1... | collective-permute-start | bytes 1179656 | tf_op jit(solution)/shard_map/p1r/ppermute | solution.py:36
  50.4 2.5 %collective-permute-done.8.rest_1_ = bf16[16,2,48,128]{3,2,1,0:T(8,128)(2,1)S(1)} collective-permute-done((bf16[16,2,48,128]{3,2,1,0:T(8,128)(2,1)S(1)}, bf16[16,2,48,128]{3,2,1,0:T(8,128)(2,1)S(1)}, u32[]{:S(2)}, u32[]{:S(2)}) %collective-permute-start.8) | collective-permute-done | bytes 393248 | tf_op jit(solution)/shard_map/p1a/ppermute | solution.py:36
  52.9 2.4 %collective-permute-start.14 = (bf16[16,2,48,128]{3,2,1,0:T(8,128)(2,1)S(1)}, bf16[16,2,48,128]{3,2,1,0:T(8,128)(2,1)S(1)}, u32[]{:S(2)}, u32[]{:S(2)}) collective-permute-start(bf16[16,2,48,128]{3,2,1,0:T(8,128)(2,1)S(1)} %collective-permute-done.8.rest_1_), channel_id=1, source_target_pairs={{0,4},{4,0},{1,5},{5,1},{2,6},{6,2},{3,7},{7,3},{8,12},{12,8},{9,1... | collective-permute-start | bytes 1179656 | tf_op jit(solution)/shard_map/p1a_swap/ppermute | solution.py:51
  55.3 0.0 collective-permute-start.9
  55.3 0.0 collective-permute-done.10.rest_3_
  55.3 1.1 %collective-permute-start.16 = (bf16[16,2,48,128]{3,2,1,0:T(8,128)(2,1)S(1)}, bf16[16,2,48,128]{3,2,1,0:T(8,128)(2,1)S(1)}, u32[]{:S(2)}, u32[]{:S(2)}) collective-permute-start(bf16[16,2,48,128]{3,2,1,0:T(8,128)(2,1)S(1)} %collective-permute-done.10.rest_3_), channel_id=1, source_target_pairs={{0,4},{4,0},{1,5},{5,1},{2,6},{6,2},{3,7},{7,3},{8,12},{12,8},{9,1... | collective-permute-start | bytes 1179656 | tf_op jit(solution)/shard_map/q0_swap/ppermute | solution.py:51
  56.5 0.0 collective-permute-done.4.t3
  56.5 1.1 %copy-done.1 = bf16[1024,384]{1,0:T(8,128)(2,1)S(1)} copy-done((bf16[1024,384]{1,0:T(8,128)(2,1)S(1)}, bf16[1024,384]{1,0:T(8,128)(2,1)}, u32[]{:S(2)}) %copy-start.1) | copy-done | bytes 786456
  57.6 1.1 %arrange_t.1 = (bf16[1024,768]{1,0:T(8,128)(2,1)S(1)}, bf16[1024,768]{1,0:T(8,128)(2,1)S(1)}) custom-call(bf16[1024,384]{1,0:T(8,128)(2,1)S(1)} %copy-done.1, bf16[1024,384]{1,0:T(8,128)(2,1)S(1)} %collective-permute-done.t1, bf16[1024,384]{1,0:T(8,128)(2,1)S(1)} %collective-permute-done.1.t2, bf16[1024,384]{1,0:T(8,128)(2,1)S(1)} %collective-permute-done.4.t3), custom_call_target="tpu_custom_call" | custom-call | bytes 6291456 | tf_op jit(solution)/shard_map/arrange_t/pallas_call | solution.py:200
  58.7 1.6 %collective-permute-start.15 = (bf16[16,2,48,128]{3,2,1,0:T(8,128)(2,1)S(1)}, bf16[16,2,48,128]{3,2,1,0:T(8,128)(2,1)S(1)}, u32[]{:S(2)}, u32[]{:S(2)}) collective-permute-start(bf16[16,2,48,128]{3,2,1,0:T(8,128)(2,1)S(1)} %collective-permute-done.12.rest_5_), channel_id=1, source_target_pairs={{0,4},{4,0},{1,5},{5,1},{2,6},{6,2},{3,7},{7,3},{8,12},{12,8},{9,1... | collective-permute-start | bytes 1179656 | tf_op jit(solution)/shard_map/p1r_swap/ppermute | solution.py:51
  60.3 1.4 %collective-permute-start.13 = (bf16[16,2,48,128]{3,2,1,0:T(8,128)(2,1)S(1)}, bf16[16,2,48,128]{3,2,1,0:T(8,128)(2,1)S(1)}, u32[]{:S(2)}, u32[]{:S(2)}) collective-permute-start(bf16[16,2,48,128]{3,2,1,0:T(8,128)(2,1)S(1)} %collective-permute-done.12.rest_5_), channel_id=1, source_target_pairs={{0,8},{4,28},{8,16},{12,4},{16,24},{20,12},{24,0},{28,20},{1,9},{5... | collective-permute-start | bytes 1179656 | tf_op jit(solution)/shard_map/q1r/ppermute | solution.py:41
  61.7 1.3 %collective-permute-start.11 = (bf16[16,2,48,128]{3,2,1,0:T(8,128)(2,1)S(1)}, bf16[16,2,48,128]{3,2,1,0:T(8,128)(2,1)S(1)}, u32[]{:S(2)}, u32[]{:S(2)}) collective-permute-start(bf16[16,2,48,128]{3,2,1,0:T(8,128)(2,1)S(1)} %collective-permute-done.10.rest_3_), channel_id=1, source_target_pairs={{0,32},{4,228},{32,64},{36,4},{64,96},{68,36},{96,128},{100,68},{1... | collective-permute-start | bytes 1179656 | tf_op jit(solution)/shard_map/q1a/ppermute | solution.py:36
  63.0 0.6 collective-permute-start.17
  63.7 3.2 %ladder_early.2.acc0 = f32[1024,1024]{1,0:T(8,128)S(1)} custom-call(s32[8,16]{1,0:T(8,128)S(1)} %copy-done.2, bf16[1024,768]{1,0:T(8,128)(2,1)S(1)} %get-tuple-element.38.t_ref, bf16[1024,2048]{1,0:T(8,128)(2,1)S(1)} %copy-done, bf16[16,2,48,128]{3,2,1,0:T(8,128)(2,1)S(1)} %get-tuple-element.35.rest_0_, ...), custom_call_target="tpu_custom_call" | custom-call | flops 1610612736 | bytes 9437184 | tf_op jit(solution)/shard_map/ladder_early/pallas_call | solution.py:240
  66.9 0.4 collective-permute-done.13.rest_5_
  67.2 1.4 %collective-permute-done.11.rest_1_ = bf16[16,2,48,128]{3,2,1,0:T(8,128)(2,1)S(1)} collective-permute-done((bf16[16,2,48,128]{3,2,1,0:T(8,128)(2,1)S(1)}, bf16[16,2,48,128]{3,2,1,0:T(8,128)(2,1)S(1)}, u32[]{:S(2)}, u32[]{:S(2)}) %collective-permute-start.11) | collective-permute-done | bytes 393248 | tf_op jit(solution)/shard_map/q1a/ppermute | solution.py:36
  68.6 3.2 %ladder_early.3.acc1 = f32[1024,1024]{1,0:T(8,128)S(1)} custom-call(s32[8,16]{1,0:T(8,128)S(1)} %copy-done.2, bf16[1024,768]{1,0:T(8,128)(2,1)S(1)} %get-tuple-element.38.t_ref, bf16[1024,2048]{1,0:T(8,128)(2,1)S(1)} %copy-done, bf16[16,2,48,128]{3,2,1,0:T(8,128)(2,1)S(1)} %get-tuple-element.35.rest_0_, ...), custom_call_target="tpu_custom_call" | custom-call | flops 1610612736 | bytes 9437184 | tf_op jit(solution)/shard_map/ladder_early/pallas_call | solution.py:240
  71.8 1.9 %collective-permute-start.21 = (bf16[16,2,48,128]{3,2,1,0:T(8,128)(2,1)S(1)}, bf16[16,2,48,128]{3,2,1,0:T(8,128)(2,1)S(1)}, u32[]{:S(2)}, u32[]{:S(2)}) collective-permute-start(bf16[16,2,48,128]{3,2,1,0:T(8,128)(2,1)S(1)} %collective-permute-done.17.rest_3_), channel_id=1, source_target_pairs={{0,4},{4,0},{1,5},{5,1},{2,6},{6,2},{3,7},{7,3},{8,12},{12,8},{9,1... | collective-permute-start | bytes 1179656 | tf_op jit(solution)/shard_map/q2_swap/ppermute | solution.py:51
  73.8 0.0 collective-permute-start.19
  73.8 0.5 collective-permute-start.20
  74.3 0.0 collective-permute-start.18
  74.3 0.8 %collective-permute-done.21.rest_7_ = bf16[16,2,48,128]{3,2,1,0:T(8,128)(2,1)S(1)} collective-permute-done((bf16[16,2,48,128]{3,2,1,0:T(8,128)(2,1)S(1)}, bf16[16,2,48,128]{3,2,1,0:T(8,128)(2,1)S(1)}, u32[]{:S(2)}, u32[]{:S(2)}) %collective-permute-start.21) | collective-permute-done | bytes 393248 | tf_op jit(solution)/shard_map/q2_swap/ppermute | solution.py:51
  75.1 0.6 collective-permute-done.19.rest_4_
  75.7 0.6 collective-permute-done.20.rest_6_
  76.3 0.6 collective-permute-done.18.rest_2_
  76.8 5.6 %ladder_late.1 = bf16[1024,2048]{1,0:T(8,128)(2,1)} custom-call(s32[8,16]{1,0:T(8,128)S(1)} %copy-done.2, bf16[1024,768]{1,0:T(8,128)(2,1)S(1)} %get-tuple-element.31.t_ref, f32[1024,1024]{1,0:T(8,128)S(1)} %ladder_early.2.acc0, f32[1024,1024]{1,0:T(8,128)S(1)} %ladder_early.3.acc1, bf16[16,2,48,128]{3,2,1,0:T(8,128)(2,1)S(1)} %collective-permute-done.9.rest_0_, ...), custom_call_target="tpu_custom_call" | custom-call | flops 3221225472 | bytes 17301504 | tf_op jit(solution)/shard_map/ladder_late/pallas_call | solution.py:284
  (14 shorter events, 0.0 us)
Async XLA Ops:
  0.0 63.6 %copy-start.2 = (s32[8,16]{1,0:T(8,128)S(1)}, s32[8,16]{1,0:T(8,128)}, u32[]{:S(2)}) copy-start(s32[8,16]{1,0:T(8,128)} %mask_ref.5) | copy-start | bytes 1540
  3.9 25.8 %all-to-all-start = ((bf16[32,48,128]{2,1,0:T(8,128)(2,1)}), bf16[32,48,128]{2,1,0:T(8,128)(2,1)S(1)}, u32[]{:S(2)}, u32[]{:S(2)}) async-start(bf16[32,48,128]{2,1,0:T(8,128)(2,1)} %get-tuple-element.27), calls=%async_computation | async-start | bytes 786432 | tf_op jit(solution)/shard_map/all_to_all | solution.py:302
  15.9 21.5 %collective-permute-start.1 = (bf16[1024,384]{1,0:T(8,128)(2,1)}, bf16[1024,384]{1,0:T(8,128)(2,1)S(1)}, u32[]{:S(2)}, u32[]{:S(2)}) collective-permute-start(bf16[1024,384]{1,0:T(8,128)(2,1)} %get-tuple-element.26.t0), channel_id=1, source_target_pairs={{0,3},{1,0},{2,1},{3,2},{4,5},{5,6},{6,7},{7,4},{8,11},{9,8},{10,9... | collective-permute-start | bytes 2359304 | tf_op jit(solution)/shard_map/t_back/ppermute | solution.py:46
  17.2 20.2 %collective-permute-start = (bf16[1024,384]{1,0:T(8,128)(2,1)}, bf16[1024,384]{1,0:T(8,128)(2,1)S(1)}, u32[]{:S(2)}, u32[]{:S(2)}) collective-permute-start(bf16[1024,384]{1,0:T(8,128)(2,1)} %get-tuple-element.26.t0), channel_id=1, source_target_pairs={{0,1},{1,2},{2,3},{3,0},{4,7},{5,4},{6,5},{7,6},{8,9},{9,10},{10,1... | collective-permute-start | bytes 2359304 | tf_op jit(solution)/shard_map/t_near/ppermute | solution.py:46
  29.7 3.8 %collective-permute-start.2 = (bf16[32,48,128]{2,1,0:T(8,128)(2,1)S(1)}, bf16[32,48,128]{2,1,0:T(8,128)(2,1)S(1)}, u32[]{:S(2)}, u32[]{:S(2)}) collective-permute-start(bf16[32,48,128]{2,1,0:T(8,128)(2,1)S(1)} %all-to-all-done.a_ref), channel_id=1, source_target_pairs={{0,4},{4,0},{1,5},{5,1},{2,6},{6,2},{3,7},{7,3},{8,12},{12,8},{9,1... | collective-permute-start | bytes 1179656 | tf_op jit(solution)/shard_map/v_swap/ppermute | solution.py:51
  32.2 31.4 %copy-start = (bf16[1024,2048]{1,0:T(8,128)(2,1)S(1)}, bf16[1024,2048]{1,0:T(8,128)(2,1)}, u32[]{:S(2)}) copy-start(bf16[1024,2048]{1,0:T(8,128)(2,1)} %r_ref.3) | copy-start | bytes 12582916
  34.3 7.3 %collective-permute-start.3 = (bf16[16,48,128]{2,1,0:T(8,128)(2,1)S(1)}, bf16[16,48,128]{2,1,0:T(8,128)(2,1)S(1)}, u32[]{:S(2)}, u32[]{:S(2)}) collective-permute-start(bf16[16,48,128]{2,1,0:T(8,128)(2,1)S(1)} %get-tuple-element.28), channel_id=1, source_target_pairs={{0,1},{1,2},{2,3},{3,0},{4,7},{5,4},{6,5},{7,6},{8,9},{9,10},{10,1... | collective-permute-start | bytes 589832 | tf_op jit(solution)/shard_map/r_near/ppermute | solution.py:46
  36.9 6.0 %collective-permute-start.6 = (bf16[8,48,128]{2,1,0:T(8,128)(2,1)S(1)}, bf16[8,48,128]{2,1,0:T(8,128)(2,1)S(1)}, u32[]{:S(2)}, u32[]{:S(2)}) collective-permute-start(bf16[8,48,128]{2,1,0:T(8,128)(2,1)S(1)} %get-tuple-element.34), channel_id=1, source_target_pairs={{0,2},{1,3},{2,0},{3,1},{4,6},{5,7},{6,4},{7,5},{8,10},{9,11},{10,... | collective-permute-start | bytes 294920 | tf_op jit(solution)/shard_map/r_far/ppermute | solution.py:308
  41.6 4.1 %collective-permute-start.5 = (bf16[16,48,128]{2,1,0:T(8,128)(2,1)S(1)}, bf16[16,48,128]{2,1,0:T(8,128)(2,1)S(1)}, u32[]{:S(2)}, u32[]{:S(2)}) collective-permute-start(bf16[16,48,128]{2,1,0:T(8,128)(2,1)S(1)} %collective-permute-done.3.r1_ref), channel_id=1, source_target_pairs={{0,4},{4,0},{1,5},{5,1},{2,6},{6,2},{3,7},{7,3},{8,12},{12,8},{9,1... | collective-permute-start | bytes 589832 | tf_op jit(solution)/shard_map/r_near_swap/ppermute | solution.py:51
  42.9 2.8 %collective-permute-start.7 = (bf16[8,48,128]{2,1,0:T(8,128)(2,1)S(1)}, bf16[8,48,128]{2,1,0:T(8,128)(2,1)S(1)}, u32[]{:S(2)}, u32[]{:S(2)}) collective-permute-start(bf16[8,48,128]{2,1,0:T(8,128)(2,1)S(1)} %collective-permute-done.6.r2_ref), channel_id=1, source_target_pairs={{0,4},{4,0},{1,5},{5,1},{2,6},{6,2},{3,7},{7,3},{8,12},{12,8},{9,1... | collective-permute-start | bytes 294920 | tf_op jit(solution)/shard_map/r_far_swap/ppermute | solution.py:51
  44.8 11.7 %collective-permute-start.4 = (bf16[1024,384]{1,0:T(8,128)(2,1)S(1)}, bf16[1024,384]{1,0:T(8,128)(2,1)S(1)}, u32[]{:S(2)}, u32[]{:S(2)}) collective-permute-start(bf16[1024,384]{1,0:T(8,128)(2,1)S(1)} %collective-permute-done.t1), channel_id=1, source_target_pairs={{0,1},{1,2},{2,3},{3,0},{4,7},{5,4},{6,5},{7,6},{8,9},{9,10},{10,1... | collective-permute-start | bytes 2359304 | tf_op jit(solution)/shard_map/t_far/ppermute | solution.py:46
  45.9 7.0 %collective-permute-start.8 = (bf16[16,2,48,128]{3,2,1,0:T(8,128)(2,1)S(1)}, bf16[16,2,48,128]{3,2,1,0:T(8,128)(2,1)S(1)}, u32[]{:S(2)}, u32[]{:S(2)}) collective-permute-start(bf16[16,2,48,128]{3,2,1,0:T(8,128)(2,1)S(1)} %get-tuple-element.35.rest_0_), channel_id=1, source_target_pairs={{0,32},{4,228},{32,64},{36,4},{64,96},{68,36},{96,128},{100,68},{1... | collective-permute-start | bytes 1179656 | tf_op jit(solution)/shard_map/p1a/ppermute | solution.py:36
  46.8 8.5 %collective-permute-start.10 = (bf16[16,2,48,128]{3,2,1,0:T(8,128)(2,1)S(1)}, bf16[16,2,48,128]{3,2,1,0:T(8,128)(2,1)S(1)}, u32[]{:S(2)}, u32[]{:S(2)}) collective-permute-start(bf16[16,2,48,128]{3,2,1,0:T(8,128)(2,1)S(1)} %get-tuple-element.35.rest_0_), channel_id=1, source_target_pairs={{0,8},{4,28},{8,16},{12,4},{16,24},{20,12},{24,0},{28,20},{1,9},{5... | collective-permute-start | bytes 1179656 | tf_op jit(solution)/shard_map/q0/ppermute | solution.py:41
  49.3 9.4 %collective-permute-start.12 = (bf16[16,2,48,128]{3,2,1,0:T(8,128)(2,1)S(1)}, bf16[16,2,48,128]{3,2,1,0:T(8,128)(2,1)S(1)}, u32[]{:S(2)}, u32[]{:S(2)}) collective-permute-start(bf16[16,2,48,128]{3,2,1,0:T(8,128)(2,1)S(1)} %get-tuple-element.36.rest_4_), channel_id=1, source_target_pairs={{0,32},{4,228},{32,64},{36,4},{64,96},{68,36},{96,128},{100,68},{1... | collective-permute-start | bytes 1179656 | tf_op jit(solution)/shard_map/p1r/ppermute | solution.py:36
  52.9 5.8 %collective-permute-start.14 = (bf16[16,2,48,128]{3,2,1,0:T(8,128)(2,1)S(1)}, bf16[16,2,48,128]{3,2,1,0:T(8,128)(2,1)S(1)}, u32[]{:S(2)}, u32[]{:S(2)}) collective-permute-start(bf16[16,2,48,128]{3,2,1,0:T(8,128)(2,1)S(1)} %collective-permute-done.8.rest_1_), channel_id=1, source_target_pairs={{0,4},{4,0},{1,5},{5,1},{2,6},{6,2},{3,7},{7,3},{8,12},{12,8},{9,1... | collective-permute-start | bytes 1179656 | tf_op jit(solution)/shard_map/p1a_swap/ppermute | solution.py:51
  55.3 7.7 %collective-permute-start.9 = (bf16[16,2,48,128]{3,2,1,0:T(8,128)(2,1)S(1)}, bf16[16,2,48,128]{3,2,1,0:T(8,128)(2,1)S(1)}, u32[]{:S(2)}, u32[]{:S(2)}) collective-permute-start(bf16[16,2,48,128]{3,2,1,0:T(8,128)(2,1)S(1)} %collective-permute-done.8.rest_1_), channel_id=1, source_target_pairs={{0,32},{4,228},{32,64},{36,4},{64,96},{68,36},{96,128},{100,68},{1... | collective-permute-start | bytes 1179656 | tf_op jit(solution)/shard_map/p2/ppermute | solution.py:36
  55.3 8.3 %collective-permute-start.16 = (bf16[16,2,48,128]{3,2,1,0:T(8,128)(2,1)S(1)}, bf16[16,2,48,128]{3,2,1,0:T(8,128)(2,1)S(1)}, u32[]{:S(2)}, u32[]{:S(2)}) collective-permute-start(bf16[16,2,48,128]{3,2,1,0:T(8,128)(2,1)S(1)} %collective-permute-done.10.rest_3_), channel_id=1, source_target_pairs={{0,4},{4,0},{1,5},{5,1},{2,6},{6,2},{3,7},{7,3},{8,12},{12,8},{9,1... | collective-permute-start | bytes 1179656 | tf_op jit(solution)/shard_map/q0_swap/ppermute | solution.py:51
  56.5 1.1 %copy-start.1 = (bf16[1024,384]{1,0:T(8,128)(2,1)S(1)}, bf16[1024,384]{1,0:T(8,128)(2,1)}, u32[]{:S(2)}) copy-start(bf16[1024,384]{1,0:T(8,128)(2,1)} %get-tuple-element.26.t0) | copy-start | bytes 2359300
  58.7 4.9 %collective-permute-start.15 = (bf16[16,2,48,128]{3,2,1,0:T(8,128)(2,1)S(1)}, bf16[16,2,48,128]{3,2,1,0:T(8,128)(2,1)S(1)}, u32[]{:S(2)}, u32[]{:S(2)}) collective-permute-start(bf16[16,2,48,128]{3,2,1,0:T(8,128)(2,1)S(1)} %collective-permute-done.12.rest_5_), channel_id=1, source_target_pairs={{0,4},{4,0},{1,5},{5,1},{2,6},{6,2},{3,7},{7,3},{8,12},{12,8},{9,1... | collective-permute-start | bytes 1179656 | tf_op jit(solution)/shard_map/p1r_swap/ppermute | solution.py:51
  60.3 6.9 %collective-permute-start.13 = (bf16[16,2,48,128]{3,2,1,0:T(8,128)(2,1)S(1)}, bf16[16,2,48,128]{3,2,1,0:T(8,128)(2,1)S(1)}, u32[]{:S(2)}, u32[]{:S(2)}) collective-permute-start(bf16[16,2,48,128]{3,2,1,0:T(8,128)(2,1)S(1)} %collective-permute-done.12.rest_5_), channel_id=1, source_target_pairs={{0,8},{4,28},{8,16},{12,4},{16,24},{20,12},{24,0},{28,20},{1,9},{5... | collective-permute-start | bytes 1179656 | tf_op jit(solution)/shard_map/q1r/ppermute | solution.py:41
  61.7 6.9 %collective-permute-start.11 = (bf16[16,2,48,128]{3,2,1,0:T(8,128)(2,1)S(1)}, bf16[16,2,48,128]{3,2,1,0:T(8,128)(2,1)S(1)}, u32[]{:S(2)}, u32[]{:S(2)}) collective-permute-start(bf16[16,2,48,128]{3,2,1,0:T(8,128)(2,1)S(1)} %collective-permute-done.10.rest_3_), channel_id=1, source_target_pairs={{0,32},{4,228},{32,64},{36,4},{64,96},{68,36},{96,128},{100,68},{1... | collective-permute-start | bytes 1179656 | tf_op jit(solution)/shard_map/q1a/ppermute | solution.py:36
  63.0 8.8 %collective-permute-start.17 = (bf16[16,2,48,128]{3,2,1,0:T(8,128)(2,1)S(1)}, bf16[16,2,48,128]{3,2,1,0:T(8,128)(2,1)S(1)}, u32[]{:S(2)}, u32[]{:S(2)}) collective-permute-start(bf16[16,2,48,128]{3,2,1,0:T(8,128)(2,1)S(1)} %collective-permute-done.9.rest_0_), channel_id=1, source_target_pairs={{0,8},{4,28},{8,16},{12,4},{16,24},{20,12},{24,0},{28,20},{1,9},{5... | collective-permute-start | bytes 1179656 | tf_op jit(solution)/shard_map/q2/ppermute | solution.py:41
  71.8 3.3 %collective-permute-start.21 = (bf16[16,2,48,128]{3,2,1,0:T(8,128)(2,1)S(1)}, bf16[16,2,48,128]{3,2,1,0:T(8,128)(2,1)S(1)}, u32[]{:S(2)}, u32[]{:S(2)}) collective-permute-start(bf16[16,2,48,128]{3,2,1,0:T(8,128)(2,1)S(1)} %collective-permute-done.17.rest_3_), channel_id=1, source_target_pairs={{0,4},{4,0},{1,5},{5,1},{2,6},{6,2},{3,7},{7,3},{8,12},{12,8},{9,1... | collective-permute-start | bytes 1179656 | tf_op jit(solution)/shard_map/q2_swap/ppermute | solution.py:51
  73.8 1.9 %collective-permute-start.19 = (bf16[16,2,48,128]{3,2,1,0:T(8,128)(2,1)S(1)}, bf16[16,2,48,128]{3,2,1,0:T(8,128)(2,1)S(1)}, u32[]{:S(2)}, u32[]{:S(2)}) collective-permute-start(bf16[16,2,48,128]{3,2,1,0:T(8,128)(2,1)S(1)} %collective-permute-done.9.rest_0_), channel_id=1, source_target_pairs={{0,4},{4,0},{1,5},{5,1},{2,6},{6,2},{3,7},{7,3},{8,12},{12,8},{9,1... | collective-permute-start | bytes 1179656 | tf_op jit(solution)/shard_map/p2_swap/ppermute | solution.py:51
  73.8 2.5 %collective-permute-start.20 = (bf16[16,2,48,128]{3,2,1,0:T(8,128)(2,1)S(1)}, bf16[16,2,48,128]{3,2,1,0:T(8,128)(2,1)S(1)}, u32[]{:S(2)}, u32[]{:S(2)}) collective-permute-start(bf16[16,2,48,128]{3,2,1,0:T(8,128)(2,1)S(1)} %collective-permute-done.11.rest_1_), channel_id=1, source_target_pairs={{0,4},{4,0},{1,5},{5,1},{2,6},{6,2},{3,7},{7,3},{8,12},{12,8},{9,1... | collective-permute-start | bytes 1179656 | tf_op jit(solution)/shard_map/q1a_swap/ppermute | solution.py:51
  74.3 2.5 %collective-permute-start.18 = (bf16[16,2,48,128]{3,2,1,0:T(8,128)(2,1)S(1)}, bf16[16,2,48,128]{3,2,1,0:T(8,128)(2,1)S(1)}, u32[]{:S(2)}, u32[]{:S(2)}) collective-permute-start(bf16[16,2,48,128]{3,2,1,0:T(8,128)(2,1)S(1)} %collective-permute-done.13.rest_5_), channel_id=1, source_target_pairs={{0,4},{4,0},{1,5},{5,1},{2,6},{6,2},{3,7},{7,3},{8,12},{12,8},{9,1... | collective-permute-start | bytes 1179656 | tf_op jit(solution)/shard_map/q1r_swap/ppermute | solution.py:51

commit v4 on v3

--- a/solution.py
+++ b/solution.py
@@ -86,15 +86,18 @@
         shift = jnp.where(lane >= q * CHUNK, (g - q) * CHUNK, shift)
     perm[...] = jnp.where(source == target + shift, 1.0, 0.0).astype(perm.dtype)
 
-    @pl.loop(0, rows // TILE)
-    def _(a):
-        at = pl.ds(pl.multiple_of(a * TILE, TILE), TILE)
-        tiles = []
-        for j in range(cols // TILE):
-            t = t_ref[at, j * TILE : (j + 1) * TILE]
-            tiles.append(jnp.where(t_mask_ref[j, a] != 0, t, jnp.zeros_like(t)))
-        kept = jnp.concatenate(tiles, axis=1)
-        t_out[at, :] = jnp.dot(kept, perm[...], preferred_element_type=jnp.float32).astype(t_out.dtype)
+    @pl.loop(0, rows // ROWS)
+    def _(i):
+        start = pl.multiple_of(i * ROWS, ROWS)
+        bands = []
+        for a in range(ROWS // TILE):
+            tiles = []
+            for j in range(cols // TILE):
+                t = t_ref[pl.ds(start + a * TILE, TILE), j * TILE : (j + 1) * TILE]
+                tiles.append(jnp.where(t_mask_ref[j, i * (ROWS // TILE) + a] != 0, t, jnp.zeros_like(t)))
+            bands.append(jnp.concatenate(tiles, axis=1))
+        kept = jnp.concatenate(bands, axis=0)
+        t_out[pl.ds(start, ROWS), :] = jnp.dot(kept, perm[...], preferred_element_type=jnp.float32).astype(t_out.dtype)
 
 
 def prepare(t_mask, v_mask, t, v):
@@ -321,12 +324,14 @@
     p1r_swap = swap("p1r_swap", near_r)
     blocks = (ahead, p1a, p1r_swap, q0, rest, p1r, p1a_swap, swap("q0_swap", q0))
     acc0 = early(0, r_mask, t_early, r_old, blocks)
-    p2, q1a, q1r, acc0 = hold((p2, q1a, q1r, acc0))
+    p2h, acc0 = hold((p2, acc0))
     acc1 = early(HALF, r_mask, t_early, r_old, blocks)
-    q2, acc1 = hold((q2, acc1))
-    swapped = [swap(n + "_swap", v) for n, v in (("q1r", q1r), ("p2", p2), ("q1a", q1a), ("q2", q2))]
-    blocks = (p2, q1a, swapped[0], q2, swapped[1], q1r, swapped[2], swapped[3])
-    return late(r_mask, t_late, (acc0, acc1), blocks)
+    q1a, q1r, acc1 = hold((q1a, q1r, acc1))
+    q1a_swap, q1r_swap, p2_swap = swap("q1a_swap", q1a), swap("q1r_swap", q1r), swap("p2_swap", p2h)
+    q2, q1a_swap, q1r_swap, p2_swap = hold((q2, q1a_swap, q1r_swap, p2_swap))
+    accs = (acc0, acc1)
+    blocks = (p2h, q1a, q1r_swap, q2, p2_swap, q1r, q1a_swap, swap("q2_swap", q2))
+    return late(r_mask, t_late, accs, blocks)
 
 
 def solution(mesh):

time: 82.8 us -> 80.8 us (0.976)
  waiting for transfers between devices: 23.9 us -> 22.9 us
    ppermute x4, waiting for transfers between devices: 3.87 us -> 2.47 us  [move_z(): return lax.ppermute(v, ('z', 'c'), pairs_zc(1))]
  transfers between devices with their start and end apart: 23 -> 23, of which waited for: 12 -> 10; matrix products, arithmetic and copies ran while one was open for 1% -> 1% of each run, Pallas kernels for 10% -> 10%
where the time goes in v4:
time: 80.8 us; the launch traced here: 80.6 us
  starting transfers between devices  38.1 us (47%)
  waiting for transfers between devices  22.9 us (28%)
  Pallas kernels  17.2 us (21%)
  local copies, waits for them, and re-layouts  1.14 us (1%)
  other arithmetic  1 us (1%)
    all_to_all x1, starting transfers between devices, body(): mine = lax.all_to_all(spread, ('z', 'y'), 0, 0)  12 us
    ppermute x10, starting transfers between devices, swap(): return lax.ppermute(v, 'c', [(0, 1), (1, 0)])  11.9 us
    all_to_all x1, waiting for transfers between devices, body(): mine = lax.all_to_all(spread, ('z', 'y'), 0, 0)  11.1 us
    pallas_call x2, Pallas kernels, early(): pl.pallas_call(functools.partial(early_kernel, first), out_shape=jax.Shap...  6.39 us
    ppermute x4, starting transfers between devices, move_x(): return lax.ppermute(v, ('c', 'x'), pairs_cx(d))  5.79 us
    pallas_call x1, Pallas kernels, late(): pl.pallas_call(late_kernel, out_shape=jax.ShapeDtypeStruct((rows, width),...  5.56 us
    ppermute x3, starting transfers between devices, move_y(): return lax.ppermute(v, ('y', 'c'), pairs_yc(1))  4.4 us
    ppermute x4, waiting for transfers between devices, move_x(): return lax.ppermute(v, ('c', 'x'), pairs_cx(d))  4.2 us
  transfers between devices with their start and end apart: 23, of which 10 were waited for; matrix products, arithmetic and copies ran while one was open for 1% of the time, Pallas kernels for 10%

profile of v4, /device:TPU:1, one launch (start us, length us, event | category | flops | bytes accessed | tf_op | source)
XLA Modules:
  0.0 80.6 jit_solution(7067879647439197660)
XLA Ops:
  0.0 3.2 %prepare.1 = (bf16[1024,384]{1,0:T(8,128)(2,1)}, bf16[32,48,128]{2,1,0:T(8,128)(2,1)}) custom-call(s32[3,8]{1,0:T(4,128)} %bitcast.2, s32[1,3]{1,0:T(1,128)} %bitcast.3, bf16[1024,384]{1,0:T(8,128)(2,1)} %t_ref.1, bf16[384,128]{1,0:T(8,128)(2,1)} %v_ref.1), custom_call_target="tpu_custom_call" | custom-call | flops 301989888 | bytes 2162688 | tf_op jit(solution)/shard_map/prepare/pallas_call | solution.py:104
  3.2 12.0 %all-to-all-start = ((bf16[32,48,128]{2,1,0:T(8,128)(2,1)}), bf16[32,48,128]{2,1,0:T(8,128)(2,1)S(1)}, u32[]{:S(2)}, u32[]{:S(2)}) async-start(bf16[32,48,128]{2,1,0:T(8,128)(2,1)} %get-tuple-element.30), calls=%async_computation | async-start | bytes 786432 | tf_op jit(solution)/shard_map/all_to_all | solution.py:305
  15.3 1.3 %collective-permute-start.1 = (bf16[1024,384]{1,0:T(8,128)(2,1)}, bf16[1024,384]{1,0:T(8,128)(2,1)S(1)}, u32[]{:S(2)}, u32[]{:S(2)}) collective-permute-start(bf16[1024,384]{1,0:T(8,128)(2,1)} %get-tuple-element.29.t0), channel_id=1, source_target_pairs={{0,3},{1,0},{2,1},{3,2},{4,5},{5,6},{6,7},{7,4},{8,11},{9,8},{10,9... | collective-permute-start | bytes 2359304 | tf_op jit(solution)/shard_map/t_back/ppermute | solution.py:46
  16.6 1.5 %collective-permute-start = (bf16[1024,384]{1,0:T(8,128)(2,1)}, bf16[1024,384]{1,0:T(8,128)(2,1)S(1)}, u32[]{:S(2)}, u32[]{:S(2)}) collective-permute-start(bf16[1024,384]{1,0:T(8,128)(2,1)} %get-tuple-element.29.t0), channel_id=1, source_target_pairs={{0,1},{1,2},{2,3},{3,0},{4,7},{5,4},{6,5},{7,6},{8,9},{9,10},{10,1... | collective-permute-start | bytes 2359304 | tf_op jit(solution)/shard_map/t_near/ppermute | solution.py:46
  18.0 11.1 %all-to-all-done.a_ref = bf16[32,48,128]{2,1,0:T(8,128)(2,1)S(1)} async-done(((bf16[32,48,128]{2,1,0:T(8,128)(2,1)}), bf16[32,48,128]{2,1,0:T(8,128)(2,1)S(1)}, u32[]{:S(2)}, u32[]{:S(2)}) %all-to-all-start) | async-done | bytes 393248 | tf_op jit(solution)/shard_map/all_to_all | solution.py:305
  29.1 2.5 %collective-permute-start.2 = (bf16[32,48,128]{2,1,0:T(8,128)(2,1)S(1)}, bf16[32,48,128]{2,1,0:T(8,128)(2,1)S(1)}, u32[]{:S(2)}, u32[]{:S(2)}) collective-permute-start(bf16[32,48,128]{2,1,0:T(8,128)(2,1)S(1)} %all-to-all-done.a_ref), channel_id=1, source_target_pairs={{0,4},{4,0},{1,5},{5,1},{2,6},{6,2},{3,7},{7,3},{8,12},{12,8},{9,1... | collective-permute-start | bytes 1179656 | tf_op jit(solution)/shard_map/v_swap/ppermute | solution.py:51
  31.6 1.0 %select_reduce_fusion.pick_ref = s32[40]{0:T(128)S(1)} fusion(s32[64]{0:T(128)S(1)} %fusion, s32[64]{0:T(128)} %param.11, s32[40]{0:T(128)S(1)} %compare_select_fusion.2), kind=kLoop, calls=%fused_computation | loop fusion | flops 7640 | bytes 832 | tf_op jit(solution)/shard_map/reduce_sum | solution.py:150
  32.6 0.3 collective-permute-done.2.b_ref
  32.9 0.8 select_columns.1
  33.7 2.6 %collective-permute-start.3 = (bf16[16,48,128]{2,1,0:T(8,128)(2,1)S(1)}, bf16[16,48,128]{2,1,0:T(8,128)(2,1)S(1)}, u32[]{:S(2)}, u32[]{:S(2)}) collective-permute-start(bf16[16,48,128]{2,1,0:T(8,128)(2,1)S(1)} %get-tuple-element.31), channel_id=1, source_target_pairs={{0,1},{1,2},{2,3},{3,0},{4,7},{5,4},{6,5},{7,6},{8,9},{9,10},{10,1... | collective-permute-start | bytes 589832 | tf_op jit(solution)/shard_map/r_near/ppermute | solution.py:46
  36.3 0.5 collective-permute-start.6
  36.8 0.0 collective-permute-done.1.t2
  36.8 0.0 collective-permute-done.t1
  36.8 4.2 %collective-permute-done.3.r1_ref = bf16[16,48,128]{2,1,0:T(8,128)(2,1)S(1)} collective-permute-done((bf16[16,48,128]{2,1,0:T(8,128)(2,1)S(1)}, bf16[16,48,128]{2,1,0:T(8,128)(2,1)S(1)}, u32[]{:S(2)}, u32[]{:S(2)}) %collective-permute-start.3) | collective-permute-done | bytes 196640 | tf_op jit(solution)/shard_map/r_near/ppermute | solution.py:46
  41.0 0.2 collective-permute-start.5
  41.2 1.0 %collective-permute-done.6.r2_ref = bf16[8,48,128]{2,1,0:T(8,128)(2,1)S(1)} collective-permute-done((bf16[8,48,128]{2,1,0:T(8,128)(2,1)S(1)}, bf16[8,48,128]{2,1,0:T(8,128)(2,1)S(1)}, u32[]{:S(2)}, u32[]{:S(2)}) %collective-permute-start.6) | collective-permute-done | bytes 98336 | tf_op jit(solution)/shard_map/r_far/ppermute | solution.py:311
  42.3 1.9 %collective-permute-start.7 = (bf16[8,48,128]{2,1,0:T(8,128)(2,1)S(1)}, bf16[8,48,128]{2,1,0:T(8,128)(2,1)S(1)}, u32[]{:S(2)}, u32[]{:S(2)}) collective-permute-start(bf16[8,48,128]{2,1,0:T(8,128)(2,1)S(1)} %collective-permute-done.6.r2_ref), channel_id=1, source_target_pairs={{0,4},{4,0},{1,5},{5,1},{2,6},{6,2},{3,7},{7,3},{8,12},{12,8},{9,1... | collective-permute-start | bytes 294920 | tf_op jit(solution)/shard_map/r_far_swap/ppermute | solution.py:51
  44.1 0.5 collective-permute-start.4
  44.6 0.5 collective-permute-done.7.w2_ref
  45.1 0.2 pack_shard.1
  45.2 1.0 %collective-permute-start.8 = (bf16[16,2,48,128]{3,2,1,0:T(8,128)(2,1)S(1)}, bf16[16,2,48,128]{3,2,1,0:T(8,128)(2,1)S(1)}, u32[]{:S(2)}, u32[]{:S(2)}) collective-permute-start(bf16[16,2,48,128]{3,2,1,0:T(8,128)(2,1)S(1)} %get-tuple-element.38.rest_0_), channel_id=1, source_target_pairs={{0,32},{4,228},{32,64},{36,4},{64,96},{68,36},{96,128},{100,68},{1... | collective-permute-start | bytes 1179656 | tf_op jit(solution)/shard_map/p1a/ppermute | solution.py:36
  46.2 2.4 %collective-permute-start.13 = (bf16[16,2,48,128]{3,2,1,0:T(8,128)(2,1)S(1)}, bf16[16,2,48,128]{3,2,1,0:T(8,128)(2,1)S(1)}, u32[]{:S(2)}, u32[]{:S(2)}) collective-permute-start(bf16[16,2,48,128]{3,2,1,0:T(8,128)(2,1)S(1)} %get-tuple-element.38.rest_0_), channel_id=1, source_target_pairs={{0,8},{4,28},{8,16},{12,4},{16,24},{20,12},{24,0},{28,20},{1,9},{5... | collective-permute-start | bytes 1179656 | tf_op jit(solution)/shard_map/q0/ppermute | solution.py:41
  48.6 1.2 %collective-permute-start.11 = (bf16[16,2,48,128]{3,2,1,0:T(8,128)(2,1)S(1)}, bf16[16,2,48,128]{3,2,1,0:T(8,128)(2,1)S(1)}, u32[]{:S(2)}, u32[]{:S(2)}) collective-permute-start(bf16[16,2,48,128]{3,2,1,0:T(8,128)(2,1)S(1)} %get-tuple-element.39.rest_4_), channel_id=1, source_target_pairs={{0,32},{4,228},{32,64},{36,4},{64,96},{68,36},{96,128},{100,68},{1... | collective-permute-start | bytes 1179656 | tf_op jit(solution)/shard_map/p1r/ppermute | solution.py:36
  49.8 2.5 %collective-permute-done.8.rest_1_ = bf16[16,2,48,128]{3,2,1,0:T(8,128)(2,1)S(1)} collective-permute-done((bf16[16,2,48,128]{3,2,1,0:T(8,128)(2,1)S(1)}, bf16[16,2,48,128]{3,2,1,0:T(8,128)(2,1)S(1)}, u32[]{:S(2)}, u32[]{:S(2)}) %collective-permute-start.8) | collective-permute-done | bytes 393248 | tf_op jit(solution)/shard_map/p1a/ppermute | solution.py:36
  52.2 2.4 %collective-permute-start.10 = (bf16[16,2,48,128]{3,2,1,0:T(8,128)(2,1)S(1)}, bf16[16,2,48,128]{3,2,1,0:T(8,128)(2,1)S(1)}, u32[]{:S(2)}, u32[]{:S(2)}) collective-permute-start(bf16[16,2,48,128]{3,2,1,0:T(8,128)(2,1)S(1)} %collective-permute-done.8.rest_1_), channel_id=1, source_target_pairs={{0,4},{4,0},{1,5},{5,1},{2,6},{6,2},{3,7},{7,3},{8,12},{12,8},{9,1... | collective-permute-start | bytes 1179656 | tf_op jit(solution)/shard_map/p1a_swap/ppermute | solution.py:51
  54.7 1.1 %collective-permute-start.14 = (bf16[16,2,48,128]{3,2,1,0:T(8,128)(2,1)S(1)}, bf16[16,2,48,128]{3,2,1,0:T(8,128)(2,1)S(1)}, u32[]{:S(2)}, u32[]{:S(2)}) collective-permute-start(bf16[16,2,48,128]{3,2,1,0:T(8,128)(2,1)S(1)} %collective-permute-done.13.rest_3_), channel_id=1, source_target_pairs={{0,4},{4,0},{1,5},{5,1},{2,6},{6,2},{3,7},{7,3},{8,12},{12,8},{9,1... | collective-permute-start | bytes 1179656 | tf_op jit(solution)/shard_map/q0_swap/ppermute | solution.py:51
  55.8 0.0 collective-permute-done.4.t3
  55.8 1.1 %copy-done.1 = bf16[1024,384]{1,0:T(8,128)(2,1)S(1)} copy-done((bf16[1024,384]{1,0:T(8,128)(2,1)S(1)}, bf16[1024,384]{1,0:T(8,128)(2,1)}, u32[]{:S(2)}) %copy-start.1) | copy-done | bytes 786456
  57.0 1.1 %arrange_t.1 = (bf16[1024,768]{1,0:T(8,128)(2,1)S(1)}, bf16[1024,768]{1,0:T(8,128)(2,1)S(1)}) custom-call(bf16[1024,384]{1,0:T(8,128)(2,1)S(1)} %copy-done.1, bf16[1024,384]{1,0:T(8,128)(2,1)S(1)} %collective-permute-done.t1, bf16[1024,384]{1,0:T(8,128)(2,1)S(1)} %collective-permute-done.1.t2, bf16[1024,384]{1,0:T(8,128)(2,1)S(1)} %collective-permute-done.4.t3), custom_call_target="tpu_custom_call" | custom-call | bytes 6291456 | tf_op jit(solution)/shard_map/arrange_t/pallas_call | solution.py:203
  58.1 0.0 collective-permute-done.10.rest_6_
  58.1 1.6 %collective-permute-start.12 = (bf16[16,2,48,128]{3,2,1,0:T(8,128)(2,1)S(1)}, bf16[16,2,48,128]{3,2,1,0:T(8,128)(2,1)S(1)}, u32[]{:S(2)}, u32[]{:S(2)}) collective-permute-start(bf16[16,2,48,128]{3,2,1,0:T(8,128)(2,1)S(1)} %collective-permute-done.11.rest_5_), channel_id=1, source_target_pairs={{0,4},{4,0},{1,5},{5,1},{2,6},{6,2},{3,7},{7,3},{8,12},{12,8},{9,1... | collective-permute-start | bytes 1179656 | tf_op jit(solution)/shard_map/p1r_swap/ppermute | solution.py:51
  59.7 1.4 %collective-permute-start.16 = (bf16[16,2,48,128]{3,2,1,0:T(8,128)(2,1)S(1)}, bf16[16,2,48,128]{3,2,1,0:T(8,128)(2,1)S(1)}, u32[]{:S(2)}, u32[]{:S(2)}) collective-permute-start(bf16[16,2,48,128]{3,2,1,0:T(8,128)(2,1)S(1)} %collective-permute-done.11.rest_5_), channel_id=1, source_target_pairs={{0,8},{4,28},{8,16},{12,4},{16,24},{20,12},{24,0},{28,20},{1,9},{5... | collective-permute-start | bytes 1179656 | tf_op jit(solution)/shard_map/q1r/ppermute | solution.py:41
  61.1 1.3 %collective-permute-start.15 = (bf16[16,2,48,128]{3,2,1,0:T(8,128)(2,1)S(1)}, bf16[16,2,48,128]{3,2,1,0:T(8,128)(2,1)S(1)}, u32[]{:S(2)}, u32[]{:S(2)}) collective-permute-start(bf16[16,2,48,128]{3,2,1,0:T(8,128)(2,1)S(1)} %collective-permute-done.13.rest_3_), channel_id=1, source_target_pairs={{0,32},{4,228},{32,64},{36,4},{64,96},{68,36},{96,128},{100,68},{1... | collective-permute-start | bytes 1179656 | tf_op jit(solution)/shard_map/q1a/ppermute | solution.py:36
  62.4 0.0 collective-permute-done.9.rest_0_
  62.4 0.6 collective-permute-start.17
  63.0 3.2 %ladder_early.2.acc0 = f32[1024,1024]{1,0:T(8,128)S(1)} custom-call(s32[8,16]{1,0:T(8,128)S(1)} %copy-done.2, bf16[1024,768]{1,0:T(8,128)(2,1)S(1)} %get-tuple-element.41.t_ref, bf16[1024,2048]{1,0:T(8,128)(2,1)S(1)} %copy-done, bf16[16,2,48,128]{3,2,1,0:T(8,128)(2,1)S(1)} %get-tuple-element.38.rest_0_, ...), custom_call_target="tpu_custom_call" | custom-call | flops 1610612736 | bytes 9437184 | tf_op jit(solution)/shard_map/ladder_early/pallas_call | solution.py:243
  66.2 3.2 %ladder_early.3.acc1 = f32[1024,1024]{1,0:T(8,128)S(1)} custom-call(s32[8,16]{1,0:T(8,128)S(1)} %copy-done.2, bf16[1024,768]{1,0:T(8,128)(2,1)S(1)} %get-tuple-element.41.t_ref, bf16[1024,2048]{1,0:T(8,128)(2,1)S(1)} %copy-done, bf16[16,2,48,128]{3,2,1,0:T(8,128)(2,1)S(1)} %get-tuple-element.38.rest_0_, ...), custom_call_target="tpu_custom_call" | custom-call | flops 1610612736 | bytes 9437184 | tf_op jit(solution)/shard_map/ladder_early/pallas_call | solution.py:243
  69.4 0.0 collective-permute-done.16.rest_5_
  69.4 0.0 collective-permute-done.15.rest_1_
  69.4 1.2 %collective-permute-start.18 = (bf16[16,2,48,128]{3,2,1,0:T(8,128)(2,1)S(1)}, bf16[16,2,48,128]{3,2,1,0:T(8,128)(2,1)S(1)}, u32[]{:S(2)}, u32[]{:S(2)}) collective-permute-start(bf16[16,2,48,128]{3,2,1,0:T(8,128)(2,1)S(1)} %collective-permute-done.15.rest_1_), channel_id=1, source_target_pairs={{0,4},{4,0},{1,5},{5,1},{2,6},{6,2},{3,7},{7,3},{8,12},{12,8},{9,1... | collective-permute-start | bytes 1179656 | tf_op jit(solution)/shard_map/q1a_swap/ppermute | solution.py:51
  70.7 0.1 collective-permute-start.19
  70.8 0.4 collective-permute-start.20
  71.2 0.8 %collective-permute-done.18.rest_6_ = bf16[16,2,48,128]{3,2,1,0:T(8,128)(2,1)S(1)} collective-permute-done((bf16[16,2,48,128]{3,2,1,0:T(8,128)(2,1)S(1)}, bf16[16,2,48,128]{3,2,1,0:T(8,128)(2,1)S(1)}, u32[]{:S(2)}, u32[]{:S(2)}) %collective-permute-start.18) | collective-permute-done | bytes 393248 | tf_op jit(solution)/shard_map/q1a_swap/ppermute | solution.py:51
  72.0 0.6 collective-permute-done.19.rest_2_
  72.6 0.6 collective-permute-done.20.rest_4_
  73.1 0.4 collective-permute-start.21
  73.5 1.3 %collective-permute-done.21.rest_7_ = bf16[16,2,48,128]{3,2,1,0:T(8,128)(2,1)S(1)} collective-permute-done((bf16[16,2,48,128]{3,2,1,0:T(8,128)(2,1)S(1)}, bf16[16,2,48,128]{3,2,1,0:T(8,128)(2,1)S(1)}, u32[]{:S(2)}, u32[]{:S(2)}) %collective-permute-start.21) | collective-permute-done | bytes 393248 | tf_op jit(solution)/shard_map/q2_swap/ppermute | solution.py:51
  74.9 5.6 %ladder_late.1 = bf16[1024,2048]{1,0:T(8,128)(2,1)} custom-call(s32[8,16]{1,0:T(8,128)S(1)} %copy-done.2, bf16[1024,768]{1,0:T(8,128)(2,1)S(1)} %get-tuple-element.34.t_ref, f32[1024,1024]{1,0:T(8,128)S(1)} %ladder_early.2.acc0, f32[1024,1024]{1,0:T(8,128)S(1)} %ladder_early.3.acc1, bf16[16,2,48,128]{3,2,1,0:T(8,128)(2,1)S(1)} %collective-permute-done.9.rest_0_, ...), custom_call_target="tpu_custom_call" | custom-call | flops 3221225472 | bytes 17301504 | tf_op jit(solution)/shard_map/ladder_late/pallas_call | solution.py:287
  (14 shorter events, 0.0 us)
Async XLA Ops:
  0.0 63.0 %copy-start.2 = (s32[8,16]{1,0:T(8,128)S(1)}, s32[8,16]{1,0:T(8,128)}, u32[]{:S(2)}) copy-start(s32[8,16]{1,0:T(8,128)} %mask_ref.5) | copy-start | bytes 1540
  3.2 25.9 %all-to-all-start = ((bf16[32,48,128]{2,1,0:T(8,128)(2,1)}), bf16[32,48,128]{2,1,0:T(8,128)(2,1)S(1)}, u32[]{:S(2)}, u32[]{:S(2)}) async-start(bf16[32,48,128]{2,1,0:T(8,128)(2,1)} %get-tuple-element.30), calls=%async_computation | async-start | bytes 786432 | tf_op jit(solution)/shard_map/all_to_all | solution.py:305
  15.3 21.5 %collective-permute-start.1 = (bf16[1024,384]{1,0:T(8,128)(2,1)}, bf16[1024,384]{1,0:T(8,128)(2,1)S(1)}, u32[]{:S(2)}, u32[]{:S(2)}) collective-permute-start(bf16[1024,384]{1,0:T(8,128)(2,1)} %get-tuple-element.29.t0), channel_id=1, source_target_pairs={{0,3},{1,0},{2,1},{3,2},{4,5},{5,6},{6,7},{7,4},{8,11},{9,8},{10,9... | collective-permute-start | bytes 2359304 | tf_op jit(solution)/shard_map/t_back/ppermute | solution.py:46
  16.6 20.2 %collective-permute-start = (bf16[1024,384]{1,0:T(8,128)(2,1)}, bf16[1024,384]{1,0:T(8,128)(2,1)S(1)}, u32[]{:S(2)}, u32[]{:S(2)}) collective-permute-start(bf16[1024,384]{1,0:T(8,128)(2,1)} %get-tuple-element.29.t0), channel_id=1, source_target_pairs={{0,1},{1,2},{2,3},{3,0},{4,7},{5,4},{6,5},{7,6},{8,9},{9,10},{10,1... | collective-permute-start | bytes 2359304 | tf_op jit(solution)/shard_map/t_near/ppermute | solution.py:46
  29.1 3.8 %collective-permute-start.2 = (bf16[32,48,128]{2,1,0:T(8,128)(2,1)S(1)}, bf16[32,48,128]{2,1,0:T(8,128)(2,1)S(1)}, u32[]{:S(2)}, u32[]{:S(2)}) collective-permute-start(bf16[32,48,128]{2,1,0:T(8,128)(2,1)S(1)} %all-to-all-done.a_ref), channel_id=1, source_target_pairs={{0,4},{4,0},{1,5},{5,1},{2,6},{6,2},{3,7},{7,3},{8,12},{12,8},{9,1... | collective-permute-start | bytes 1179656 | tf_op jit(solution)/shard_map/v_swap/ppermute | solution.py:51
  31.6 31.4 %copy-start = (bf16[1024,2048]{1,0:T(8,128)(2,1)S(1)}, bf16[1024,2048]{1,0:T(8,128)(2,1)}, u32[]{:S(2)}) copy-start(bf16[1024,2048]{1,0:T(8,128)(2,1)} %r_ref.3) | copy-start | bytes 12582916
  33.7 7.3 %collective-permute-start.3 = (bf16[16,48,128]{2,1,0:T(8,128)(2,1)S(1)}, bf16[16,48,128]{2,1,0:T(8,128)(2,1)S(1)}, u32[]{:S(2)}, u32[]{:S(2)}) collective-permute-start(bf16[16,48,128]{2,1,0:T(8,128)(2,1)S(1)} %get-tuple-element.31), channel_id=1, source_target_pairs={{0,1},{1,2},{2,3},{3,0},{4,7},{5,4},{6,5},{7,6},{8,9},{9,10},{10,1... | collective-permute-start | bytes 589832 | tf_op jit(solution)/shard_map/r_near/ppermute | solution.py:46
  36.3 6.0 %collective-permute-start.6 = (bf16[8,48,128]{2,1,0:T(8,128)(2,1)S(1)}, bf16[8,48,128]{2,1,0:T(8,128)(2,1)S(1)}, u32[]{:S(2)}, u32[]{:S(2)}) collective-permute-start(bf16[8,48,128]{2,1,0:T(8,128)(2,1)S(1)} %get-tuple-element.37), channel_id=1, source_target_pairs={{0,2},{1,3},{2,0},{3,1},{4,6},{5,7},{6,4},{7,5},{8,10},{9,11},{10,... | collective-permute-start | bytes 294920 | tf_op jit(solution)/shard_map/r_far/ppermute | solution.py:311
  41.0 4.1 %collective-permute-start.5 = (bf16[16,48,128]{2,1,0:T(8,128)(2,1)S(1)}, bf16[16,48,128]{2,1,0:T(8,128)(2,1)S(1)}, u32[]{:S(2)}, u32[]{:S(2)}) collective-permute-start(bf16[16,48,128]{2,1,0:T(8,128)(2,1)S(1)} %collective-permute-done.3.r1_ref), channel_id=1, source_target_pairs={{0,4},{4,0},{1,5},{5,1},{2,6},{6,2},{3,7},{7,3},{8,12},{12,8},{9,1... | collective-permute-start | bytes 589832 | tf_op jit(solution)/shard_map/r_near_swap/ppermute | solution.py:51
  42.3 2.8 %collective-permute-start.7 = (bf16[8,48,128]{2,1,0:T(8,128)(2,1)S(1)}, bf16[8,48,128]{2,1,0:T(8,128)(2,1)S(1)}, u32[]{:S(2)}, u32[]{:S(2)}) collective-permute-start(bf16[8,48,128]{2,1,0:T(8,128)(2,1)S(1)} %collective-permute-done.6.r2_ref), channel_id=1, source_target_pairs={{0,4},{4,0},{1,5},{5,1},{2,6},{6,2},{3,7},{7,3},{8,12},{12,8},{9,1... | collective-permute-start | bytes 294920 | tf_op jit(solution)/shard_map/r_far_swap/ppermute | solution.py:51
  44.1 11.7 %collective-permute-start.4 = (bf16[1024,384]{1,0:T(8,128)(2,1)S(1)}, bf16[1024,384]{1,0:T(8,128)(2,1)S(1)}, u32[]{:S(2)}, u32[]{:S(2)}) collective-permute-start(bf16[1024,384]{1,0:T(8,128)(2,1)S(1)} %collective-permute-done.t1), channel_id=1, source_target_pairs={{0,1},{1,2},{2,3},{3,0},{4,7},{5,4},{6,5},{7,6},{8,9},{9,10},{10,1... | collective-permute-start | bytes 2359304 | tf_op jit(solution)/shard_map/t_far/ppermute | solution.py:46
  45.2 7.0 %collective-permute-start.8 = (bf16[16,2,48,128]{3,2,1,0:T(8,128)(2,1)S(1)}, bf16[16,2,48,128]{3,2,1,0:T(8,128)(2,1)S(1)}, u32[]{:S(2)}, u32[]{:S(2)}) collective-permute-start(bf16[16,2,48,128]{3,2,1,0:T(8,128)(2,1)S(1)} %get-tuple-element.38.rest_0_), channel_id=1, source_target_pairs={{0,32},{4,228},{32,64},{36,4},{64,96},{68,36},{96,128},{100,68},{1... | collective-permute-start | bytes 1179656 | tf_op jit(solution)/shard_map/p1a/ppermute | solution.py:36
  46.2 8.5 %collective-permute-start.13 = (bf16[16,2,48,128]{3,2,1,0:T(8,128)(2,1)S(1)}, bf16[16,2,48,128]{3,2,1,0:T(8,128)(2,1)S(1)}, u32[]{:S(2)}, u32[]{:S(2)}) collective-permute-start(bf16[16,2,48,128]{3,2,1,0:T(8,128)(2,1)S(1)} %get-tuple-element.38.rest_0_), channel_id=1, source_target_pairs={{0,8},{4,28},{8,16},{12,4},{16,24},{20,12},{24,0},{28,20},{1,9},{5... | collective-permute-start | bytes 1179656 | tf_op jit(solution)/shard_map/q0/ppermute | solution.py:41
  48.6 9.4 %collective-permute-start.11 = (bf16[16,2,48,128]{3,2,1,0:T(8,128)(2,1)S(1)}, bf16[16,2,48,128]{3,2,1,0:T(8,128)(2,1)S(1)}, u32[]{:S(2)}, u32[]{:S(2)}) collective-permute-start(bf16[16,2,48,128]{3,2,1,0:T(8,128)(2,1)S(1)} %get-tuple-element.39.rest_4_), channel_id=1, source_target_pairs={{0,32},{4,228},{32,64},{36,4},{64,96},{68,36},{96,128},{100,68},{1... | collective-permute-start | bytes 1179656 | tf_op jit(solution)/shard_map/p1r/ppermute | solution.py:36
  52.2 5.8 %collective-permute-start.10 = (bf16[16,2,48,128]{3,2,1,0:T(8,128)(2,1)S(1)}, bf16[16,2,48,128]{3,2,1,0:T(8,128)(2,1)S(1)}, u32[]{:S(2)}, u32[]{:S(2)}) collective-permute-start(bf16[16,2,48,128]{3,2,1,0:T(8,128)(2,1)S(1)} %collective-permute-done.8.rest_1_), channel_id=1, source_target_pairs={{0,4},{4,0},{1,5},{5,1},{2,6},{6,2},{3,7},{7,3},{8,12},{12,8},{9,1... | collective-permute-start | bytes 1179656 | tf_op jit(solution)/shard_map/p1a_swap/ppermute | solution.py:51
  54.7 7.7 %collective-permute-start.9 = (bf16[16,2,48,128]{3,2,1,0:T(8,128)(2,1)S(1)}, bf16[16,2,48,128]{3,2,1,0:T(8,128)(2,1)S(1)}, u32[]{:S(2)}, u32[]{:S(2)}) collective-permute-start(bf16[16,2,48,128]{3,2,1,0:T(8,128)(2,1)S(1)} %collective-permute-done.8.rest_1_), channel_id=1, source_target_pairs={{0,32},{4,228},{32,64},{36,4},{64,96},{68,36},{96,128},{100,68},{1... | collective-permute-start | bytes 1179656 | tf_op jit(solution)/shard_map/p2/ppermute | solution.py:36
  54.7 8.3 %collective-permute-start.14 = (bf16[16,2,48,128]{3,2,1,0:T(8,128)(2,1)S(1)}, bf16[16,2,48,128]{3,2,1,0:T(8,128)(2,1)S(1)}, u32[]{:S(2)}, u32[]{:S(2)}) collective-permute-start(bf16[16,2,48,128]{3,2,1,0:T(8,128)(2,1)S(1)} %collective-permute-done.13.rest_3_), channel_id=1, source_target_pairs={{0,4},{4,0},{1,5},{5,1},{2,6},{6,2},{3,7},{7,3},{8,12},{12,8},{9,1... | collective-permute-start | bytes 1179656 | tf_op jit(solution)/shard_map/q0_swap/ppermute | solution.py:51
  55.8 1.1 %copy-start.1 = (bf16[1024,384]{1,0:T(8,128)(2,1)S(1)}, bf16[1024,384]{1,0:T(8,128)(2,1)}, u32[]{:S(2)}) copy-start(bf16[1024,384]{1,0:T(8,128)(2,1)} %get-tuple-element.29.t0) | copy-start | bytes 2359300
  58.1 4.9 %collective-permute-start.12 = (bf16[16,2,48,128]{3,2,1,0:T(8,128)(2,1)S(1)}, bf16[16,2,48,128]{3,2,1,0:T(8,128)(2,1)S(1)}, u32[]{:S(2)}, u32[]{:S(2)}) collective-permute-start(bf16[16,2,48,128]{3,2,1,0:T(8,128)(2,1)S(1)} %collective-permute-done.11.rest_5_), channel_id=1, source_target_pairs={{0,4},{4,0},{1,5},{5,1},{2,6},{6,2},{3,7},{7,3},{8,12},{12,8},{9,1... | collective-permute-start | bytes 1179656 | tf_op jit(solution)/shard_map/p1r_swap/ppermute | solution.py:51
  59.7 9.7 %collective-permute-start.16 = (bf16[16,2,48,128]{3,2,1,0:T(8,128)(2,1)S(1)}, bf16[16,2,48,128]{3,2,1,0:T(8,128)(2,1)S(1)}, u32[]{:S(2)}, u32[]{:S(2)}) collective-permute-start(bf16[16,2,48,128]{3,2,1,0:T(8,128)(2,1)S(1)} %collective-permute-done.11.rest_5_), channel_id=1, source_target_pairs={{0,8},{4,28},{8,16},{12,4},{16,24},{20,12},{24,0},{28,20},{1,9},{5... | collective-permute-start | bytes 1179656 | tf_op jit(solution)/shard_map/q1r/ppermute | solution.py:41
  61.1 8.4 %collective-permute-start.15 = (bf16[16,2,48,128]{3,2,1,0:T(8,128)(2,1)S(1)}, bf16[16,2,48,128]{3,2,1,0:T(8,128)(2,1)S(1)}, u32[]{:S(2)}, u32[]{:S(2)}) collective-permute-start(bf16[16,2,48,128]{3,2,1,0:T(8,128)(2,1)S(1)} %collective-permute-done.13.rest_3_), channel_id=1, source_target_pairs={{0,32},{4,228},{32,64},{36,4},{64,96},{68,36},{96,128},{100,68},{1... | collective-permute-start | bytes 1179656 | tf_op jit(solution)/shard_map/q1a/ppermute | solution.py:36
  62.4 8.8 %collective-permute-start.17 = (bf16[16,2,48,128]{3,2,1,0:T(8,128)(2,1)S(1)}, bf16[16,2,48,128]{3,2,1,0:T(8,128)(2,1)S(1)}, u32[]{:S(2)}, u32[]{:S(2)}) collective-permute-start(bf16[16,2,48,128]{3,2,1,0:T(8,128)(2,1)S(1)} %collective-permute-done.9.rest_0_), channel_id=1, source_target_pairs={{0,8},{4,28},{8,16},{12,4},{16,24},{20,12},{24,0},{28,20},{1,9},{5... | collective-permute-start | bytes 1179656 | tf_op jit(solution)/shard_map/q2/ppermute | solution.py:41
  69.4 2.6 %collective-permute-start.18 = (bf16[16,2,48,128]{3,2,1,0:T(8,128)(2,1)S(1)}, bf16[16,2,48,128]{3,2,1,0:T(8,128)(2,1)S(1)}, u32[]{:S(2)}, u32[]{:S(2)}) collective-permute-start(bf16[16,2,48,128]{3,2,1,0:T(8,128)(2,1)S(1)} %collective-permute-done.15.rest_1_), channel_id=1, source_target_pairs={{0,4},{4,0},{1,5},{5,1},{2,6},{6,2},{3,7},{7,3},{8,12},{12,8},{9,1... | collective-permute-start | bytes 1179656 | tf_op jit(solution)/shard_map/q1a_swap/ppermute | solution.py:51
  70.7 1.9 %collective-permute-start.19 = (bf16[16,2,48,128]{3,2,1,0:T(8,128)(2,1)S(1)}, bf16[16,2,48,128]{3,2,1,0:T(8,128)(2,1)S(1)}, u32[]{:S(2)}, u32[]{:S(2)}) collective-permute-start(bf16[16,2,48,128]{3,2,1,0:T(8,128)(2,1)S(1)} %collective-permute-done.16.rest_5_), channel_id=1, source_target_pairs={{0,4},{4,0},{1,5},{5,1},{2,6},{6,2},{3,7},{7,3},{8,12},{12,8},{9,1... | collective-permute-start | bytes 1179656 | tf_op jit(solution)/shard_map/q1r_swap/ppermute | solution.py:51
  70.8 2.4 %collective-permute-start.20 = (bf16[16,2,48,128]{3,2,1,0:T(8,128)(2,1)S(1)}, bf16[16,2,48,128]{3,2,1,0:T(8,128)(2,1)S(1)}, u32[]{:S(2)}, u32[]{:S(2)}) collective-permute-start(bf16[16,2,48,128]{3,2,1,0:T(8,128)(2,1)S(1)} %collective-permute-done.9.rest_0_), channel_id=1, source_target_pairs={{0,4},{4,0},{1,5},{5,1},{2,6},{6,2},{3,7},{7,3},{8,12},{12,8},{9,1... | collective-permute-start | bytes 1179656 | tf_op jit(solution)/shard_map/p2_swap/ppermute | solution.py:51
  73.1 1.7 %collective-permute-start.21 = (bf16[16,2,48,128]{3,2,1,0:T(8,128)(2,1)S(1)}, bf16[16,2,48,128]{3,2,1,0:T(8,128)(2,1)S(1)}, u32[]{:S(2)}, u32[]{:S(2)}) collective-permute-start(bf16[16,2,48,128]{3,2,1,0:T(8,128)(2,1)S(1)} %collective-permute-done.17.rest_3_), channel_id=1, source_target_pairs={{0,4},{4,0},{1,5},{5,1},{2,6},{6,2},{3,7},{7,3},{8,12},{12,8},{9,1... | collective-permute-start | bytes 1179656 | tf_op jit(solution)/shard_map/q2_swap/ppermute | solution.py:51

commit v5 on v4

--- a/solution.py
+++ b/solution.py
@@ -63,8 +63,10 @@
     return pl.BlockSpec(memory_space=pltpu.VMEM)
 
 
-def prepare_kernel(t_mask_ref, v_mask_ref, t_ref, v_ref, t_out, v_out, perm):
+def prepare_kernel(t_mask_ref, v_mask_ref, t_hbm, v_ref, t_out, v_out, perm, t_ref, sem):
     rows, cols = t_ref.shape
+    fetch = pltpu.make_async_copy(t_hbm, t_ref, sem)
+    fetch.start()
     z, y, c = (lax.axis_index(n) for n in ("z", "y", "c"))
     s = 1 - 2 * c
     for g in range(8):
@@ -85,6 +87,7 @@
         g = lax.rem(z + dz + NZ, 4) * 2 + lax.rem(y + dy, 2)
         shift = jnp.where(lane >= q * CHUNK, (g - q) * CHUNK, shift)
     perm[...] = jnp.where(source == target + shift, 1.0, 0.0).astype(perm.dtype)
+    fetch.wait()
 
     @pl.loop(0, rows // ROWS)
     def _(i):
@@ -107,9 +110,9 @@
             jax.ShapeDtypeStruct(t.shape, t.dtype),
             jax.ShapeDtypeStruct((NZ * NY, CHUNK, TILE), v.dtype),
         ),
-        in_specs=[in_smem()] * 2 + [in_vmem()] * 2,
+        in_specs=[in_smem()] * 2 + [pl.BlockSpec(memory_space=pl.ANY), in_vmem()],
         out_specs=(in_vmem(), in_vmem()),
-        scratch_shapes=[pltpu.VMEM((t.shape[1], t.shape[1]), t.dtype)],
+        scratch_shapes=[pltpu.VMEM((t.shape[1], t.shape[1]), t.dtype), pltpu.VMEM(t.shape, t.dtype), pltpu.SemaphoreType.DMA],
         compiler_params=pltpu.CompilerParams(vmem_limit_bytes=WHOLE),
         cost_estimate=cost(2 * t.size * t.shape[1], 4 * t.size + 12 * v.size),
         name="prepare",

time: 80.8 us -> 81.7 us (1.011)
  no operation moved by 1% of the time
where the time goes in v5:
time: 81.7 us; the launch traced here: 81.4 us
  starting transfers between devices  38.1 us (47%)
  waiting for transfers between devices  22.9 us (28%)
  Pallas kernels  18 us (22%)
  local copies, waits for them, and re-layouts  1.14 us (1%)
  other arithmetic  1 us (1%)
    all_to_all x1, starting transfers between devices, body(): mine = lax.all_to_all(spread, ('z', 'y'), 0, 0)  12 us
    ppermute x10, starting transfers between devices, swap(): return lax.ppermute(v, 'c', [(0, 1), (1, 0)])  11.9 us
    all_to_all x1, waiting for transfers between devices, body(): mine = lax.all_to_all(spread, ('z', 'y'), 0, 0)  11.1 us
    pallas_call x2, Pallas kernels, early(): pl.pallas_call(functools.partial(early_kernel, first), out_shape=jax.Shap...  6.39 us
    ppermute x4, starting transfers between devices, move_x(): return lax.ppermute(v, ('c', 'x'), pairs_cx(d))  5.8 us
    pallas_call x1, Pallas kernels, late(): pl.pallas_call(late_kernel, out_shape=jax.ShapeDtypeStruct((rows, width),...  5.56 us
    ppermute x3, starting transfers between devices, move_y(): return lax.ppermute(v, ('y', 'c'), pairs_yc(1))  4.4 us
    ppermute x4, waiting for transfers between devices, move_x(): return lax.ppermute(v, ('c', 'x'), pairs_cx(d))  4.21 us
  transfers between devices with their start and end apart: 23, of which 10 were waited for; matrix products, arithmetic and copies ran while one was open for 1% of the time, Pallas kernels for 10%

profile of v5, /device:TPU:1, one launch (start us, length us, event | category | flops | bytes accessed | tf_op | source)
XLA Modules:
  0.0 81.4 jit_solution(2478192732556768266)
XLA Ops:
  0.0 4.0 %prepare.1 = (bf16[1024,384]{1,0:T(8,128)(2,1)}, bf16[32,48,128]{2,1,0:T(8,128)(2,1)}) custom-call(s32[3,8]{1,0:T(4,128)} %bitcast.2, s32[1,3]{1,0:T(1,128)} %bitcast.3, bf16[1024,384]{1,0:T(8,128)(2,1)} %t_hbm.1, bf16[384,128]{1,0:T(8,128)(2,1)} %v_ref.1), custom_call_target="tpu_custom_call" | custom-call | flops 301989888 | bytes 2162688 | tf_op jit(solution)/shard_map/prepare/pallas_call | solution.py:107
  4.0 12.0 %all-to-all-start = ((bf16[32,48,128]{2,1,0:T(8,128)(2,1)}), bf16[32,48,128]{2,1,0:T(8,128)(2,1)S(1)}, u32[]{:S(2)}, u32[]{:S(2)}) async-start(bf16[32,48,128]{2,1,0:T(8,128)(2,1)} %get-tuple-element.30), calls=%async_computation | async-start | bytes 786432 | tf_op jit(solution)/shard_map/all_to_all | solution.py:308
  16.1 1.3 %collective-permute-start.1 = (bf16[1024,384]{1,0:T(8,128)(2,1)}, bf16[1024,384]{1,0:T(8,128)(2,1)S(1)}, u32[]{:S(2)}, u32[]{:S(2)}) collective-permute-start(bf16[1024,384]{1,0:T(8,128)(2,1)} %get-tuple-element.29.t0), channel_id=1, source_target_pairs={{0,3},{1,0},{2,1},{3,2},{4,5},{5,6},{6,7},{7,4},{8,11},{9,8},{10,9... | collective-permute-start | bytes 2359304 | tf_op jit(solution)/shard_map/t_back/ppermute | solution.py:46
  17.4 1.5 %collective-permute-start = (bf16[1024,384]{1,0:T(8,128)(2,1)}, bf16[1024,384]{1,0:T(8,128)(2,1)S(1)}, u32[]{:S(2)}, u32[]{:S(2)}) collective-permute-start(bf16[1024,384]{1,0:T(8,128)(2,1)} %get-tuple-element.29.t0), channel_id=1, source_target_pairs={{0,1},{1,2},{2,3},{3,0},{4,7},{5,4},{6,5},{7,6},{8,9},{9,10},{10,1... | collective-permute-start | bytes 2359304 | tf_op jit(solution)/shard_map/t_near/ppermute | solution.py:46
  18.8 11.1 %all-to-all-done.a_ref = bf16[32,48,128]{2,1,0:T(8,128)(2,1)S(1)} async-done(((bf16[32,48,128]{2,1,0:T(8,128)(2,1)}), bf16[32,48,128]{2,1,0:T(8,128)(2,1)S(1)}, u32[]{:S(2)}, u32[]{:S(2)}) %all-to-all-start) | async-done | bytes 393248 | tf_op jit(solution)/shard_map/all_to_all | solution.py:308
  29.9 2.5 %collective-permute-start.2 = (bf16[32,48,128]{2,1,0:T(8,128)(2,1)S(1)}, bf16[32,48,128]{2,1,0:T(8,128)(2,1)S(1)}, u32[]{:S(2)}, u32[]{:S(2)}) collective-permute-start(bf16[32,48,128]{2,1,0:T(8,128)(2,1)S(1)} %all-to-all-done.a_ref), channel_id=1, source_target_pairs={{0,4},{4,0},{1,5},{5,1},{2,6},{6,2},{3,7},{7,3},{8,12},{12,8},{9,1... | collective-permute-start | bytes 1179656 | tf_op jit(solution)/shard_map/v_swap/ppermute | solution.py:51
  32.4 1.0 %select_reduce_fusion.pick_ref = s32[40]{0:T(128)S(1)} fusion(s32[64]{0:T(128)S(1)} %fusion, s32[64]{0:T(128)} %param.11, s32[40]{0:T(128)S(1)} %compare_select_fusion.2), kind=kLoop, calls=%fused_computation | loop fusion | flops 7640 | bytes 832 | tf_op jit(solution)/shard_map/reduce_sum | solution.py:153
  33.4 0.3 collective-permute-done.2.b_ref
  33.7 0.8 select_columns.1
  34.5 2.6 %collective-permute-start.3 = (bf16[16,48,128]{2,1,0:T(8,128)(2,1)S(1)}, bf16[16,48,128]{2,1,0:T(8,128)(2,1)S(1)}, u32[]{:S(2)}, u32[]{:S(2)}) collective-permute-start(bf16[16,48,128]{2,1,0:T(8,128)(2,1)S(1)} %get-tuple-element.31), channel_id=1, source_target_pairs={{0,1},{1,2},{2,3},{3,0},{4,7},{5,4},{6,5},{7,6},{8,9},{9,10},{10,1... | collective-permute-start | bytes 589832 | tf_op jit(solution)/shard_map/r_near/ppermute | solution.py:46
  37.1 0.5 collective-permute-start.6
  37.6 0.0 collective-permute-done.1.t2
  37.6 0.0 collective-permute-done.t1
  37.6 4.2 %collective-permute-done.3.r1_ref = bf16[16,48,128]{2,1,0:T(8,128)(2,1)S(1)} collective-permute-done((bf16[16,48,128]{2,1,0:T(8,128)(2,1)S(1)}, bf16[16,48,128]{2,1,0:T(8,128)(2,1)S(1)}, u32[]{:S(2)}, u32[]{:S(2)}) %collective-permute-start.3) | collective-permute-done | bytes 196640 | tf_op jit(solution)/shard_map/r_near/ppermute | solution.py:46
  41.8 0.2 collective-permute-start.5
  42.0 1.1 %collective-permute-done.6.r2_ref = bf16[8,48,128]{2,1,0:T(8,128)(2,1)S(1)} collective-permute-done((bf16[8,48,128]{2,1,0:T(8,128)(2,1)S(1)}, bf16[8,48,128]{2,1,0:T(8,128)(2,1)S(1)}, u32[]{:S(2)}, u32[]{:S(2)}) %collective-permute-start.6) | collective-permute-done | bytes 98336 | tf_op jit(solution)/shard_map/r_far/ppermute | solution.py:314
  43.1 1.9 %collective-permute-start.7 = (bf16[8,48,128]{2,1,0:T(8,128)(2,1)S(1)}, bf16[8,48,128]{2,1,0:T(8,128)(2,1)S(1)}, u32[]{:S(2)}, u32[]{:S(2)}) collective-permute-start(bf16[8,48,128]{2,1,0:T(8,128)(2,1)S(1)} %collective-permute-done.6.r2_ref), channel_id=1, source_target_pairs={{0,4},{4,0},{1,5},{5,1},{2,6},{6,2},{3,7},{7,3},{8,12},{12,8},{9,1... | collective-permute-start | bytes 294920 | tf_op jit(solution)/shard_map/r_far_swap/ppermute | solution.py:51
  44.9 0.5 collective-permute-start.4
  45.4 0.5 collective-permute-done.7.w2_ref
  45.9 0.2 pack_shard.1
  46.0 1.0 %collective-permute-start.8 = (bf16[16,2,48,128]{3,2,1,0:T(8,128)(2,1)S(1)}, bf16[16,2,48,128]{3,2,1,0:T(8,128)(2,1)S(1)}, u32[]{:S(2)}, u32[]{:S(2)}) collective-permute-start(bf16[16,2,48,128]{3,2,1,0:T(8,128)(2,1)S(1)} %get-tuple-element.38.rest_0_), channel_id=1, source_target_pairs={{0,32},{4,228},{32,64},{36,4},{64,96},{68,36},{96,128},{100,68},{1... | collective-permute-start | bytes 1179656 | tf_op jit(solution)/shard_map/p1a/ppermute | solution.py:36
  47.0 2.4 %collective-permute-start.13 = (bf16[16,2,48,128]{3,2,1,0:T(8,128)(2,1)S(1)}, bf16[16,2,48,128]{3,2,1,0:T(8,128)(2,1)S(1)}, u32[]{:S(2)}, u32[]{:S(2)}) collective-permute-start(bf16[16,2,48,128]{3,2,1,0:T(8,128)(2,1)S(1)} %get-tuple-element.38.rest_0_), channel_id=1, source_target_pairs={{0,8},{4,28},{8,16},{12,4},{16,24},{20,12},{24,0},{28,20},{1,9},{5... | collective-permute-start | bytes 1179656 | tf_op jit(solution)/shard_map/q0/ppermute | solution.py:41
  49.4 1.2 %collective-permute-start.11 = (bf16[16,2,48,128]{3,2,1,0:T(8,128)(2,1)S(1)}, bf16[16,2,48,128]{3,2,1,0:T(8,128)(2,1)S(1)}, u32[]{:S(2)}, u32[]{:S(2)}) collective-permute-start(bf16[16,2,48,128]{3,2,1,0:T(8,128)(2,1)S(1)} %get-tuple-element.39.rest_4_), channel_id=1, source_target_pairs={{0,32},{4,228},{32,64},{36,4},{64,96},{68,36},{96,128},{100,68},{1... | collective-permute-start | bytes 1179656 | tf_op jit(solution)/shard_map/p1r/ppermute | solution.py:36
  50.6 2.5 %collective-permute-done.8.rest_1_ = bf16[16,2,48,128]{3,2,1,0:T(8,128)(2,1)S(1)} collective-permute-done((bf16[16,2,48,128]{3,2,1,0:T(8,128)(2,1)S(1)}, bf16[16,2,48,128]{3,2,1,0:T(8,128)(2,1)S(1)}, u32[]{:S(2)}, u32[]{:S(2)}) %collective-permute-start.8) | collective-permute-done | bytes 393248 | tf_op jit(solution)/shard_map/p1a/ppermute | solution.py:36
  53.1 2.4 %collective-permute-start.10 = (bf16[16,2,48,128]{3,2,1,0:T(8,128)(2,1)S(1)}, bf16[16,2,48,128]{3,2,1,0:T(8,128)(2,1)S(1)}, u32[]{:S(2)}, u32[]{:S(2)}) collective-permute-start(bf16[16,2,48,128]{3,2,1,0:T(8,128)(2,1)S(1)} %collective-permute-done.8.rest_1_), channel_id=1, source_target_pairs={{0,4},{4,0},{1,5},{5,1},{2,6},{6,2},{3,7},{7,3},{8,12},{12,8},{9,1... | collective-permute-start | bytes 1179656 | tf_op jit(solution)/shard_map/p1a_swap/ppermute | solution.py:51
  55.5 1.1 %collective-permute-start.14 = (bf16[16,2,48,128]{3,2,1,0:T(8,128)(2,1)S(1)}, bf16[16,2,48,128]{3,2,1,0:T(8,128)(2,1)S(1)}, u32[]{:S(2)}, u32[]{:S(2)}) collective-permute-start(bf16[16,2,48,128]{3,2,1,0:T(8,128)(2,1)S(1)} %collective-permute-done.13.rest_3_), channel_id=1, source_target_pairs={{0,4},{4,0},{1,5},{5,1},{2,6},{6,2},{3,7},{7,3},{8,12},{12,8},{9,1... | collective-permute-start | bytes 1179656 | tf_op jit(solution)/shard_map/q0_swap/ppermute | solution.py:51
  56.6 0.0 collective-permute-done.4.t3
  56.6 1.1 %copy-done.1 = bf16[1024,384]{1,0:T(8,128)(2,1)S(1)} copy-done((bf16[1024,384]{1,0:T(8,128)(2,1)S(1)}, bf16[1024,384]{1,0:T(8,128)(2,1)}, u32[]{:S(2)}) %copy-start.1) | copy-done | bytes 786456
  57.8 1.1 %arrange_t.1 = (bf16[1024,768]{1,0:T(8,128)(2,1)S(1)}, bf16[1024,768]{1,0:T(8,128)(2,1)S(1)}) custom-call(bf16[1024,384]{1,0:T(8,128)(2,1)S(1)} %copy-done.1, bf16[1024,384]{1,0:T(8,128)(2,1)S(1)} %collective-permute-done.t1, bf16[1024,384]{1,0:T(8,128)(2,1)S(1)} %collective-permute-done.1.t2, bf16[1024,384]{1,0:T(8,128)(2,1)S(1)} %collective-permute-done.4.t3), custom_call_target="tpu_custom_call" | custom-call | bytes 6291456 | tf_op jit(solution)/shard_map/arrange_t/pallas_call | solution.py:206
  58.9 0.0 collective-permute-done.11.rest_5_
  58.9 0.0 collective-permute-done.10.rest_6_
  58.9 1.6 %collective-permute-start.12 = (bf16[16,2,48,128]{3,2,1,0:T(8,128)(2,1)S(1)}, bf16[16,2,48,128]{3,2,1,0:T(8,128)(2,1)S(1)}, u32[]{:S(2)}, u32[]{:S(2)}) collective-permute-start(bf16[16,2,48,128]{3,2,1,0:T(8,128)(2,1)S(1)} %collective-permute-done.11.rest_5_), channel_id=1, source_target_pairs={{0,4},{4,0},{1,5},{5,1},{2,6},{6,2},{3,7},{7,3},{8,12},{12,8},{9,1... | collective-permute-start | bytes 1179656 | tf_op jit(solution)/shard_map/p1r_swap/ppermute | solution.py:51
  60.5 1.4 %collective-permute-start.16 = (bf16[16,2,48,128]{3,2,1,0:T(8,128)(2,1)S(1)}, bf16[16,2,48,128]{3,2,1,0:T(8,128)(2,1)S(1)}, u32[]{:S(2)}, u32[]{:S(2)}) collective-permute-start(bf16[16,2,48,128]{3,2,1,0:T(8,128)(2,1)S(1)} %collective-permute-done.11.rest_5_), channel_id=1, source_target_pairs={{0,8},{4,28},{8,16},{12,4},{16,24},{20,12},{24,0},{28,20},{1,9},{5... | collective-permute-start | bytes 1179656 | tf_op jit(solution)/shard_map/q1r/ppermute | solution.py:41
  61.9 1.3 %collective-permute-start.15 = (bf16[16,2,48,128]{3,2,1,0:T(8,128)(2,1)S(1)}, bf16[16,2,48,128]{3,2,1,0:T(8,128)(2,1)S(1)}, u32[]{:S(2)}, u32[]{:S(2)}) collective-permute-start(bf16[16,2,48,128]{3,2,1,0:T(8,128)(2,1)S(1)} %collective-permute-done.13.rest_3_), channel_id=1, source_target_pairs={{0,32},{4,228},{32,64},{36,4},{64,96},{68,36},{96,128},{100,68},{1... | collective-permute-start | bytes 1179656 | tf_op jit(solution)/shard_map/q1a/ppermute | solution.py:36
  63.2 0.0 collective-permute-done.9.rest_0_
  63.2 0.6 collective-permute-start.17
  63.8 3.2 %ladder_early.2.acc0 = f32[1024,1024]{1,0:T(8,128)S(1)} custom-call(s32[8,16]{1,0:T(8,128)S(1)} %copy-done.2, bf16[1024,768]{1,0:T(8,128)(2,1)S(1)} %get-tuple-element.41.t_ref, bf16[1024,2048]{1,0:T(8,128)(2,1)S(1)} %copy-done, bf16[16,2,48,128]{3,2,1,0:T(8,128)(2,1)S(1)} %get-tuple-element.38.rest_0_, ...), custom_call_target="tpu_custom_call" | custom-call | flops 1610612736 | bytes 9437184 | tf_op jit(solution)/shard_map/ladder_early/pallas_call | solution.py:246
  67.0 3.2 %ladder_early.3.acc1 = f32[1024,1024]{1,0:T(8,128)S(1)} custom-call(s32[8,16]{1,0:T(8,128)S(1)} %copy-done.2, bf16[1024,768]{1,0:T(8,128)(2,1)S(1)} %get-tuple-element.41.t_ref, bf16[1024,2048]{1,0:T(8,128)(2,1)S(1)} %copy-done, bf16[16,2,48,128]{3,2,1,0:T(8,128)(2,1)S(1)} %get-tuple-element.38.rest_0_, ...), custom_call_target="tpu_custom_call" | custom-call | flops 1610612736 | bytes 9437184 | tf_op jit(solution)/shard_map/ladder_early/pallas_call | solution.py:246
  70.2 0.0 collective-permute-done.15.rest_1_
  70.2 1.2 %collective-permute-start.18 = (bf16[16,2,48,128]{3,2,1,0:T(8,128)(2,1)S(1)}, bf16[16,2,48,128]{3,2,1,0:T(8,128)(2,1)S(1)}, u32[]{:S(2)}, u32[]{:S(2)}) collective-permute-start(bf16[16,2,48,128]{3,2,1,0:T(8,128)(2,1)S(1)} %collective-permute-done.15.rest_1_), channel_id=1, source_target_pairs={{0,4},{4,0},{1,5},{5,1},{2,6},{6,2},{3,7},{7,3},{8,12},{12,8},{9,1... | collective-permute-start | bytes 1179656 | tf_op jit(solution)/shard_map/q1a_swap/ppermute | solution.py:51
  71.5 0.1 collective-permute-start.19
  71.6 0.4 collective-permute-start.20
  72.0 0.8 %collective-permute-done.18.rest_6_ = bf16[16,2,48,128]{3,2,1,0:T(8,128)(2,1)S(1)} collective-permute-done((bf16[16,2,48,128]{3,2,1,0:T(8,128)(2,1)S(1)}, bf16[16,2,48,128]{3,2,1,0:T(8,128)(2,1)S(1)}, u32[]{:S(2)}, u32[]{:S(2)}) %collective-permute-start.18) | collective-permute-done | bytes 393248 | tf_op jit(solution)/shard_map/q1a_swap/ppermute | solution.py:51
  72.8 0.6 collective-permute-done.19.rest_2_
  73.4 0.6 collective-permute-done.20.rest_4_
  73.9 0.4 collective-permute-start.21
  74.3 1.3 %collective-permute-done.21.rest_7_ = bf16[16,2,48,128]{3,2,1,0:T(8,128)(2,1)S(1)} collective-permute-done((bf16[16,2,48,128]{3,2,1,0:T(8,128)(2,1)S(1)}, bf16[16,2,48,128]{3,2,1,0:T(8,128)(2,1)S(1)}, u32[]{:S(2)}, u32[]{:S(2)}) %collective-permute-start.21) | collective-permute-done | bytes 393248 | tf_op jit(solution)/shard_map/q2_swap/ppermute | solution.py:51
  75.7 5.6 %ladder_late.1 = bf16[1024,2048]{1,0:T(8,128)(2,1)} custom-call(s32[8,16]{1,0:T(8,128)S(1)} %copy-done.2, bf16[1024,768]{1,0:T(8,128)(2,1)S(1)} %get-tuple-element.34.t_ref, f32[1024,1024]{1,0:T(8,128)S(1)} %ladder_early.2.acc0, f32[1024,1024]{1,0:T(8,128)S(1)} %ladder_early.3.acc1, bf16[16,2,48,128]{3,2,1,0:T(8,128)(2,1)S(1)} %collective-permute-done.9.rest_0_, ...), custom_call_target="tpu_custom_call" | custom-call | flops 3221225472 | bytes 17301504 | tf_op jit(solution)/shard_map/ladder_late/pallas_call | solution.py:290
  (14 shorter events, 0.0 us)
Async XLA Ops:
  0.0 63.8 %copy-start.2 = (s32[8,16]{1,0:T(8,128)S(1)}, s32[8,16]{1,0:T(8,128)}, u32[]{:S(2)}) copy-start(s32[8,16]{1,0:T(8,128)} %mask_ref.5) | copy-start | bytes 1540
  4.0 25.9 %all-to-all-start = ((bf16[32,48,128]{2,1,0:T(8,128)(2,1)}), bf16[32,48,128]{2,1,0:T(8,128)(2,1)S(1)}, u32[]{:S(2)}, u32[]{:S(2)}) async-start(bf16[32,48,128]{2,1,0:T(8,128)(2,1)} %get-tuple-element.30), calls=%async_computation | async-start | bytes 786432 | tf_op jit(solution)/shard_map/all_to_all | solution.py:308
  16.1 21.5 %collective-permute-start.1 = (bf16[1024,384]{1,0:T(8,128)(2,1)}, bf16[1024,384]{1,0:T(8,128)(2,1)S(1)}, u32[]{:S(2)}, u32[]{:S(2)}) collective-permute-start(bf16[1024,384]{1,0:T(8,128)(2,1)} %get-tuple-element.29.t0), channel_id=1, source_target_pairs={{0,3},{1,0},{2,1},{3,2},{4,5},{5,6},{6,7},{7,4},{8,11},{9,8},{10,9... | collective-permute-start | bytes 2359304 | tf_op jit(solution)/shard_map/t_back/ppermute | solution.py:46
  17.4 20.2 %collective-permute-start = (bf16[1024,384]{1,0:T(8,128)(2,1)}, bf16[1024,384]{1,0:T(8,128)(2,1)S(1)}, u32[]{:S(2)}, u32[]{:S(2)}) collective-permute-start(bf16[1024,384]{1,0:T(8,128)(2,1)} %get-tuple-element.29.t0), channel_id=1, source_target_pairs={{0,1},{1,2},{2,3},{3,0},{4,7},{5,4},{6,5},{7,6},{8,9},{9,10},{10,1... | collective-permute-start | bytes 2359304 | tf_op jit(solution)/shard_map/t_near/ppermute | solution.py:46
  29.9 3.8 %collective-permute-start.2 = (bf16[32,48,128]{2,1,0:T(8,128)(2,1)S(1)}, bf16[32,48,128]{2,1,0:T(8,128)(2,1)S(1)}, u32[]{:S(2)}, u32[]{:S(2)}) collective-permute-start(bf16[32,48,128]{2,1,0:T(8,128)(2,1)S(1)} %all-to-all-done.a_ref), channel_id=1, source_target_pairs={{0,4},{4,0},{1,5},{5,1},{2,6},{6,2},{3,7},{7,3},{8,12},{12,8},{9,1... | collective-permute-start | bytes 1179656 | tf_op jit(solution)/shard_map/v_swap/ppermute | solution.py:51
  32.4 31.4 %copy-start = (bf16[1024,2048]{1,0:T(8,128)(2,1)S(1)}, bf16[1024,2048]{1,0:T(8,128)(2,1)}, u32[]{:S(2)}) copy-start(bf16[1024,2048]{1,0:T(8,128)(2,1)} %r_ref.3) | copy-start | bytes 12582916
  34.5 7.3 %collective-permute-start.3 = (bf16[16,48,128]{2,1,0:T(8,128)(2,1)S(1)}, bf16[16,48,128]{2,1,0:T(8,128)(2,1)S(1)}, u32[]{:S(2)}, u32[]{:S(2)}) collective-permute-start(bf16[16,48,128]{2,1,0:T(8,128)(2,1)S(1)} %get-tuple-element.31), channel_id=1, source_target_pairs={{0,1},{1,2},{2,3},{3,0},{4,7},{5,4},{6,5},{7,6},{8,9},{9,10},{10,1... | collective-permute-start | bytes 589832 | tf_op jit(solution)/shard_map/r_near/ppermute | solution.py:46
  37.1 6.0 %collective-permute-start.6 = (bf16[8,48,128]{2,1,0:T(8,128)(2,1)S(1)}, bf16[8,48,128]{2,1,0:T(8,128)(2,1)S(1)}, u32[]{:S(2)}, u32[]{:S(2)}) collective-permute-start(bf16[8,48,128]{2,1,0:T(8,128)(2,1)S(1)} %get-tuple-element.37), channel_id=1, source_target_pairs={{0,2},{1,3},{2,0},{3,1},{4,6},{5,7},{6,4},{7,5},{8,10},{9,11},{10,... | collective-permute-start | bytes 294920 | tf_op jit(solution)/shard_map/r_far/ppermute | solution.py:314
  41.8 4.1 %collective-permute-start.5 = (bf16[16,48,128]{2,1,0:T(8,128)(2,1)S(1)}, bf16[16,48,128]{2,1,0:T(8,128)(2,1)S(1)}, u32[]{:S(2)}, u32[]{:S(2)}) collective-permute-start(bf16[16,48,128]{2,1,0:T(8,128)(2,1)S(1)} %collective-permute-done.3.r1_ref), channel_id=1, source_target_pairs={{0,4},{4,0},{1,5},{5,1},{2,6},{6,2},{3,7},{7,3},{8,12},{12,8},{9,1... | collective-permute-start | bytes 589832 | tf_op jit(solution)/shard_map/r_near_swap/ppermute | solution.py:51
  43.1 2.8 %collective-permute-start.7 = (bf16[8,48,128]{2,1,0:T(8,128)(2,1)S(1)}, bf16[8,48,128]{2,1,0:T(8,128)(2,1)S(1)}, u32[]{:S(2)}, u32[]{:S(2)}) collective-permute-start(bf16[8,48,128]{2,1,0:T(8,128)(2,1)S(1)} %collective-permute-done.6.r2_ref), channel_id=1, source_target_pairs={{0,4},{4,0},{1,5},{5,1},{2,6},{6,2},{3,7},{7,3},{8,12},{12,8},{9,1... | collective-permute-start | bytes 294920 | tf_op jit(solution)/shard_map/r_far_swap/ppermute | solution.py:51
  44.9 11.7 %collective-permute-start.4 = (bf16[1024,384]{1,0:T(8,128)(2,1)S(1)}, bf16[1024,384]{1,0:T(8,128)(2,1)S(1)}, u32[]{:S(2)}, u32[]{:S(2)}) collective-permute-start(bf16[1024,384]{1,0:T(8,128)(2,1)S(1)} %collective-permute-done.t1), channel_id=1, source_target_pairs={{0,1},{1,2},{2,3},{3,0},{4,7},{5,4},{6,5},{7,6},{8,9},{9,10},{10,1... | collective-permute-start | bytes 2359304 | tf_op jit(solution)/shard_map/t_far/ppermute | solution.py:46
  46.0 7.0 %collective-permute-start.8 = (bf16[16,2,48,128]{3,2,1,0:T(8,128)(2,1)S(1)}, bf16[16,2,48,128]{3,2,1,0:T(8,128)(2,1)S(1)}, u32[]{:S(2)}, u32[]{:S(2)}) collective-permute-start(bf16[16,2,48,128]{3,2,1,0:T(8,128)(2,1)S(1)} %get-tuple-element.38.rest_0_), channel_id=1, source_target_pairs={{0,32},{4,228},{32,64},{36,4},{64,96},{68,36},{96,128},{100,68},{1... | collective-permute-start | bytes 1179656 | tf_op jit(solution)/shard_map/p1a/ppermute | solution.py:36
  47.0 8.5 %collective-permute-start.13 = (bf16[16,2,48,128]{3,2,1,0:T(8,128)(2,1)S(1)}, bf16[16,2,48,128]{3,2,1,0:T(8,128)(2,1)S(1)}, u32[]{:S(2)}, u32[]{:S(2)}) collective-permute-start(bf16[16,2,48,128]{3,2,1,0:T(8,128)(2,1)S(1)} %get-tuple-element.38.rest_0_), channel_id=1, source_target_pairs={{0,8},{4,28},{8,16},{12,4},{16,24},{20,12},{24,0},{28,20},{1,9},{5... | collective-permute-start | bytes 1179656 | tf_op jit(solution)/shard_map/q0/ppermute | solution.py:41
  49.4 9.4 %collective-permute-start.11 = (bf16[16,2,48,128]{3,2,1,0:T(8,128)(2,1)S(1)}, bf16[16,2,48,128]{3,2,1,0:T(8,128)(2,1)S(1)}, u32[]{:S(2)}, u32[]{:S(2)}) collective-permute-start(bf16[16,2,48,128]{3,2,1,0:T(8,128)(2,1)S(1)} %get-tuple-element.39.rest_4_), channel_id=1, source_target_pairs={{0,32},{4,228},{32,64},{36,4},{64,96},{68,36},{96,128},{100,68},{1... | collective-permute-start | bytes 1179656 | tf_op jit(solution)/shard_map/p1r/ppermute | solution.py:36
  53.1 5.8 %collective-permute-start.10 = (bf16[16,2,48,128]{3,2,1,0:T(8,128)(2,1)S(1)}, bf16[16,2,48,128]{3,2,1,0:T(8,128)(2,1)S(1)}, u32[]{:S(2)}, u32[]{:S(2)}) collective-permute-start(bf16[16,2,48,128]{3,2,1,0:T(8,128)(2,1)S(1)} %collective-permute-done.8.rest_1_), channel_id=1, source_target_pairs={{0,4},{4,0},{1,5},{5,1},{2,6},{6,2},{3,7},{7,3},{8,12},{12,8},{9,1... | collective-permute-start | bytes 1179656 | tf_op jit(solution)/shard_map/p1a_swap/ppermute | solution.py:51
  55.5 7.7 %collective-permute-start.9 = (bf16[16,2,48,128]{3,2,1,0:T(8,128)(2,1)S(1)}, bf16[16,2,48,128]{3,2,1,0:T(8,128)(2,1)S(1)}, u32[]{:S(2)}, u32[]{:S(2)}) collective-permute-start(bf16[16,2,48,128]{3,2,1,0:T(8,128)(2,1)S(1)} %collective-permute-done.8.rest_1_), channel_id=1, source_target_pairs={{0,32},{4,228},{32,64},{36,4},{64,96},{68,36},{96,128},{100,68},{1... | collective-permute-start | bytes 1179656 | tf_op jit(solution)/shard_map/p2/ppermute | solution.py:36
  55.5 8.3 %collective-permute-start.14 = (bf16[16,2,48,128]{3,2,1,0:T(8,128)(2,1)S(1)}, bf16[16,2,48,128]{3,2,1,0:T(8,128)(2,1)S(1)}, u32[]{:S(2)}, u32[]{:S(2)}) collective-permute-start(bf16[16,2,48,128]{3,2,1,0:T(8,128)(2,1)S(1)} %collective-permute-done.13.rest_3_), channel_id=1, source_target_pairs={{0,4},{4,0},{1,5},{5,1},{2,6},{6,2},{3,7},{7,3},{8,12},{12,8},{9,1... | collective-permute-start | bytes 1179656 | tf_op jit(solution)/shard_map/q0_swap/ppermute | solution.py:51
  56.6 1.1 %copy-start.1 = (bf16[1024,384]{1,0:T(8,128)(2,1)S(1)}, bf16[1024,384]{1,0:T(8,128)(2,1)}, u32[]{:S(2)}) copy-start(bf16[1024,384]{1,0:T(8,128)(2,1)} %get-tuple-element.29.t0) | copy-start | bytes 2359300
  58.9 4.9 %collective-permute-start.12 = (bf16[16,2,48,128]{3,2,1,0:T(8,128)(2,1)S(1)}, bf16[16,2,48,128]{3,2,1,0:T(8,128)(2,1)S(1)}, u32[]{:S(2)}, u32[]{:S(2)}) collective-permute-start(bf16[16,2,48,128]{3,2,1,0:T(8,128)(2,1)S(1)} %collective-permute-done.11.rest_5_), channel_id=1, source_target_pairs={{0,4},{4,0},{1,5},{5,1},{2,6},{6,2},{3,7},{7,3},{8,12},{12,8},{9,1... | collective-permute-start | bytes 1179656 | tf_op jit(solution)/shard_map/p1r_swap/ppermute | solution.py:51
  60.5 9.7 %collective-permute-start.16 = (bf16[16,2,48,128]{3,2,1,0:T(8,128)(2,1)S(1)}, bf16[16,2,48,128]{3,2,1,0:T(8,128)(2,1)S(1)}, u32[]{:S(2)}, u32[]{:S(2)}) collective-permute-start(bf16[16,2,48,128]{3,2,1,0:T(8,128)(2,1)S(1)} %collective-permute-done.11.rest_5_), channel_id=1, source_target_pairs={{0,8},{4,28},{8,16},{12,4},{16,24},{20,12},{24,0},{28,20},{1,9},{5... | collective-permute-start | bytes 1179656 | tf_op jit(solution)/shard_map/q1r/ppermute | solution.py:41
  61.9 8.4 %collective-permute-start.15 = (bf16[16,2,48,128]{3,2,1,0:T(8,128)(2,1)S(1)}, bf16[16,2,48,128]{3,2,1,0:T(8,128)(2,1)S(1)}, u32[]{:S(2)}, u32[]{:S(2)}) collective-permute-start(bf16[16,2,48,128]{3,2,1,0:T(8,128)(2,1)S(1)} %collective-permute-done.13.rest_3_), channel_id=1, source_target_pairs={{0,32},{4,228},{32,64},{36,4},{64,96},{68,36},{96,128},{100,68},{1... | collective-permute-start | bytes 1179656 | tf_op jit(solution)/shard_map/q1a/ppermute | solution.py:36
  63.2 8.8 %collective-permute-start.17 = (bf16[16,2,48,128]{3,2,1,0:T(8,128)(2,1)S(1)}, bf16[16,2,48,128]{3,2,1,0:T(8,128)(2,1)S(1)}, u32[]{:S(2)}, u32[]{:S(2)}) collective-permute-start(bf16[16,2,48,128]{3,2,1,0:T(8,128)(2,1)S(1)} %collective-permute-done.9.rest_0_), channel_id=1, source_target_pairs={{0,8},{4,28},{8,16},{12,4},{16,24},{20,12},{24,0},{28,20},{1,9},{5... | collective-permute-start | bytes 1179656 | tf_op jit(solution)/shard_map/q2/ppermute | solution.py:41
  70.2 2.6 %collective-permute-start.18 = (bf16[16,2,48,128]{3,2,1,0:T(8,128)(2,1)S(1)}, bf16[16,2,48,128]{3,2,1,0:T(8,128)(2,1)S(1)}, u32[]{:S(2)}, u32[]{:S(2)}) collective-permute-start(bf16[16,2,48,128]{3,2,1,0:T(8,128)(2,1)S(1)} %collective-permute-done.15.rest_1_), channel_id=1, source_target_pairs={{0,4},{4,0},{1,5},{5,1},{2,6},{6,2},{3,7},{7,3},{8,12},{12,8},{9,1... | collective-permute-start | bytes 1179656 | tf_op jit(solution)/shard_map/q1a_swap/ppermute | solution.py:51
  71.5 1.9 %collective-permute-start.19 = (bf16[16,2,48,128]{3,2,1,0:T(8,128)(2,1)S(1)}, bf16[16,2,48,128]{3,2,1,0:T(8,128)(2,1)S(1)}, u32[]{:S(2)}, u32[]{:S(2)}) collective-permute-start(bf16[16,2,48,128]{3,2,1,0:T(8,128)(2,1)S(1)} %collective-permute-done.16.rest_5_), channel_id=1, source_target_pairs={{0,4},{4,0},{1,5},{5,1},{2,6},{6,2},{3,7},{7,3},{8,12},{12,8},{9,1... | collective-permute-start | bytes 1179656 | tf_op jit(solution)/shard_map/q1r_swap/ppermute | solution.py:51
  71.6 2.4 %collective-permute-start.20 = (bf16[16,2,48,128]{3,2,1,0:T(8,128)(2,1)S(1)}, bf16[16,2,48,128]{3,2,1,0:T(8,128)(2,1)S(1)}, u32[]{:S(2)}, u32[]{:S(2)}) collective-permute-start(bf16[16,2,48,128]{3,2,1,0:T(8,128)(2,1)S(1)} %collective-permute-done.9.rest_0_), channel_id=1, source_target_pairs={{0,4},{4,0},{1,5},{5,1},{2,6},{6,2},{3,7},{7,3},{8,12},{12,8},{9,1... | collective-permute-start | bytes 1179656 | tf_op jit(solution)/shard_map/p2_swap/ppermute | solution.py:51
  73.9 1.7 %collective-permute-start.21 = (bf16[16,2,48,128]{3,2,1,0:T(8,128)(2,1)S(1)}, bf16[16,2,48,128]{3,2,1,0:T(8,128)(2,1)S(1)}, u32[]{:S(2)}, u32[]{:S(2)}) collective-permute-start(bf16[16,2,48,128]{3,2,1,0:T(8,128)(2,1)S(1)} %collective-permute-done.17.rest_3_), channel_id=1, source_target_pairs={{0,4},{4,0},{1,5},{5,1},{2,6},{6,2},{3,7},{7,3},{8,12},{12,8},{9,1... | collective-permute-start | bytes 1179656 | tf_op jit(solution)/shard_map/q2_swap/ppermute | solution.py:51
